TPU v7x, 32 devices: a whole 2x2x4 slice. The times are simulated.
32 devices in a mesh: rep: 4 (over y, x), fsdp: 8 (over z, core).
Axes of the slice: x: 2, y: 2, z: 4, core: 2. Of those that a mesh axis runs over, the one named last changes fastest.
Arguments:
- tokens: bfloat16 [4, 512, 8192], P('rep', None, 'fsdp'), may hold values from -6 to 6
- targets: bfloat16 [4, 512, 1024], P('rep', 'fsdp'), may hold values from -6 to 6
- inner_weights: float32 [4, 8192, 1024], P('rep', 'fsdp'), may hold values from -6 to 6
- outer_weights: float32 [8192, 1024], P('fsdp'), may hold values from -6 to 6
- outer_momentum: float32 [8192, 1024], P('fsdp'), may hold values from -3 to 3
- replica_weights: bfloat16 [4, 8192, 1024], P('rep', 'fsdp'), may hold values from -6 to 6
Outputs:
- new_inner: float32 [4, 8192, 1024], P('rep', 'fsdp')
- new_outer: float32 [8192, 1024], P('fsdp')
- new_moment: float32 [8192, 1024], P('fsdp')
- merged: bfloat16 [4, 8192, 1024], P('rep', 'fsdp')
All inputs are finite; a program needn't handle non-finite values.
Results may differ from a plain program's by a relative error of at most 0.005.
Values may be sent and summed in bfloat16 or wider, within the bound.
No kernel may reach another device: no remote copies, remote signals or barrier semaphores. Data moves between devices by JAX's collectives and lax.ppermute only.
A program may use at most 64 MiB of HBM per device.

v0:
```python
import jax
import jax.numpy as jnp
from jax import lax
from jax.sharding import PartitionSpec as P

D = 8192
INNER = 2


inner_rate = 0.5
momentum_coef = 0.9
outer_rate = 0.7
merge_keep = 0.5


def outer_update(outer_part, moment_part, outer_delta):
    new_moment = momentum_coef * moment_part + outer_delta
    new_outer = outer_part - outer_rate * (outer_delta + momentum_coef * new_moment)
    return (new_outer, new_moment)


def outer_sync(outer_weights, outer_momentum, replica_weights):
    replica_rows = replica_weights[0].astype(jnp.float32)
    replica_term = outer_weights - replica_rows
    replica_count = lax.axis_size("rep")
    pseudo_sum = lax.psum(replica_term, "rep")
    new_outer, new_moment = outer_update(outer_weights, outer_momentum, pseudo_sum / replica_count)
    mixed = merge_keep * replica_rows + (1.0 - merge_keep) * new_outer
    merged = mixed.astype(jnp.bfloat16)[None]
    return (new_outer, new_moment, merged)


def inner_run(tokens, targets, inner_weights):
    token_cols = tokens[0]
    target_rows = targets[0]
    weights_now = inner_weights[0]
    weight_scale = D ** (-0.5)
    for inner_turn in range(INNER):
        weights_half = weights_now.astype(jnp.bfloat16)
        predicted = (
            lax.psum_scatter(
                jnp.dot(token_cols, weights_half, preferred_element_type=jnp.float32).astype(
                    jnp.bfloat16
                ),
                "fsdp",
                scatter_dimension=0,
                tiled=True,
            ).astype(jnp.float32)
            * weight_scale
        )
        errors = (predicted - target_rows.astype(jnp.float32)).astype(jnp.bfloat16)
        gradient = (
            lax.dot_general(
                token_cols,
                lax.all_gather(errors, "fsdp", axis=0, tiled=True),
                (((0,), (0,)), ((), ())),
                preferred_element_type=jnp.float32,
            )
            * weight_scale
        )
        weights_now = weights_now - inner_rate * gradient
    return weights_now[None]


def local(tokens, targets, inner_weights, outer_weights, outer_momentum, replica_weights):
    new_outer, new_moment, merged = outer_sync(outer_weights, outer_momentum, replica_weights)
    new_inner = inner_run(tokens, targets, inner_weights)
    return (new_inner, new_outer, new_moment, merged)


def solution(mesh):
    placed = (
        P("rep", None, "fsdp"),
        P("rep", "fsdp", None),
        P("rep", "fsdp", None),
        P("fsdp", None),
        P("fsdp", None),
        P("rep", "fsdp", None),
    )
    return jax.shard_map(
        local,
        mesh=mesh,
        in_specs=placed,
        out_specs=(
            P("rep", "fsdp", None),
            P("fsdp", None),
            P("fsdp", None),
            P("rep", "fsdp", None),
        ),
        check_vma=False,
    )
```

profile of v0, /device:TPU:0, one launch (start us, length us, event | category | flops | bytes accessed | tf_op | source)
XLA Modules:
  0.0 217.6 jit_solution(1529033209000001528)
XLA Ops:
  8.0 0.0 reduce-scatter.3.cloned.1.call-start
  8.1 1.2 copy-done
  9.2 4.4 %fusion.12 = bf16[512,1024]{1,0:T(8,128)(2,1)} fusion(f32[1,1024,1024]{2,1,0:T(8,128)} %param.8, bf16[1,512,1024]{2,1,0:T(8,128)(2,1)S(1)} %copy-done), kind=kOutput, calls=%fused_computation.16 | convolution fusion | flops 1075314688 | bytes 6291456 | tf_op jit(solution)/shard_map/dot_general | solution.py:42
  13.6 0.0 reduce-scatter.3.cloned.1.call-update
  13.7 0.0 all-gather.3.cloned.1.call-start
  13.7 35.1 %reduce-scatter.3.cloned.1.call-done = bf16[64,1024]{1,0:T(8,128)(2,1)} async-done(((bf16[512,1024]{1,0:T(8,128)(2,1)}), bf16[64,1024]{1,0:T(8,128)(2,1)}) %reduce-scatter.3.cloned.1.call-update) | async-done | bytes 131088 | tf_op jit(solution)/shard_map/reduce_scatter | solution.py:41
  48.8 1.6 fusion.22
  50.4 0.0 all-gather.3.cloned.1.call-update
  50.5 0.0 reduce-scatter.5.cloned.1.call-start
  50.5 5.3 %copy.10 = f32[1,1024,1024]{1,2,0:T(8,128)} copy(f32[1,1024,1024]{2,1,0:T(8,128)} %param.8) | data formatting | bytes 8388608 | tf_op args[2]
  55.9 15.5 %all-gather.3.cloned.1.call-done = bf16[512,1024]{1,0:T(8,128)(2,1)} async-done(((bf16[64,1024]{1,0:T(8,128)(2,1)}), bf16[512,1024]{1,0:T(8,128)(2,1)}) %all-gather.3.cloned.1.call-update) | async-done | bytes 1048592 | tf_op jit(solution)/shard_map/all_gather | solution.py:55
  71.4 3.8 %bitcast_subtract_fusion.1 = f32[1024,1024]{0,1:T(8,128)S(1)} fusion(f32[1,1024,1024]{1,2,0:T(8,128)} %copy.10, bf16[512,1024]{1,0:T(8,128)(2,1)} %all-gather.3.cloned.1.call-done, bf16[1,512,1024]{2,1,0:T(8,128)(2,1)S(1)} %copy-done), kind=kOutput, calls=%fused_computation.6 | convolution fusion | flops 1075838976 | bytes 10485760 | tf_op jit(solution)/shard_map/dot_general | solution.py:53
  75.2 2.0 copy-done.1
  77.2 2.3 %fusion.15 = bf16[512,1024]{1,0:T(8,128)(2,1)} fusion(f32[1024,1024]{0,1:T(8,128)S(1)} %bitcast_subtract_fusion.1, bf16[1,512,1024]{2,1,0:T(8,128)(2,1)S(1)} %copy-done), kind=kOutput, calls=%fused_computation.17 | convolution fusion | flops 1075314688 | bytes 6291456 | tf_op jit(solution)/shard_map/dot_general | solution.py:42
  79.6 0.0 all-reduce.2.cloned.1.call-start
  79.6 5.3 %convert_subtract_fusion = f32[1024,1024]{1,0:T(8,128)} fusion(f32[1024,1024]{1,0:T(8,128)} %param.9, bf16[1,1024,1024]{2,1,0:T(8,128)(2,1)S(1)} %copy-done.2), kind=kLoop, calls=%fused_computation.1 | loop fusion | flops 2097152 | bytes 10485760 | tf_op jit(solution)/shard_map/sub | solution.py:24
  84.9 0.0 all-reduce.2.cloned.1.call-update
  84.9 0.0 all-gather.5.cloned.1.call-start
  85.0 26.8 %reduce-scatter.5.cloned.1.call-done = bf16[64,1024]{1,0:T(8,128)(2,1)} async-done(((bf16[512,1024]{1,0:T(8,128)(2,1)}), bf16[64,1024]{1,0:T(8,128)(2,1)}) %reduce-scatter.5.cloned.1.call-update) | async-done | bytes 131088 | tf_op jit(solution)/shard_map/reduce_scatter | solution.py:41
  111.7 1.6 fusion.23
  113.4 74.7 %all-reduce.2.cloned.1.call-done = f32[1024,1024]{1,0:T(8,128)} async-done(((f32[1024,1024]{1,0:T(8,128)}), f32[1024,1024]{1,0:T(8,128)}) %all-reduce.2.cloned.1.call-update) | async-done | bytes 4194320 | tf_op jit(solution)/shard_map/psum | solution.py:26
  188.1 11.3 %fusion.3 = (bf16[1,1024,1024]{2,1,0:T(8,128)(2,1)}, f32[1024,1024]{1,0:T(8,128)}, f32[1024,1024]{1,0:T(8,128)}) fusion(bf16[1,1024,1024]{2,1,0:T(8,128)(2,1)S(1)} %copy-done.2, f32[1024,1024]{1,0:T(8,128)} %param.9, f32[1024,1024]{1,0:T(8,128)} %all-reduce.2.cloned.1.call-done, f32[1024,1024]{1,0:T(8,128)} %param.10), kind=kLoop, calls=%fused_computation.9 | loop fusion | flops 11534336 | bytes 25165824 | tf_op jit(solution)/shard_map/broadcast_in_dim | solution.py:29
  199.4 5.8 %fusion.2 = f32[1,1024,1024]{1,2,0:T(8,128)} fusion(f32[1024,1024]{0,1:T(8,128)} %copy-done.1, bf16[512,1024]{1,0:T(8,128)(2,1)} %all-gather.5.cloned.1.call-done, bf16[1,512,1024]{2,1,0:T(8,128)(2,1)S(1)} %copy-done), kind=kOutput, calls=%fused_computation.5 | convolution fusion | flops 1075838976 | bytes 10485760 | tf_op jit(solution)/shard_map/dot_general | solution.py:53
  205.2 5.3 %copy.11 = f32[1,1024,1024]{2,1,0:T(8,128)} copy(f32[1,1024,1024]{1,2,0:T(8,128)} %fusion.2) | data formatting | bytes 8388608
  (9 shorter events, 0.1 us)
Async XLA Ops:
  8.0 1.2 copy-start
  8.0 40.8 %copy-start.3 = (bf16[1,64,1024]{2,1,0:T(8,128)(2,1)S(1)}, bf16[1,64,1024]{2,1,0:T(8,128)(2,1)}, u32[]{:S(2)}) copy-start(bf16[1,64,1024]{2,1,0:T(8,128)(2,1)} %param.7) | copy-start | bytes 393220
  8.0 40.8 %reduce-scatter.3.cloned.1.call-start = ((), (), s32[]{:S(2)}) async-start(), calls=%async_computation.2 | async-start | bytes 1179648 | tf_op jit(solution)/shard_map/reduce_scatter | solution.py:41
  13.7 57.8 %all-gather.3.cloned.1.call-start = ((), (), s32[]{:S(2)}) async-start(), calls=%async_computation.3 | async-start | bytes 1179648 | tf_op jit(solution)/shard_map/all_gather | solution.py:55
  50.5 61.3 %reduce-scatter.5.cloned.1.call-start = ((), (), s32[]{:S(2)}) async-start(), calls=%async_computation.4 | async-start | bytes 1179648 | tf_op jit(solution)/shard_map/reduce_scatter | solution.py:41
  75.2 2.0 copy-start.1
  77.2 2.4 %copy-start.2 = (bf16[1,1024,1024]{2,1,0:T(8,128)(2,1)S(1)}, bf16[1,1024,1024]{2,1,0:T(8,128)(2,1)}, u32[]{:S(2)}) copy-start(bf16[1,1024,1024]{2,1,0:T(8,128)(2,1)} %param.11) | copy-start | bytes 6291460
  79.6 108.5 %all-reduce.2.cloned.1.call-start = ((), (), s32[]{:S(2)}) async-start(), calls=%async_computation.6 | async-start | bytes 8388608 | tf_op jit(solution)/shard_map/psum | solution.py:26
  84.9 114.5 %all-gather.5.cloned.1.call-start = ((), (), s32[]{:S(2)}) async-start(), calls=%async_computation.5 | async-start | bytes 1179648 | tf_op jit(solution)/shard_map/all_gather | solution.py:55
Sparse Core Ops, SparseCore 0:
  13.8 35.0 reduce-scatter.2
  51.0 20.3 all-gather.2
  79.7 32.0 reduce-scatter.4
  113.5 20.4 all-gather.4
Sparse Core Ops, SparseCore 1:
  85.0 103.1 all-reduce.1
where the time goes:
time: 218 us
  waiting for transfers between devices  152 us (70%)
  other arithmetic  19.7 us (9%)
  matrix products  16.3 us (7%)
  between operations  15.3 us (7%)
  local copies, waits for them, and re-layouts  13.9 us (6%)
    psum x1, waiting for transfers between devices, outer_sync(): pseudo_sum = lax.psum(replica_term, 'rep')  74.7 us
    reduce_scatter x2, waiting for transfers between devices, inner_run(): lax.psum_scatter(jnp.dot(token_cols, weights_half, preferred_element_type...  61.9 us
    all_gather x2, waiting for transfers between devices, inner_run(): lax.all_gather(errors, 'fsdp', axis=0, tiled=True)  15.5 us
    unnamed x10, local copies, waits for them, and re-layouts  13.9 us
    broadcast_in_dim x1, other arithmetic, outer_sync(): merged = mixed.astype(jnp.bfloat16)[None]  11.3 us
    dot_general x2, matrix products, inner_run(): lax.dot_general(token_cols, lax.all_gather(errors, 'fsdp', axis=0, tiled=...  9.58 us
    dot_general x2, matrix products, inner_run(): jnp.dot(token_cols, weights_half, preferred_element_type=jnp.float32)  6.7 us
    sub x1, other arithmetic, outer_sync(): replica_term = outer_weights - replica_rows  5.26 us
  transfers between devices with their start and end apart: 5, of which 4 were waited for; matrix products, arithmetic and copies ran while one was open for 11% of the time, Pallas kernels for 0%

commit v1 on v0

v1 whole, which is shorter than its diff:
```python
import functools

import jax
import jax.numpy as jnp
from jax import lax
from jax.experimental import pallas as pl
from jax.experimental.pallas import tpu as pltpu
from jax.sharding import PartitionSpec as P

INNER = 2

inner_rate = 0.5
momentum_coef = 0.9
outer_rate = 0.7
merge_keep = 0.5

F32 = jnp.float32
BF16 = jnp.bfloat16
LANES = 128
MIB = 1 << 20

CODE_SCALE = 2.0**60
CODE_LEAST = 2.0**-30
CODE_CUT = 2.0**20


def encode(total, outer_rows, count):
    away = count * outer_rows - total
    held = jnp.where(jnp.abs(total) < CODE_LEAST, CODE_LEAST, total) * CODE_SCALE
    return jnp.where(jnp.abs(total) < jnp.abs(away), held, away).astype(BF16)


def decode_total(code, outer_rows, count):
    code = code.astype(F32)
    return jnp.where(jnp.abs(code) > CODE_CUT, code * (1.0 / CODE_SCALE), count * outer_rows - code)


def decode_away(code, outer_rows, count):
    code = code.astype(F32)
    return jnp.where(jnp.abs(code) > CODE_CUT, count * outer_rows - code * (1.0 / CODE_SCALE), code)


def swap(value, axis, flip):
    count = lax.axis_size(axis)
    return lax.ppermute(value, axis, [(i, i ^ flip) for i in range(count)])


def params(mib):
    return pltpu.CompilerParams(vmem_limit_bytes=mib * MIB)


def cost(flops, nbytes):
    return pl.CostEstimate(flops=int(flops), bytes_accessed=int(nbytes), transcendentals=0)


def row_slice(value, start, size):
    return lax.dynamic_slice_in_dim(value, start, size, 0)


def update_kernel(replicas, blocks, pos_ref, code_a, code_b, outer_ref, moment_ref, rep_ref, *rest):
    new_outer_ref, new_moment_ref, merged_ref = rest[-3:]
    step = pl.program_id(0)

    def update(code_ref):
        outer = outer_ref[...]
        delta = decode_away(code_ref[...], outer, float(replicas)) * (1.0 / replicas)
        moment = momentum_coef * moment_ref[...] + delta
        new_outer = outer - outer_rate * (delta + momentum_coef * moment)
        new_outer_ref[...] = new_outer
        new_moment_ref[...] = moment
        mixed = merge_keep * rep_ref[...].astype(F32) + (1.0 - merge_keep) * new_outer
        merged_ref[...] = mixed.astype(BF16)

    @pl.when(step < blocks)
    def _():
        update(code_a)

    @pl.when(step >= blocks)
    def _():
        update(code_b)


def outer_update(start_a, start_b, code_a, code_b, outer, moment, rep_rows, before):
    replicas = lax.axis_size("rep")
    size, width = code_a.shape
    block = min(size, 128)
    blocks = size // block
    pos = jnp.stack([start_a // block, start_b // block]).astype(jnp.int32)

    def at(i, pos_ref):
        return (jnp.where(i < blocks, pos_ref[0] + i, pos_ref[1] + i - blocks), 0)

    code_specs = [
        pl.BlockSpec((block, width), lambda i, pos_ref: (jnp.minimum(i, blocks - 1), 0)),
        pl.BlockSpec((block, width), lambda i, pos_ref: (jnp.maximum(i - blocks, 0), 0)),
    ]
    row_spec = pl.BlockSpec((block, width), at)
    rows = outer.shape[0]
    aliases = {} if before is None else {6: 0, 7: 1, 8: 2}
    held = () if before is None else before
    return pl.pallas_call(
        functools.partial(update_kernel, replicas, blocks),
        out_shape=(
            jax.ShapeDtypeStruct((rows, width), F32),
            jax.ShapeDtypeStruct((rows, width), F32),
            jax.ShapeDtypeStruct((rows, width), BF16),
        ),
        grid_spec=pltpu.PrefetchScalarGridSpec(
            num_scalar_prefetch=1,
            grid=(2 * blocks,),
            in_specs=code_specs + [row_spec] * 3 + [pl.BlockSpec(memory_space=pl.ANY)] * len(held),
            out_specs=[row_spec] * 3,
        ),
        input_output_aliases=aliases,
        compiler_params=params(16),
        cost_estimate=cost(20 * size * width, 2 * size * width * 22),
        name="outer_update",
    )(pos, code_a, code_b, outer, moment, rep_rows, *held)


def outer_sync(outer, moment, rep_rows):
    replicas = lax.axis_size("rep")
    index = lax.axis_index("rep")
    bits = replicas.bit_length() - 1
    rows = rep_rows.shape[0]
    half = rows // 2
    orders = (tuple(range(bits)), tuple(reversed(range(bits))))
    bases = (0, half)
    current = [rep_rows, rep_rows]
    offsets = [jnp.int32(0), jnp.int32(half)]
    starts = [jnp.int32(0), jnp.int32(half)]
    size = half
    count = 1
    for turn in range(bits):
        size //= 2
        sends, keeps = [], []
        for s in range(2):
            bit = (index >> orders[s][turn]) & 1
            send_at = (1 - bit) * size
            keep_at = bit * size
            send = row_slice(current[s], offsets[s] + send_at, size)
            keep = row_slice(current[s], offsets[s] + keep_at, size)
            if count > 1:
                send = encode(send, row_slice(outer, starts[s] + send_at, size), float(count))
            starts[s] = starts[s] + keep_at
            offsets[s] = jnp.int32(0)
            sends.append(send)
            keeps.append(keep)
        for s in range(2):
            got = swap(sends[s], "rep", 1 << orders[s][turn])
            if count > 1:
                got = decode_total(got, row_slice(outer, starts[s], size), float(count))
            current[s] = keeps[s].astype(F32) + got.astype(F32)
        count *= 2
    codes = [
        encode(current[s], row_slice(outer, starts[s], size), float(replicas)) for s in range(2)
    ]
    for turn in reversed(range(bits)):
        got = [swap(codes[s], "rep", 1 << orders[s][turn]) for s in range(2)]
        set_bits = [(index >> orders[s][turn]) & 1 for s in range(2)]
        low = [starts[s] - set_bits[s] * size for s in range(2)]
        if turn == 0:
            first = outer_update(starts[0], starts[1], codes[0], codes[1], outer, moment, rep_rows, None)
            far = [low[s] + (1 - set_bits[s]) * size for s in range(2)]
            return outer_update(far[0], far[1], got[0], got[1], outer, moment, rep_rows, first)
        for s in range(2):
            pair = jnp.where(
                set_bits[s] == 0,
                jnp.concatenate([codes[s], got[s]], 0),
                jnp.concatenate([got[s], codes[s]], 0),
            )
            codes[s] = pair
            starts[s] = low[s]
        size *= 2


def gram_kernel(scale, x_ref, keep_ref, send_ref, turned_ref, core_ref):
    x = x_ref[...]
    gram = lax.dot_general(x, x, (((1,), (1,)), ((), ())), preferred_element_type=F32) * scale
    tiles = x.shape[0] // LANES
    pairs = [(i, j) for i in range(tiles) for j in range(i, tiles)]
    each = len(pairs) // 2
    mine = core_ref[0]
    for place, (i, j) in enumerate(pairs):
        part = gram[i * LANES : (i + 1) * LANES, j * LANES : (j + 1) * LANES].astype(BF16)
        side, spot = place // each, place % each
        rows = pl.ds(spot * LANES, LANES)

        @pl.when(mine == side)
        def _():
            keep_ref[rows, :] = part

        @pl.when(mine != side)
        def _():
            send_ref[rows, :] = part

    turned_ref[...] = x.T


def gram_parts(x, core, scale):
    tokens, depth = x.shape
    tiles = tokens // LANES
    each = tiles * (tiles + 1) // 4
    vmem = pl.BlockSpec(memory_space=pltpu.VMEM)
    part = jax.ShapeDtypeStruct((each * LANES, LANES), BF16)
    return pl.pallas_call(
        lambda core_ref, x_ref, keep_ref, send_ref, turned_ref: gram_kernel(
            scale, x_ref, keep_ref, send_ref, turned_ref, core_ref
        ),
        out_shape=(part, part, jax.ShapeDtypeStruct((depth, tokens), BF16)),
        in_specs=[pl.BlockSpec(memory_space=pltpu.SMEM), vmem],
        out_specs=(vmem, vmem, vmem),
        compiler_params=params(16),
        cost_estimate=cost(2 * tokens * tokens * depth, 4 * tokens * depth),
        name="gram_parts",
    )(core, x)


def project_kernel(scale, info_ref, x_ref, w_ref, t_ref, out_ref, acc_ref):
    acc_ref[...] = scale * jnp.dot(x_ref[...], w_ref[...].astype(BF16), preferred_element_type=F32)
    own = t_ref.shape[0]
    rows = pl.ds(pl.multiple_of(info_ref[1] * own, own), own)
    acc_ref[rows, :] = acc_ref[rows, :] - t_ref[...].astype(F32)
    for piece in range(out_ref.shape[0]):
        out_ref[piece] = acc_ref[:, piece * LANES : (piece + 1) * LANES].astype(BF16)


def project(x, w, t, info, scale):
    tokens, depth = x.shape
    width = w.shape[1]
    span = 2 * LANES
    steps = width // 2 // span
    return pl.pallas_call(
        functools.partial(project_kernel, scale),
        out_shape=jax.ShapeDtypeStruct((width // 2 // LANES, tokens, LANES), BF16),
        grid_spec=pltpu.PrefetchScalarGridSpec(
            num_scalar_prefetch=1,
            grid=(steps,),
            in_specs=[
                pl.BlockSpec((tokens, depth), lambda j, info_ref: (0, 0)),
                pl.BlockSpec((depth, span), lambda j, info_ref: (0, info_ref[0] * steps + j)),
                pl.BlockSpec((t.shape[0], span), lambda j, info_ref: (0, info_ref[0] * steps + j)),
            ],
            out_specs=pl.BlockSpec((span // LANES, tokens, LANES), lambda j, info_ref: (j, 0, 0)),
            scratch_shapes=[pltpu.VMEM((tokens, span), F32)],
        ),
        compiler_params=params(16),
        cost_estimate=cost(tokens * depth * width, 2 * depth * width + 2 * tokens * depth),
        name="project",
    )(info, x, w, t)


def whole_gram_kernel(pos_ref, mine_ref, other_ref, out_ref, pack_ref):
    pieces, rows, _ = mine_ref.shape
    for spot in range(pieces):
        mine_at = pos_ref[spot] * rows
        other_at = pos_ref[pieces + spot] * rows
        pack_ref[pl.ds(pl.multiple_of(mine_at, rows), rows), :] = mine_ref[spot]
        pack_ref[pl.ds(pl.multiple_of(other_at, rows), rows), :] = other_ref[spot]
    tiles = out_ref.shape[0] // LANES
    pairs = [(i, j) for i in range(tiles) for j in range(i, tiles)]
    for place, (i, j) in enumerate(pairs):
        part = pack_ref[place * LANES : (place + 1) * LANES, :]
        out_ref[i * LANES : (i + 1) * LANES, j * LANES : (j + 1) * LANES] = part
        if i != j:
            out_ref[j * LANES : (j + 1) * LANES, i * LANES : (i + 1) * LANES] = part.T


def whole_gram(pos, mine, other, tokens):
    vmem = pl.BlockSpec(memory_space=pltpu.VMEM)
    pieces, rows, _ = mine.shape
    return pl.pallas_call(
        whole_gram_kernel,
        out_shape=jax.ShapeDtypeStruct((tokens, tokens), BF16),
        in_specs=[pl.BlockSpec(memory_space=pltpu.SMEM), vmem, vmem],
        out_specs=vmem,
        scratch_shapes=[pltpu.VMEM((2 * pieces * rows, LANES), BF16)],
        compiler_params=params(16),
        cost_estimate=cost(0, 4 * pieces * rows * LANES + 2 * tokens * tokens),
        name="whole_gram",
    )(pos, mine, other)


def residual_kernel(own_ref, *refs):
    got, gram_ref, out_ref = refs[:-2], refs[-2], refs[-1]
    error = own_ref[...].astype(F32)
    for ref in got:
        error = error + ref[...].astype(F32)
    moved = jnp.dot(gram_ref[...], error.astype(BF16), preferred_element_type=F32)
    out_ref[...] = (2.0 * error - moved).astype(BF16)


def residual(own, got, gram):
    vmem = pl.BlockSpec(memory_space=pltpu.VMEM)
    tokens, width = own.shape
    return pl.pallas_call(
        residual_kernel,
        out_shape=jax.ShapeDtypeStruct((tokens, width), BF16),
        in_specs=[vmem] * (2 + len(got)),
        out_specs=vmem,
        compiler_params=params(16),
        cost_estimate=cost(2 * tokens * tokens * width, 2 * tokens * (tokens + 5 * width)),
        name="residual",
    )(own, *got, gram)


def step_kernel(rate, pos_ref, turned_ref, *refs):
    out_ref = refs[-1]
    pieces, w_ref = refs[0], refs[1]
    grad = jnp.dot(turned_ref[...], pieces[0], preferred_element_type=F32)
    out_ref[...] = w_ref[...] - rate * grad


def weight_step(turned, pieces, pos, w, rate, before):
    depth, tokens = turned.shape
    count, _, width = pieces.shape
    held = () if before is None else (before,)
    return pl.pallas_call(
        functools.partial(step_kernel, rate),
        out_shape=jax.ShapeDtypeStruct(w.shape, F32),
        grid_spec=pltpu.PrefetchScalarGridSpec(
            num_scalar_prefetch=1,
            grid=(count,),
            in_specs=[
                pl.BlockSpec((depth, tokens), lambda j, pos_ref: (0, 0)),
                pl.BlockSpec((1, tokens, width), lambda j, pos_ref: (j, 0, 0)),
                pl.BlockSpec((depth, width), lambda j, pos_ref: (0, pos_ref[j])),
            ]
            + [pl.BlockSpec(memory_space=pl.ANY)] * len(held),
            out_specs=pl.BlockSpec((depth, width), lambda j, pos_ref: (0, pos_ref[j])),
        ),
        input_output_aliases={} if before is None else {4: 0},
        compiler_params=params(16),
        cost_estimate=cost(2 * tokens * depth * width * count, 8 * depth * width * count),
        name="weight_step",
    )(pos, turned, pieces, w, *held)


def inner_run(x, t, w):
    shards = lax.axis_size("fsdp")
    index = lax.axis_index("fsdp")
    core, chip = index & 1, index >> 1
    chips = shards // 2
    features = x.shape[1] * shards
    scale = features**-0.5
    tokens = x.shape[0]

    gram_keep, gram_send, turned = gram_parts(
        x, core.astype(jnp.int32)[None], inner_rate * scale * scale
    )
    gram_got = swap(gram_send, "fsdp", 1)

    def info(side):
        return jnp.stack([side, index]).astype(jnp.int32)

    error_send = project(x, w, t, info(1 - core), scale)
    error_got = swap(error_send, "fsdp", 1)
    error_keep = project(x, w, t, info(core), scale)

    def chip_sum(keep, got, place):
        return lax.dynamic_index_in_dim(keep, place, 0, False).astype(F32) + lax.dynamic_index_in_dim(
            got, place, 0, False
        ).astype(F32)

    def spread(keep, got):
        received = [
            swap(chip_sum(keep, got, chip ^ k).astype(BF16), "fsdp", 2 * k) for k in range(1, chips)
        ]
        return chip_sum(keep, got, chip), received

    def collect(piece):
        return jnp.stack([piece] + [swap(piece, "fsdp", 2 * k) for k in range(1, chips)])

    cut = (chips, gram_keep.shape[0] // chips, LANES)
    gram_own, gram_parts_got = spread(gram_keep.reshape(cut), gram_got.reshape(cut))
    for part in gram_parts_got:
        gram_own = gram_own + part.astype(F32)
    gram_mine = collect(gram_own.astype(BF16))
    gram_other = swap(gram_mine, "fsdp", 1)
    mine_at = jnp.stack([core * chips + (chip ^ k) for k in range(chips)]).astype(jnp.int32)
    other_at = jnp.stack([(1 - core) * chips + (chip ^ k) for k in range(chips)]).astype(jnp.int32)
    gram = whole_gram(jnp.concatenate([mine_at, other_at]), gram_mine, gram_other, tokens)

    error_own, error_parts = spread(error_keep, error_got)
    moved = residual(error_own, error_parts, gram)
    mine = collect(moved)
    other = swap(mine, "fsdp", 1)
    first = weight_step(turned, mine, mine_at, w, inner_rate * scale, None)
    return weight_step(turned, other, other_at, w, inner_rate * scale, first)


def plain_outer(outer, moment, rep_rows):
    replica_rows = rep_rows.astype(F32)
    delta = lax.psum(outer - replica_rows, "rep") / lax.axis_size("rep")
    new_moment = momentum_coef * moment + delta
    new_outer = outer - outer_rate * (delta + momentum_coef * new_moment)
    mixed = merge_keep * replica_rows + (1.0 - merge_keep) * new_outer
    return new_outer, new_moment, mixed.astype(BF16)


def plain_inner(x, t, w):
    scale = (x.shape[1] * lax.axis_size("fsdp")) ** -0.5
    for _ in range(INNER):
        part = jnp.dot(x, w.astype(BF16), preferred_element_type=F32).astype(BF16)
        predicted = lax.psum_scatter(part, "fsdp", scatter_dimension=0, tiled=True).astype(F32) * scale
        errors = lax.all_gather((predicted - t.astype(F32)).astype(BF16), "fsdp", axis=0, tiled=True)
        gradient = lax.dot_general(x, errors, (((0,), (0,)), ((), ())), preferred_element_type=F32)
        w = w - inner_rate * scale * gradient
    return w


def power_of_two(value):
    return value > 1 and value & (value - 1) == 0


def local(tokens, targets, inner_weights, outer_weights, outer_momentum, replica_weights):
    x, t, w, rep_rows = tokens[0], targets[0], inner_weights[0], replica_weights[0]
    replicas, shards = lax.axis_size("rep"), lax.axis_size("fsdp")
    if power_of_two(replicas) and rep_rows.shape[0] % (32 * replicas) == 0:
        new_outer, new_moment, merged = outer_sync(outer_weights, outer_momentum, rep_rows)
    else:
        new_outer, new_moment, merged = plain_outer(outer_weights, outer_momentum, rep_rows)
    tiles = x.shape[0] // LANES
    if (
        power_of_two(shards)
        and w.shape[1] == shards * LANES
        and x.shape[0] % LANES == 0
        and tiles * (tiles + 1) // 2 * LANES % (16 * shards) == 0
    ):
        new_inner = inner_run(x, t, w)
    else:
        new_inner = plain_inner(x, t, w)
    return new_inner[None], new_outer, new_moment, merged[None]


def solution(mesh):
    placed = (
        P("rep", None, "fsdp"),
        P("rep", "fsdp", None),
        P("rep", "fsdp", None),
        P("fsdp", None),
        P("fsdp", None),
        P("rep", "fsdp", None),
    )
    return jax.shard_map(
        local,
        mesh=mesh,
        in_specs=placed,
        out_specs=(
            P("rep", "fsdp", None),
            P("fsdp", None),
            P("fsdp", None),
            P("rep", "fsdp", None),
        ),
        check_vma=False,
    )
```

time: 218 us -> 90.8 us (0.42)
  waiting for transfers between devices: 152 us -> 18.5 us
  starting transfers between devices: 0.21 us -> 30.2 us
  Pallas kernels: 0 us -> 21 us
  matrix products: 16.3 us -> 0 us
  between operations: 15.3 us -> 0.86 us
  other arithmetic: 19.7 us -> 10.4 us
  local copies, waits for them, and re-layouts: 13.9 us -> 9.5 us
    psum x1 -> x0, waiting for transfers between devices: 74.7 us -> none  [outer_sync(): pseudo_sum = lax.psum(replica_term, 'rep')]
    reduce_scatter x2 -> x0, waiting for transfers between devices: 61.9 us -> none  [inner_run(): lax.psum_scatter(jnp.dot(token_cols, weights_half, preferred_element_type...]
    ppermute x0 -> x24, starting transfers between devices: none -> 30.2 us  [swap(): return lax.ppermute(value, axis, [(i, i ^ flip) for i in range(count)])]
    pallas_call x0 -> x9, Pallas kernels: none -> 21 us  [the longest x2 7.53 us: outer_update(): pl.pallas_call(functools.partial(update_kernel, replicas, blocks), out_sh...]
    ppermute x0 -> x24, waiting for transfers between devices: none -> 18.5 us  [swap(): return lax.ppermute(value, axis, [(i, i ^ flip) for i in range(count)])]
    dot_general x4 -> x0, matrix products: 16.3 us -> none  [the longest x2 9.58 us: inner_run(): lax.dot_general(token_cols, lax.all_gather(errors, 'fsdp', axis=0, tiled=...]
    all_gather x2 -> x0, waiting for transfers between devices: 15.5 us -> none  [inner_run(): lax.all_gather(errors, 'fsdp', axis=0, tiled=True)]
    broadcast_in_dim x1 -> x0, other arithmetic: 11.3 us -> none  [outer_sync(): merged = mixed.astype(jnp.bfloat16)[None]]
  transfers between devices with their start and end apart: 5 -> 24, of which waited for: 4 -> 5; matrix products, arithmetic and copies ran while one was open for 11% -> 14% of each run, Pallas kernels for 0% -> 17%
where the time goes in v1:
time: 90.8 us; the launch traced here: 90.4 us
  starting transfers between devices  30.2 us (33%)
  Pallas kernels  21 us (23%)
  waiting for transfers between devices  18.5 us (20%)
  other arithmetic  10.4 us (11%)
  local copies, waits for them, and re-layouts  9.5 us (10%)
    ppermute x24, starting transfers between devices, swap(): return lax.ppermute(value, axis, [(i, i ^ flip) for i in range(count)])  30.2 us
    ppermute x24, waiting for transfers between devices, swap(): return lax.ppermute(value, axis, [(i, i ^ flip) for i in range(count)])  18.5 us
    pallas_call x2, Pallas kernels, outer_update(): pl.pallas_call(functools.partial(update_kernel, replicas, blocks), out_sh...  7.53 us
    pallas_call x2, Pallas kernels, weight_step(): pl.pallas_call(functools.partial(step_kernel, rate), out_shape=jax.ShapeD...  7.46 us
    unnamed x26, local copies, waits for them, and re-layouts  7.04 us
    pallas_call x2, Pallas kernels, project(): pl.pallas_call(functools.partial(project_kernel, scale), out_shape=jax.Sh...  3.49 us
    select_n x2, other arithmetic, outer_sync(): jnp.where(set_bits[s] == 0, jnp.concatenate([codes[s], got[s]], 0), jnp.c...  2.7 us
    dynamic_slice x1, local copies, waits for them, and re-layouts, row_slice(): return lax.dynamic_slice_in_dim(value, start, size, 0)  2.38 us
  transfers between devices with their start and end apart: 24, of which 5 were waited for; matrix products, arithmetic and copies ran while one was open for 14% of the time, Pallas kernels for 17%

profile of v1, /device:TPU:0, one launch (start us, length us, event | category | flops | bytes accessed | tf_op | source)
XLA Modules:
  0.0 90.4 jit_solution(7115233818671185025)
XLA Ops:
  4.8 2.4 %dynamic-slice_bitcast_fusion = (bf16[256,1024]{1,0:T(8,128)(2,1)}, bf16[256,1024]{1,0:T(8,128)(2,1)}) fusion(bf16[1,1024,1024]{2,1,0:T(8,128)(2,1)} %param.11, s32[]{:T(128)S(6)} %select_n.145, s32[]{:T(128)S(6)} %select_n.132), kind=kLoop, calls=%fused_computation.21 | loop fusion | bytes 2097160 | tf_op jit(solution)/shard_map/dynamic_slice | solution.py:57
  7.2 2.5 %collective-permute-start.16 = (bf16[256,1024]{1,0:T(8,128)(2,1)}, bf16[256,1024]{1,0:T(8,128)(2,1)}, u32[]{:S(2)}, u32[]{:S(2)}) collective-permute-start(bf16[256,1024]{1,0:T(8,128)(2,1)} %get-tuple-element.29), channel_id=1, source_target_pairs={{0,8},{8,0},{16,24},{24,16},{1,9},{9,1},{17,25},{25,17},{2,10},{10... | collective-permute-start | bytes 1572872 | tf_op jit(solution)/shard_map/ppermute | solution.py:45
  12.7 1.6 %collective-permute-start.5 = (bf16[160,128]{1,0:T(8,128)(2,1)}, bf16[160,128]{1,0:T(8,128)(2,1)S(1)}, u32[]{:S(2)}, u32[]{:S(2)}) collective-permute-start(bf16[160,128]{1,0:T(8,128)(2,1)} %get-tuple-element.34), channel_id=1, source_target_pairs={{0,2},{1,3},{2,0},{3,1},{4,6},{5,7},{6,4},{7,5},{8,10},{9,11},{10,... | collective-permute-start | bytes 122888 | tf_op jit(solution)/shard_map/ppermute | solution.py:45
  14.2 2.6 %collective-permute-start.6 = (bf16[160,128]{1,0:T(8,128)(2,1)}, bf16[160,128]{1,0:T(8,128)(2,1)}, u32[]{:S(2)}, u32[]{:S(2)}) collective-permute-start(bf16[160,128]{1,0:T(8,128)(2,1)} %get-tuple-element.36), channel_id=1, source_target_pairs={{0,4},{1,5},{2,6},{3,7},{4,0},{5,1},{6,2},{7,3},{8,12},{9,13},{10,... | collective-permute-start | bytes 122888 | tf_op jit(solution)/shard_map/ppermute | solution.py:45
  17.2 2.9 %collective-permute-done.6 = bf16[160,128]{1,0:T(8,128)(2,1)} collective-permute-done((bf16[160,128]{1,0:T(8,128)(2,1)}, bf16[160,128]{1,0:T(8,128)(2,1)}, u32[]{:S(2)}, u32[]{:S(2)}) %collective-permute-start.6) | collective-permute-done | bytes 40992 | tf_op jit(solution)/shard_map/ppermute | solution.py:45
  20.1 2.6 %collective-permute-done.7 = bf16[160,128]{1,0:T(8,128)(2,1)} collective-permute-done((bf16[160,128]{1,0:T(8,128)(2,1)S(1)}, bf16[160,128]{1,0:T(8,128)(2,1)}, u32[]{:S(2)}, u32[]{:S(2)}) %collective-permute-start.7) | collective-permute-done | bytes 40992 | tf_op jit(solution)/shard_map/ppermute | solution.py:45
  24.9 3.2 %collective-permute-start.10 = (bf16[160,128]{1,0:T(8,128)(2,1)S(1)}, bf16[160,128]{1,0:T(8,128)(2,1)S(1)}, u32[]{:S(2)}, u32[]{:S(2)}) collective-permute-start(bf16[160,128]{1,0:T(8,128)(2,1)S(1)} %fusion.11), channel_id=1, source_target_pairs={{0,6},{1,7},{2,4},{3,5},{4,2},{5,3},{6,0},{7,1},{8,14},{9,15},{10,... | collective-permute-start | bytes 122888 | tf_op jit(solution)/shard_map/ppermute | solution.py:45
  28.1 2.2 %copy-done = f32[1,1024,1024]{2,1,0:T(8,128)S(1)} copy-done((f32[1,1024,1024]{2,1,0:T(8,128)S(1)}, f32[1,1024,1024]{2,1,0:T(8,128)}, u32[]{:S(2)}) %copy-start) | copy-done | bytes 4194328
  30.2 1.7 %project.3 = bf16[4,512,128]{2,1,0:T(8,128)(2,1)S(1)} custom-call(s32[2]{0:T(128)S(1)} %pad_add_fusion.2.info_ref, bf16[512,1024]{1,0:T(8,128)(2,1)S(1)} %bitcast.70, f32[1024,1024]{1,0:T(8,128)S(1)} %bitcast.63, bf16[64,1024]{1,0:T(8,128)(2,1)S(1)} %bitcast.72), custom_call_target="tpu_custom_call" | custom-call | flops 536870912 | bytes 3145728 | tf_op jit(solution)/shard_map/project/pallas_call | solution.py:233
  32.7 1.9 %convert_add_fusion = (f32[256,1024]{1,0:T(8,128)S(1)}, f32[256,1024]{1,0:T(8,128)S(1)}) fusion(bf16[256,1024]{1,0:T(8,128)(2,1)} %collective-permute-done.20, bf16[1,1024,1024]{2,1,0:T(8,128)(2,1)S(1)} %copy-done.6, s32[]{:T(128)S(6)} %select_n.144, bf16[256,1024]{1,0:T(8,128)(2,1)} %collective-permute-done.16, s32[]{:T(128)S(6)} %select_n.131), kind=kLoop, calls=%fused_computation | loop fusion | flops 1572864 | bytes 4194312 | tf_op jit(solution)/shard_map/add | solution.py:153
  36.2 1.7 %project.2 = bf16[4,512,128]{2,1,0:T(8,128)(2,1)S(1)} custom-call(s32[2]{0:T(128)S(1)} %pad_add_fusion.1.info_ref, bf16[512,1024]{1,0:T(8,128)(2,1)S(1)} %bitcast.71, f32[1024,1024]{1,0:T(8,128)S(1)} %bitcast.64, bf16[64,1024]{1,0:T(8,128)(2,1)S(1)} %bitcast.73), custom_call_target="tpu_custom_call" | custom-call | flops 536870912 | bytes 3145728 | tf_op jit(solution)/shard_map/project/pallas_call | solution.py:233
  38.9 1.5 %collective-permute-start.2 = (bf16[512,128]{1,0:T(8,128)(2,1)S(1)}, bf16[512,128]{1,0:T(8,128)(2,1)S(1)}, u32[]{:S(2)}, u32[]{:S(2)}) collective-permute-start(bf16[512,128]{1,0:T(8,128)(2,1)S(1)} %get-tuple-element.31), channel_id=1, source_target_pairs={{0,4},{1,5},{2,6},{3,7},{4,0},{5,1},{6,2},{7,3},{8,12},{9,13},{10,... | collective-permute-start | bytes 393224 | tf_op jit(solution)/shard_map/ppermute | solution.py:45
  40.4 2.8 %collective-permute-start.3 = (bf16[512,128]{1,0:T(8,128)(2,1)S(1)}, bf16[512,128]{1,0:T(8,128)(2,1)S(1)}, u32[]{:S(2)}, u32[]{:S(2)}) collective-permute-start(bf16[512,128]{1,0:T(8,128)(2,1)S(1)} %get-tuple-element.30), channel_id=1, source_target_pairs={{0,6},{1,7},{2,4},{3,5},{4,2},{5,3},{6,0},{7,1},{8,14},{9,15},{10,... | collective-permute-start | bytes 393224 | tf_op jit(solution)/shard_map/ppermute | solution.py:45
  46.1 5.4 %collective-permute-done.2.refs_1_ = bf16[512,128]{1,0:T(8,128)(2,1)S(1)} collective-permute-done((bf16[512,128]{1,0:T(8,128)(2,1)S(1)}, bf16[512,128]{1,0:T(8,128)(2,1)S(1)}, u32[]{:S(2)}, u32[]{:S(2)}) %collective-permute-start.2) | collective-permute-done | bytes 131104 | tf_op jit(solution)/shard_map/ppermute | solution.py:45
  51.8 2.0 %collective-permute-start.12 = (bf16[512,128]{1,0:T(8,128)(2,1)S(1)}, bf16[512,128]{1,0:T(8,128)(2,1)}, u32[]{:S(2)}, u32[]{:S(2)}) collective-permute-start(bf16[512,128]{1,0:T(8,128)(2,1)S(1)} %residual.1), channel_id=1, source_target_pairs={{0,2},{1,3},{2,0},{3,1},{4,6},{5,7},{6,4},{7,5},{8,10},{9,11},{10,... | collective-permute-start | bytes 393224 | tf_op jit(solution)/shard_map/ppermute | solution.py:45
  54.2 2.1 %collective-permute-start.14 = (bf16[512,128]{1,0:T(8,128)(2,1)S(1)}, bf16[512,128]{1,0:T(8,128)(2,1)}, u32[]{:S(2)}, u32[]{:S(2)}) collective-permute-start(bf16[512,128]{1,0:T(8,128)(2,1)S(1)} %residual.1), channel_id=1, source_target_pairs={{0,6},{1,7},{2,4},{3,5},{4,2},{5,3},{6,0},{7,1},{8,14},{9,15},{10,... | collective-permute-start | bytes 393224 | tf_op jit(solution)/shard_map/ppermute | solution.py:45
  58.3 7.0 %collective-permute-done.13 = bf16[512,128]{1,0:T(8,128)(2,1)} collective-permute-done((bf16[512,128]{1,0:T(8,128)(2,1)S(1)}, bf16[512,128]{1,0:T(8,128)(2,1)}, u32[]{:S(2)}, u32[]{:S(2)}) %collective-permute-start.13) | collective-permute-done | bytes 131104 | tf_op jit(solution)/shard_map/ppermute | solution.py:45
  68.0 1.6 %collective-permute-start.23 = (bf16[256,1024]{1,0:T(8,128)(2,1)S(1)}, bf16[256,1024]{1,0:T(8,128)(2,1)S(1)}, u32[]{:S(2)}, u32[]{:S(2)}) collective-permute-start(bf16[256,1024]{1,0:T(8,128)(2,1)S(1)} %maximum_select_fusion.1.code_b), channel_id=1, source_target_pairs={{0,16},{8,24},{16,0},{24,8},{1,17},{9,25},{17,1},{25,9},{2,18},{10... | collective-permute-start | bytes 1572872 | tf_op jit(solution)/shard_map/ppermute | solution.py:45
  70.9 1.6 %collective-permute-start.19 = (bf16[256,1024]{1,0:T(8,128)(2,1)S(1)}, bf16[256,1024]{1,0:T(8,128)(2,1)S(1)}, u32[]{:S(2)}, u32[]{:S(2)}) collective-permute-start(bf16[256,1024]{1,0:T(8,128)(2,1)S(1)} %maximum_select_fusion.code_a), channel_id=1, source_target_pairs={{0,8},{8,0},{16,24},{24,16},{1,9},{9,1},{17,25},{25,17},{2,10},{10... | collective-permute-start | bytes 1572872 | tf_op jit(solution)/shard_map/ppermute | solution.py:45
  72.7 2.2 %copy-done.2 = f32[1,1024,1024]{2,1,0:T(8,128)S(1)} copy-done((f32[1,1024,1024]{2,1,0:T(8,128)S(1)}, f32[1,1024,1024]{2,1,0:T(8,128)}, u32[]{:S(2)}) %copy-start.2) | copy-done | bytes 4194328
  74.9 3.7 %weight_step.2.refs_2_ = f32[1024,1024]{1,0:T(8,128)} custom-call(s32[4]{0:T(128)S(1)} %pad_add_fusion.3.pos_ref, bf16[1024,512]{1,0:T(8,128)(2,1)S(1)} %copy-done.11, bf16[4,512,128]{2,1,0:T(8,128)(2,1)S(1)} %pad_maximum_fusion.refs_0_, f32[1024,1024]{1,0:T(8,128)S(1)} %bitcast.65), custom_call_target="tpu_custom_call" | custom-call | flops 536870912 | bytes 4194304 | tf_op jit(solution)/shard_map/weight_step/pallas_call | solution.py:318
  79.1 3.8 %outer_update.2 = (f32[1024,1024]{1,0:T(8,128)}, f32[1024,1024]{1,0:T(8,128)}, bf16[1024,1024]{1,0:T(8,128)(2,1)}) custom-call(s32[2]{0:T(128)S(1)} %pad_add_fusion.5.pos_ref, bf16[256,1024]{1,0:T(8,128)(2,1)S(1)} %maximum_select_fusion.code_a, bf16[256,1024]{1,0:T(8,128)(2,1)S(1)} %maximum_select_fusion.1.code_b, f32[1024,1024]{1,0:T(8,128)S(1)} %copy-done.5, ...), custom_call_target="tpu_custom_call" | custom-call | flops 5242880 | bytes 11534336 | tf_op jit(solution)/shard_map/outer_update/pallas_call | solution.py:101
  82.9 3.7 %weight_step.3 = f32[1024,1024]{1,0:T(8,128)} custom-call(s32[4]{0:T(128)S(1)} %pad_add_fusion.pos_ref, bf16[1024,512]{1,0:T(8,128)(2,1)S(1)} %copy-done.11, bf16[4,512,128]{2,1,0:T(8,128)(2,1)S(1)} %collective-permute-done.15.refs_0_, f32[1024,1024]{1,0:T(8,128)S(1)} %bitcast.66, f32[1024,1024]{1,0:T(8,128)} %weight_step.2.refs_2_), custom_call_target="tpu_custom_call", output_to_operand_aliasing={{}: (4, {})} | custom-call | flops 536870912 | bytes 4194304 | tf_op jit(solution)/shard_map/weight_step/pallas_call | solution.py:318
  86.6 3.8 %outer_update.3 = (f32[1024,1024]{1,0:T(8,128)}, f32[1024,1024]{1,0:T(8,128)}, bf16[1024,1024]{1,0:T(8,128)(2,1)}) custom-call(s32[2]{0:T(128)S(1)} %pad_add_fusion.4.pos_ref, bf16[256,1024]{1,0:T(8,128)(2,1)S(1)} %collective-permute-done.19.code_a, ...), custom_call_target="tpu_custom_call", output_to_operand_aliasing={{0}: (6, {}), {1}: (7, {}), {2}: (8, {})} | custom-call | flops 5242880 | bytes 11534336 | tf_op jit(solution)/shard_map/outer_update/pallas_call | solution.py:101
  (77 shorter events, 23.0 us)
Async XLA Ops:
  4.3 6.8 %collective-permute-start.4 = (bf16[640,128]{1,0:T(8,128)(2,1)}, bf16[640,128]{1,0:T(8,128)(2,1)}, u32[]{:S(2)}, u32[]{:S(2)}) collective-permute-start(bf16[640,128]{1,0:T(8,128)(2,1)} %get-tuple-element.15), channel_id=1, source_target_pairs={{0,1},{1,0},{2,3},{3,2},{4,5},{5,4},{6,7},{7,6},{8,9},{9,8},{10,11... | collective-permute-start | bytes 491528 | tf_op jit(solution)/shard_map/ppermute | solution.py:45
  7.2 25.5 %collective-permute-start.16 = (bf16[256,1024]{1,0:T(8,128)(2,1)}, bf16[256,1024]{1,0:T(8,128)(2,1)}, u32[]{:S(2)}, u32[]{:S(2)}) collective-permute-start(bf16[256,1024]{1,0:T(8,128)(2,1)} %get-tuple-element.29), channel_id=1, source_target_pairs={{0,8},{8,0},{16,24},{24,16},{1,9},{9,1},{17,25},{25,17},{2,10},{10... | collective-permute-start | bytes 1572872 | tf_op jit(solution)/shard_map/ppermute | solution.py:45
  9.7 23.0 %collective-permute-start.20 = (bf16[256,1024]{1,0:T(8,128)(2,1)}, bf16[256,1024]{1,0:T(8,128)(2,1)}, u32[]{:S(2)}, u32[]{:S(2)}) collective-permute-start(bf16[256,1024]{1,0:T(8,128)(2,1)} %get-tuple-element.28), channel_id=1, source_target_pairs={{0,16},{8,24},{16,0},{24,8},{1,17},{9,25},{17,1},{25,9},{2,18},{10... | collective-permute-start | bytes 1572872 | tf_op jit(solution)/shard_map/ppermute | solution.py:45
  12.7 4.6 %collective-permute-start.5 = (bf16[160,128]{1,0:T(8,128)(2,1)}, bf16[160,128]{1,0:T(8,128)(2,1)S(1)}, u32[]{:S(2)}, u32[]{:S(2)}) collective-permute-start(bf16[160,128]{1,0:T(8,128)(2,1)} %get-tuple-element.34), channel_id=1, source_target_pairs={{0,2},{1,3},{2,0},{3,1},{4,6},{5,7},{6,4},{7,5},{8,10},{9,11},{10,... | collective-permute-start | bytes 122888 | tf_op jit(solution)/shard_map/ppermute | solution.py:45
  14.2 5.9 %collective-permute-start.6 = (bf16[160,128]{1,0:T(8,128)(2,1)}, bf16[160,128]{1,0:T(8,128)(2,1)}, u32[]{:S(2)}, u32[]{:S(2)}) collective-permute-start(bf16[160,128]{1,0:T(8,128)(2,1)} %get-tuple-element.36), channel_id=1, source_target_pairs={{0,4},{1,5},{2,6},{3,7},{4,0},{5,1},{6,2},{7,3},{8,12},{9,13},{10,... | collective-permute-start | bytes 122888 | tf_op jit(solution)/shard_map/ppermute | solution.py:45
  16.8 5.9 %collective-permute-start.7 = (bf16[160,128]{1,0:T(8,128)(2,1)S(1)}, bf16[160,128]{1,0:T(8,128)(2,1)}, u32[]{:S(2)}, u32[]{:S(2)}) collective-permute-start(bf16[160,128]{1,0:T(8,128)(2,1)S(1)} %get-tuple-element.35), channel_id=1, source_target_pairs={{0,6},{1,7},{2,4},{3,5},{4,2},{5,3},{6,0},{7,1},{8,14},{9,15},{10,... | collective-permute-start | bytes 122888 | tf_op jit(solution)/shard_map/ppermute | solution.py:45
  23.6 8.4 %collective-permute-start.8 = (bf16[160,128]{1,0:T(8,128)(2,1)S(1)}, bf16[160,128]{1,0:T(8,128)(2,1)S(1)}, u32[]{:S(2)}, u32[]{:S(2)}) collective-permute-start(bf16[160,128]{1,0:T(8,128)(2,1)S(1)} %fusion.11), channel_id=1, source_target_pairs={{0,2},{1,3},{2,0},{3,1},{4,6},{5,7},{6,4},{7,5},{8,10},{9,11},{10,... | collective-permute-start | bytes 122888 | tf_op jit(solution)/shard_map/ppermute | solution.py:45
  23.7 8.4 %collective-permute-start.9 = (bf16[160,128]{1,0:T(8,128)(2,1)S(1)}, bf16[160,128]{1,0:T(8,128)(2,1)S(1)}, u32[]{:S(2)}, u32[]{:S(2)}) collective-permute-start(bf16[160,128]{1,0:T(8,128)(2,1)S(1)} %fusion.11), channel_id=1, source_target_pairs={{0,4},{1,5},{2,6},{3,7},{4,0},{5,1},{6,2},{7,3},{8,12},{9,13},{10,... | collective-permute-start | bytes 122888 | tf_op jit(solution)/shard_map/ppermute | solution.py:45
  24.9 7.2 %collective-permute-start.10 = (bf16[160,128]{1,0:T(8,128)(2,1)S(1)}, bf16[160,128]{1,0:T(8,128)(2,1)S(1)}, u32[]{:S(2)}, u32[]{:S(2)}) collective-permute-start(bf16[160,128]{1,0:T(8,128)(2,1)S(1)} %fusion.11), channel_id=1, source_target_pairs={{0,6},{1,7},{2,4},{3,5},{4,2},{5,3},{6,0},{7,1},{8,14},{9,15},{10,... | collective-permute-start | bytes 122888 | tf_op jit(solution)/shard_map/ppermute | solution.py:45
  32.0 6.6 %collective-permute-start = (bf16[4,512,128]{2,1,0:T(8,128)(2,1)S(1)}, bf16[4,512,128]{2,1,0:T(8,128)(2,1)S(1)}, u32[]{:S(2)}, u32[]{:S(2)}) collective-permute-start(bf16[4,512,128]{2,1,0:T(8,128)(2,1)S(1)} %project.3), channel_id=1, source_target_pairs={{0,1},{1,0},{2,3},{3,2},{4,5},{5,4},{6,7},{7,6},{8,9},{9,8},{10,11... | collective-permute-start | bytes 1572872 | tf_op jit(solution)/shard_map/ppermute | solution.py:45
  32.2 5.8 %collective-permute-start.11 = (bf16[4,160,128]{2,1,0:T(8,128)(2,1)S(1)}, bf16[4,160,128]{2,1,0:T(8,128)(2,1)S(1)}, u32[]{:S(2)}, u32[]{:S(2)}) collective-permute-start(bf16[4,160,128]{2,1,0:T(8,128)(2,1)S(1)} %pad_maximum_fusion.1.mine_ref), channel_id=1, source_target_pairs={{0,1},{1,0},{2,3},{3,2},{4,5},{5,4},{6,7},{7,6},{8,9},{9,8},{10,11... | collective-permute-start | bytes 491528 | tf_op jit(solution)/shard_map/ppermute | solution.py:45
  35.0 8.3 %collective-permute-start.17 = (bf16[128,1024]{1,0:T(8,128)(2,1)S(1)}, bf16[128,1024]{1,0:T(8,128)(2,1)S(1)}, u32[]{:S(2)}, u32[]{:S(2)}) collective-permute-start(bf16[128,1024]{1,0:T(8,128)(2,1)S(1)} %get-tuple-element.25), channel_id=1, source_target_pairs={{0,16},{8,24},{16,0},{24,8},{1,17},{9,25},{17,1},{25,9},{2,18},{10... | collective-permute-start | bytes 786440 | tf_op jit(solution)/shard_map/ppermute | solution.py:45
  35.6 7.7 %collective-permute-start.21 = (bf16[128,1024]{1,0:T(8,128)(2,1)S(1)}, bf16[128,1024]{1,0:T(8,128)(2,1)S(1)}, u32[]{:S(2)}, u32[]{:S(2)}) collective-permute-start(bf16[128,1024]{1,0:T(8,128)(2,1)S(1)} %get-tuple-element.24), channel_id=1, source_target_pairs={{0,8},{8,0},{16,24},{24,16},{1,9},{9,1},{17,25},{25,17},{2,10},{10... | collective-permute-start | bytes 786440 | tf_op jit(solution)/shard_map/ppermute | solution.py:45
  38.8 7.3 %collective-permute-start.1 = (bf16[512,128]{1,0:T(8,128)(2,1)S(1)}, bf16[512,128]{1,0:T(8,128)(2,1)S(1)}, u32[]{:S(2)}, u32[]{:S(2)}) collective-permute-start(bf16[512,128]{1,0:T(8,128)(2,1)S(1)} %get-tuple-element.32), channel_id=1, source_target_pairs={{0,2},{1,3},{2,0},{3,1},{4,6},{5,7},{6,4},{7,5},{8,10},{9,11},{10,... | collective-permute-start | bytes 393224 | tf_op jit(solution)/shard_map/ppermute | solution.py:45
  38.9 12.6 %collective-permute-start.2 = (bf16[512,128]{1,0:T(8,128)(2,1)S(1)}, bf16[512,128]{1,0:T(8,128)(2,1)S(1)}, u32[]{:S(2)}, u32[]{:S(2)}) collective-permute-start(bf16[512,128]{1,0:T(8,128)(2,1)S(1)} %get-tuple-element.31), channel_id=1, source_target_pairs={{0,4},{1,5},{2,6},{3,7},{4,0},{5,1},{6,2},{7,3},{8,12},{9,13},{10,... | collective-permute-start | bytes 393224 | tf_op jit(solution)/shard_map/ppermute | solution.py:45
  40.4 11.1 %collective-permute-start.3 = (bf16[512,128]{1,0:T(8,128)(2,1)S(1)}, bf16[512,128]{1,0:T(8,128)(2,1)S(1)}, u32[]{:S(2)}, u32[]{:S(2)}) collective-permute-start(bf16[512,128]{1,0:T(8,128)(2,1)S(1)} %get-tuple-element.30), channel_id=1, source_target_pairs={{0,6},{1,7},{2,4},{3,5},{4,2},{5,3},{6,0},{7,1},{8,14},{9,15},{10,... | collective-permute-start | bytes 393224 | tf_op jit(solution)/shard_map/ppermute | solution.py:45
  44.6 21.9 %collective-permute-start.22 = (bf16[128,1024]{1,0:T(8,128)(2,1)}, bf16[128,1024]{1,0:T(8,128)(2,1)}, u32[]{:S(2)}, u32[]{:S(2)}) collective-permute-start(bf16[128,1024]{1,0:T(8,128)(2,1)} %get-tuple-element.22), channel_id=1, source_target_pairs={{0,8},{8,0},{16,24},{24,16},{1,9},{9,1},{17,25},{25,17},{2,10},{10... | collective-permute-start | bytes 786440 | tf_op jit(solution)/shard_map/ppermute | solution.py:45
  51.8 6.5 %collective-permute-start.12 = (bf16[512,128]{1,0:T(8,128)(2,1)S(1)}, bf16[512,128]{1,0:T(8,128)(2,1)}, u32[]{:S(2)}, u32[]{:S(2)}) collective-permute-start(bf16[512,128]{1,0:T(8,128)(2,1)S(1)} %residual.1), channel_id=1, source_target_pairs={{0,2},{1,3},{2,0},{3,1},{4,6},{5,7},{6,4},{7,5},{8,10},{9,11},{10,... | collective-permute-start | bytes 393224 | tf_op jit(solution)/shard_map/ppermute | solution.py:45
  53.9 11.5 %collective-permute-start.13 = (bf16[512,128]{1,0:T(8,128)(2,1)S(1)}, bf16[512,128]{1,0:T(8,128)(2,1)}, u32[]{:S(2)}, u32[]{:S(2)}) collective-permute-start(bf16[512,128]{1,0:T(8,128)(2,1)S(1)} %residual.1), channel_id=1, source_target_pairs={{0,4},{1,5},{2,6},{3,7},{4,0},{5,1},{6,2},{7,3},{8,12},{9,13},{10,... | collective-permute-start | bytes 393224 | tf_op jit(solution)/shard_map/ppermute | solution.py:45
  54.2 11.1 %collective-permute-start.14 = (bf16[512,128]{1,0:T(8,128)(2,1)S(1)}, bf16[512,128]{1,0:T(8,128)(2,1)}, u32[]{:S(2)}, u32[]{:S(2)}) collective-permute-start(bf16[512,128]{1,0:T(8,128)(2,1)S(1)} %residual.1), channel_id=1, source_target_pairs={{0,6},{1,7},{2,4},{3,5},{4,2},{5,3},{6,0},{7,1},{8,14},{9,15},{10,... | collective-permute-start | bytes 393224 | tf_op jit(solution)/shard_map/ppermute | solution.py:45
  56.3 13.3 %collective-permute-start.18 = (bf16[128,1024]{1,0:T(8,128)(2,1)S(1)}, bf16[128,1024]{1,0:T(8,128)(2,1)}, u32[]{:S(2)}, u32[]{:S(2)}) collective-permute-start(bf16[128,1024]{1,0:T(8,128)(2,1)S(1)} %get-tuple-element.23), channel_id=1, source_target_pairs={{0,16},{8,24},{16,0},{24,8},{1,17},{9,25},{17,1},{25,9},{2,18},{10... | collective-permute-start | bytes 786440 | tf_op jit(solution)/shard_map/ppermute | solution.py:45
  66.5 16.4 %collective-permute-start.15 = (bf16[4,512,128]{2,1,0:T(8,128)(2,1)S(1)}, bf16[4,512,128]{2,1,0:T(8,128)(2,1)S(1)}, u32[]{:S(2)}, u32[]{:S(2)}) collective-permute-start(bf16[4,512,128]{2,1,0:T(8,128)(2,1)S(1)} %pad_maximum_fusion.refs_0_), channel_id=1, source_target_pairs={{0,1},{1,0},{2,3},{3,2},{4,5},{5,4},{6,7},{7,6},{8,9},{9,8},{10,11... | collective-permute-start | bytes 1572872 | tf_op jit(solution)/shard_map/ppermute | solution.py:45
  68.0 18.6 %collective-permute-start.23 = (bf16[256,1024]{1,0:T(8,128)(2,1)S(1)}, bf16[256,1024]{1,0:T(8,128)(2,1)S(1)}, u32[]{:S(2)}, u32[]{:S(2)}) collective-permute-start(bf16[256,1024]{1,0:T(8,128)(2,1)S(1)} %maximum_select_fusion.1.code_b), channel_id=1, source_target_pairs={{0,16},{8,24},{16,0},{24,8},{1,17},{9,25},{17,1},{25,9},{2,18},{10... | collective-permute-start | bytes 1572872 | tf_op jit(solution)/shard_map/ppermute | solution.py:45
  70.9 15.7 %collective-permute-start.19 = (bf16[256,1024]{1,0:T(8,128)(2,1)S(1)}, bf16[256,1024]{1,0:T(8,128)(2,1)S(1)}, u32[]{:S(2)}, u32[]{:S(2)}) collective-permute-start(bf16[256,1024]{1,0:T(8,128)(2,1)S(1)} %maximum_select_fusion.code_a), channel_id=1, source_target_pairs={{0,8},{8,0},{16,24},{24,16},{1,9},{9,1},{17,25},{25,17},{2,10},{10... | collective-permute-start | bytes 1572872 | tf_op jit(solution)/shard_map/ppermute | solution.py:45
  (13 other events, 141.0 us)

commit v2 on v0

v2 whole, which is shorter than its diff:
```python
import functools

import jax
import jax.numpy as jnp
from jax import lax
from jax.experimental import pallas as pl
from jax.experimental.pallas import tpu as pltpu
from jax.sharding import PartitionSpec as P

INNER = 2

inner_rate = 0.5
momentum_coef = 0.9
outer_rate = 0.7
merge_keep = 0.5

F32 = jnp.float32
BF16 = jnp.bfloat16
LANES = 128
SPAN = 2 * LANES
MIB = 1 << 20

CODE_SCALE = 2.0**60
CODE_LEAST = 2.0**-30
CODE_CUT = 2.0**20


WEIGHT = {
    "opening": 4,
    "project": 1,
    "add_1": 0,
    "add_2": 0,
    "add_3": 0,
    "fold_1": 0,
    "fold_2": 400,
    "code_1": 0,
    "code_2": 0,
    "code_3": 0,
    "code_4": 0,
    "whole_gram": 0,
    "residual": 0,
    "near_update": 40,
    "weight_step": 10,
    "far_update": 10,
}


def encode(total, outer_rows, count):
    away = count * outer_rows - total
    held = jnp.where(jnp.abs(total) < CODE_LEAST, CODE_LEAST, total) * CODE_SCALE
    return jnp.where(jnp.abs(total) < jnp.abs(away), held, away).astype(BF16)


def decode_total(code, outer_rows, count):
    code = code.astype(F32)
    return jnp.where(jnp.abs(code) > CODE_CUT, code * (1.0 / CODE_SCALE), count * outer_rows - code)


def decode_away(code, outer_rows, count):
    code = code.astype(F32)
    return jnp.where(jnp.abs(code) > CODE_CUT, count * outer_rows - code * (1.0 / CODE_SCALE), code)


def swap(value, axis, flip):
    count = lax.axis_size(axis)
    return lax.ppermute(value, axis, [(i, i ^ flip) for i in range(count)])


VMEM = pl.BlockSpec(memory_space=pltpu.VMEM)
HBM = pl.BlockSpec(memory_space=pl.ANY)
SMEM = pl.BlockSpec(memory_space=pltpu.SMEM)


def in_hbm(value):
    return pltpu.with_memory_space_constraint(value, pltpu.HBM)


def near(shape, dtype):
    return pltpu.VMEM(tuple(shape), dtype)


def far(shape, dtype):
    return pltpu.HBM(tuple(shape), dtype)


def run(kernel, outs, ins, copies, scratch=(), weight=0, mib=8, aliases=None, name="kernel"):
    specs = [spec for _, spec in ins]
    return pl.pallas_call(
        kernel,
        out_shape=tuple(outs),
        in_specs=specs,
        out_specs=tuple(VMEM if out.memory_space == pltpu.VMEM else HBM for out in outs),
        scratch_shapes=list(scratch) + ([pltpu.SemaphoreType.DMA((copies,))] if copies else []),
        input_output_aliases=aliases or {},
        compiler_params=pltpu.CompilerParams(vmem_limit_bytes=mib * MIB),
        cost_estimate=pl.CostEstimate(flops=0, bytes_accessed=weight * MIB, transcendentals=0),
        name=name,
    )(*[value for value, _ in ins])


def rows_at(block, size):
    return pl.ds(pl.multiple_of(block * size, size), size)


CORE, SHARD, CHIP_BIT_0, CHIP_BIT_1, KEEP_A, SEND_A, KEEP_B, SEND_B, CHIP = range(9)


def positions(quarters):
    shard, rep = lax.axis_index("fsdp"), lax.axis_index("rep")
    chip = shard >> 1
    bit_a, bit_b = rep & 1, (rep >> 1) & 1
    return jnp.stack(
        [shard & 1, shard, chip & 1, (chip >> 1) & 1, bit_a, 1 - bit_a, 2 + bit_b, 3 - bit_b, chip]
    ).astype(jnp.int32)


def open_kernel(scale, pos_ref, x_ref, rep_ref, keep_ref, send_ref, x_out, first_a, first_b, sems):
    quarter = first_a.shape[0]
    copy_x = pltpu.make_async_copy(x_ref, x_out, sems.at[0])
    copy_a = pltpu.make_async_copy(rep_ref.at[rows_at(pos_ref[SEND_A], quarter)], first_a, sems.at[1])
    copy_b = pltpu.make_async_copy(rep_ref.at[rows_at(pos_ref[SEND_B], quarter)], first_b, sems.at[2])
    copy_x.start()
    copy_a.start()
    copy_b.start()
    copy_x.wait()
    x = x_out[...]
    gram = lax.dot_general(x, x, (((1,), (1,)), ((), ())), preferred_element_type=F32) * scale
    tiles = x.shape[0] // LANES
    pairs = [(i, j) for i in range(tiles) for j in range(i, tiles)]
    each = len(pairs) // 2
    mine = pos_ref[CORE]
    for place, (i, j) in enumerate(pairs):
        part = gram[i * LANES : (i + 1) * LANES, j * LANES : (j + 1) * LANES].astype(BF16)
        side, spot = place // each, place % each
        rows = pl.ds(spot * LANES, LANES)

        @pl.when(mine == side)
        def _():
            keep_ref[rows, :] = part

        @pl.when(mine != side)
        def _():
            send_ref[rows, :] = part

    copy_a.wait()
    copy_b.wait()


def opening(pos, x, rep_rows, scale):
    tokens, depth = x.shape
    tiles = tokens // LANES
    each = tiles * (tiles + 1) // 4 * LANES
    quarter = (rep_rows.shape[0] // 4, rep_rows.shape[1])
    return run(
        functools.partial(open_kernel, scale),
        [near((each, LANES), BF16)] * 2 + [near(x.shape, BF16)] + [near(quarter, BF16)] * 2,
        [(pos, SMEM), (in_hbm(x), HBM), (in_hbm(rep_rows), HBM)],
        3,
        weight=WEIGHT["opening"],
        name="opening",
    )


def reversed_bits(value, bits):
    return sum(((value >> bit) & 1) << (bits - 1 - bit) for bit in range(bits))


def project_kernel(
    scale, pos_ref, x_ref, t_hbm, w_ref, rep_ref, outer_ref, keep_ref, *refs
):
    sends, (w_out, rep_a, rep_b, outer_a, outer_b, acc_ref, t_ref, sems) = refs[:-8], refs[-8:]
    steps = keep_ref.shape[0]
    bits = steps.bit_length() - 1
    quarter = rep_a.shape[0]
    copy_t = pltpu.make_async_copy(t_hbm, t_ref, sems.at[steps + 4])
    copy_t.start()
    copies = []
    for j in range(steps):
        place = reversed_bits(j, bits)
        copy = pltpu.make_async_copy(w_ref.at[:, pl.ds(place * SPAN, SPAN)], w_out.at[place], sems.at[j])
        copy.start()
        copies.append(copy)
    others = []
    for k, (source, entry, target) in enumerate(
        [(rep_ref, KEEP_A, rep_a), (rep_ref, KEEP_B, rep_b), (outer_ref, KEEP_A, outer_a), (outer_ref, KEEP_B, outer_b)]
    ):
        copy = pltpu.make_async_copy(source.at[rows_at(pos_ref[entry], quarter)], target, sems.at[steps + k])
        copy.start()
        others.append(copy)
    own = t_ref.shape[0]
    rows = rows_at(pos_ref[SHARD], own)
    copy_t.wait()
    for j in range(steps):
        place = reversed_bits(j, bits)
        copies[j].wait()
        acc_ref[...] = scale * jnp.dot(x_ref[...], w_out[place].astype(BF16), preferred_element_type=F32)
        acc_ref[rows, :] = acc_ref[rows, :] - t_ref[:, place * SPAN : (place + 1) * SPAN].astype(F32)
        for side in range(2):

            @pl.when(pos_ref[CORE] == side)
            def _():
                keep_ref[j] = acc_ref[:, side * LANES : (side + 1) * LANES].astype(BF16)

            @pl.when(pos_ref[CORE] != side)
            def _():
                sends[j][...] = acc_ref[:, side * LANES : (side + 1) * LANES].astype(BF16)

    for copy in others:
        copy.wait()


def project(pos, x, t, w, rep_rows, outer, scale):
    tokens, depth = x.shape
    steps = w.shape[1] // SPAN
    quarter = (rep_rows.shape[0] // 4, rep_rows.shape[1])
    return run(
        functools.partial(project_kernel, scale),
        [near((steps, tokens, LANES), BF16)]
        + [near((tokens, LANES), BF16)] * steps
        + [near((steps, depth, SPAN), F32)]
        + [near(quarter, BF16)] * 2
        + [near(quarter, F32)] * 2,
        [(pos, SMEM), (x, VMEM), (in_hbm(t), HBM), (in_hbm(w), HBM), (in_hbm(rep_rows), HBM), (in_hbm(outer), HBM)],
        steps + 5,
        scratch=[pltpu.VMEM((tokens, SPAN), F32), pltpu.VMEM(t.shape, BF16)],
        weight=WEIGHT["project"],
        name="project",
    )


def fold_kernel(entry, pos_ref, own_ref, *refs):
    gots, leave_ref, stay_ref = refs[:-2], refs[-2], refs[-1]
    size = stay_ref.shape[0]
    each = own_ref.shape[0] // len(gots)

    def total(place):
        got = gots[place // each]
        got = got[...] if each == 1 and len(got.shape) == 2 else got[place % each]
        return own_ref[place].astype(F32) + got.astype(F32)

    for side in range(2):

        @pl.when(pos_ref[entry] == side)
        def _():
            for k in range(size):
                leave_ref[k] = total((1 - side) * size + k).astype(BF16)
                stay_ref[k] = total(side * size + k)


def fold(pos, own, gots, entry, weight):
    size, tokens, width = own.shape
    shape = (size // 2, tokens, width)
    return run(
        functools.partial(fold_kernel, entry),
        [near(shape, BF16), near(shape, F32)],
        [(pos, SMEM), (own, VMEM)] + [(got, VMEM) for got in gots],
        0,
        weight=weight,
        name="fold",
    )


def add_kernel(own_ref, got_ref, out_ref):
    out_ref[...] = (own_ref[...].astype(F32) + got_ref[...].astype(F32)).astype(BF16)


def add(own, got, weight):
    return run(
        add_kernel,
        [near(own.shape, BF16)],
        [(own, VMEM), (got, VMEM)],
        0,
        weight=weight,
        name="add",
    )[0]


def whole_gram_kernel(pos_ref, x_ref, mine_ref, other_ref, out_ref, turned_ref):
    tiles = out_ref.shape[0] // LANES
    pairs = [(i, j) for i in range(tiles) for j in range(i, tiles)]
    each = len(pairs) // 2
    mine_first = pos_ref[CORE] == 0
    for place, (i, j) in enumerate(pairs):
        rows = pl.ds((place % each) * LANES, LANES)
        here = mine_first if place < each else jnp.logical_not(mine_first)
        part = jnp.where(here, mine_ref[rows, :], other_ref[rows, :])
        out_ref[i * LANES : (i + 1) * LANES, j * LANES : (j + 1) * LANES] = part
        if i != j:
            out_ref[j * LANES : (j + 1) * LANES, i * LANES : (i + 1) * LANES] = part.T
    turned_ref[...] = x_ref[...].T


def whole_gram(pos, x, mine, other):
    tokens, depth = x.shape
    return run(
        whole_gram_kernel,
        [near((tokens, tokens), BF16), near((depth, tokens), BF16)],
        [(pos, SMEM), (x, VMEM), (mine, VMEM), (other, VMEM)],
        0,
        weight=WEIGHT["whole_gram"],
        name="whole_gram",
    )


def residual_kernel(own_ref, got_ref, gram_ref, out_ref):
    error = own_ref[0] + got_ref[0].astype(F32)
    moved = jnp.dot(gram_ref[...], error.astype(BF16), preferred_element_type=F32)
    out_ref[...] = (2.0 * error - moved).astype(BF16)


def residual(own, got, gram):
    _, tokens, width = own.shape
    return run(
        residual_kernel,
        [near((tokens, width), BF16)],
        [(own, VMEM), (got, VMEM), (gram, VMEM)],
        0,
        weight=WEIGHT["residual"],
        name="residual",
    )[0]


def step_kernel(rate, places, pos_ref, turned_ref, w_ref, *refs):
    count = len(places)
    pieces = refs[: 2 * count]
    out_ref, pair_ref, buffer_ref, sems = refs[-4:]
    first = pos_ref[CORE] == 0
    copies = []
    for k, flip in enumerate(places):
        mine, other = pieces[2 * k][...], pieces[2 * k + 1][...]
        pair_ref[:, :LANES] = jnp.where(first, mine, other)
        pair_ref[:, LANES:] = jnp.where(first, other, mine)
        place = jnp.bitwise_xor(pos_ref[CHIP], flip)
        grad = jnp.dot(turned_ref[...], pair_ref[...], preferred_element_type=F32)
        buffer_ref[k] = w_ref[place] - rate * grad
        copy = pltpu.make_async_copy(
            buffer_ref.at[k], out_ref.at[:, pl.ds(pl.multiple_of(place * SPAN, SPAN), SPAN)], sems.at[k]
        )
        copy.start()
        copies.append(copy)
    for copy in copies:
        copy.wait()


def weight_step(pos, turned, w, pairs, places, rate, before):
    depth, tokens = turned.shape
    count = len(pairs)
    flat = [piece for pair in pairs for piece in pair]
    ins = [(pos, SMEM), (turned, VMEM), (w, VMEM)] + [(piece, VMEM) for piece in flat]
    aliases = {}
    if before is not None:
        aliases = {len(ins): 0}
        ins.append((before, HBM))
    return run(
        functools.partial(step_kernel, rate, tuple(places)),
        [far((depth, w.shape[0] * SPAN), F32)],
        ins,
        count,
        scratch=[pltpu.VMEM((tokens, SPAN), BF16), pltpu.VMEM((count, depth, SPAN), F32)],
        aliases=aliases,
        weight=WEIGHT["weight_step"],
        name="weight_step",
    )[0]


def first_code_kernel(rep_ref, got_ref, outer_ref, code_ref):
    total = rep_ref[...].astype(F32) + got_ref[...].astype(F32)
    code_ref[...] = encode(total, outer_ref[...], 2.0)


def second_code_kernel(own_ref, got_ref, outer_ref, code_ref):
    outer = outer_ref[...]
    total = decode_total(own_ref[...], outer, 2.0) + decode_total(got_ref[...], outer, 2.0)
    code_ref[...] = encode(total, outer, 4.0)


def code(kernel, own, got, outer_rows, weight):
    return run(
        kernel,
        [near(own.shape, BF16)],
        [(own, VMEM), (got, VMEM), (outer_rows, VMEM)],
        0,
        weight=weight,
        name="code",
    )[0]


PART = 128


def update_rows(entries, pos_ref, codes, outers, moments, reps, outs, buffers, sems, ready):
    size = codes[0].shape[0]
    copies = []
    part = min(PART, size)
    for half in range(2):
        for cut in range(size // part):
            spot = half * (size // part) + cut
            rows = pl.ds(cut * part, part)
            here = pl.ds(spot * part, part)
            if cut == 0:
                ready(half)
            outer = outers[half][rows, :]
            delta = decode_away(codes[half][rows, :], outer, 4.0) * 0.25
            moment = momentum_coef * moments[half][rows, :] + delta
            new_outer = outer - outer_rate * (delta + momentum_coef * moment)
            mixed = merge_keep * reps[half][rows, :].astype(F32) + (1.0 - merge_keep) * new_outer
            for k, value in enumerate((new_outer, moment, mixed.astype(BF16))):
                buffers[k][here, :] = value
                target = rows_at(pos_ref[entries[half]] * (size // part) + cut, part)
                copy = pltpu.make_async_copy(buffers[k].at[here], outs[k].at[target], sems.at[3 * spot + k])
                copy.start()
                copies.append(copy)
    for copy in copies:
        copy.wait()


def near_update_kernel(
    pos_ref, code_a, code_b, outer_a, outer_b, rep_a, rep_b, outer_ref, moment_ref, rep_ref,
    new_outer, new_moment, merged, far_outer_a, far_outer_b, far_moment_a, far_moment_b, far_rep_a, far_rep_b,
    moment_a, moment_b, buffer_outer, buffer_moment, buffer_merged, sems,
):
    size = code_a.shape[0]
    base = 6 * max(size // PART, 1)
    fetches = [
        (moment_ref, KEEP_A, moment_a),
        (moment_ref, KEEP_B, moment_b),
        (outer_ref, SEND_A, far_outer_a),
        (outer_ref, SEND_B, far_outer_b),
        (moment_ref, SEND_A, far_moment_a),
        (moment_ref, SEND_B, far_moment_b),
        (rep_ref, SEND_A, far_rep_a),
        (rep_ref, SEND_B, far_rep_b),
    ]
    copies = []
    for k, (source, entry, target) in enumerate(fetches):
        copy = pltpu.make_async_copy(source.at[rows_at(pos_ref[entry], size)], target, sems.at[base + k])
        copy.start()
        copies.append(copy)
    update_rows(
        (KEEP_A, KEEP_B), pos_ref, (code_a, code_b), (outer_a, outer_b), (moment_a, moment_b), (rep_a, rep_b),
        (new_outer, new_moment, merged), (buffer_outer, buffer_moment, buffer_merged), sems,
        lambda half: copies[half].wait(),
    )
    for copy in copies[2:]:
        copy.wait()


def far_update_kernel(
    pos_ref, code_a, code_b, outer_a, outer_b, moment_a, moment_b, rep_a, rep_b, held_a, held_b, held_c,
    new_outer, new_moment, merged, buffer_outer, buffer_moment, buffer_merged, sems,
):
    del held_a, held_b, held_c
    update_rows(
        (SEND_A, SEND_B), pos_ref, (code_a, code_b), (outer_a, outer_b), (moment_a, moment_b), (rep_a, rep_b),
        (new_outer, new_moment, merged), (buffer_outer, buffer_moment, buffer_merged), sems,
        lambda half: None,
    )


def update_scratch(size, width):
    return [pltpu.VMEM((2 * size, width), dtype) for dtype in (F32, F32, BF16)]


def near_update(pos, codes, outers, reps, outer, moment, rep_rows):
    size, width = codes[0].shape
    full = outer.shape
    return run(
        near_update_kernel,
        [far(full, F32), far(full, F32), far(full, BF16)]
        + [near((size, width), F32)] * 4
        + [near((size, width), BF16)] * 2,
        [(pos, SMEM)]
        + [(value, VMEM) for value in (*codes, *outers, *reps)]
        + [(in_hbm(value), HBM) for value in (outer, moment, rep_rows)],
        6 * max(size // PART, 1) + 8,
        scratch=[pltpu.VMEM((size, width), F32)] * 2 + update_scratch(size, width),
        mib=16,
        weight=WEIGHT["near_update"],
        name="near_update",
    )


def far_update(pos, codes, fetched, before):
    size, width = codes[0].shape
    outs = [far(value.shape, value.dtype) for value in before]
    ins = [(pos, SMEM)] + [(value, VMEM) for value in (*codes, *fetched)]
    return run(
        far_update_kernel,
        outs,
        ins + [(value, HBM) for value in before],
        6 * max(size // PART, 1),
        scratch=update_scratch(size, width),
        mib=16,
        aliases={len(ins) + k: k for k in range(3)},
        weight=WEIGHT["far_update"],
        name="far_update",
    )


def after(value, *others):
    return lax.optimization_barrier((value, *others))[0]


def both(x, t, w, outer, moment, rep_rows):
    shards = lax.axis_size("fsdp")
    chips = shards // 2
    scale = (x.shape[1] * shards) ** -0.5
    pos = positions(4)

    gram_keep, gram_send, x, first_a, first_b = opening(pos, x, rep_rows, inner_rate * scale * scale)
    gram_got = swap(gram_send, "fsdp", 1)
    got_a, got_b = swap(first_a, "rep", 1), swap(first_b, "rep", 2)
    gram_1 = add(gram_keep, gram_got, WEIGHT["add_1"])
    gram_got = swap(gram_1, "fsdp", 2)

    keep, *refs = project(after(pos, gram_1), x, t, w, rep_rows, outer, scale)
    sends, (w, rep_a, rep_b, outer_a, outer_b) = refs[:-5], refs[-5:]
    gram_2 = add(after(gram_1, keep), gram_got, WEIGHT["add_2"])
    gram_got = swap(gram_2, "fsdp", 4)
    got = [swap(send, "fsdp", 1) for send in sends]
    leave_1, stay = fold(pos, after(keep, gram_2), got, CHIP_BIT_0, WEIGHT["fold_1"])
    got = swap(leave_1, "fsdp", 2)

    code_a = code(first_code_kernel, after(rep_a, leave_1), got_a, outer_a, WEIGHT["code_1"])
    got_a = swap(code_a, "rep", 2)
    code_b = code(first_code_kernel, after(rep_b, code_a), got_b, outer_b, WEIGHT["code_2"])
    got_b = swap(code_b, "rep", 1)

    leave_2, stay = fold(pos, after(stay, code_b), [got], CHIP_BIT_1, WEIGHT["fold_2"])
    got = swap(leave_2, "fsdp", 4)
    gram = add(after(gram_2, leave_2), gram_got, WEIGHT["add_3"])
    pieces = [gram[: gram.shape[0] // 2], gram[gram.shape[0] // 2 :]]
    gram_got = [swap(piece, "fsdp", 1) for piece in pieces]

    code_a = code(second_code_kernel, after(code_a, gram), got_a, outer_a, WEIGHT["code_3"])
    got_a = swap(code_a, "rep", 1)
    code_b = code(second_code_kernel, after(code_b, code_a), got_b, outer_b, WEIGHT["code_4"])
    got_b = swap(code_b, "rep", 2)

    gram, turned = whole_gram(after(pos, code_b), x, gram, jnp.concatenate(gram_got, 0))
    moved = residual(stay, got, gram)
    updated = near_update(
        after(pos, moved), (code_a, code_b), (outer_a, outer_b), (rep_a, rep_b), outer, moment, rep_rows
    )
    mine = [moved] + [swap(moved, "fsdp", 2 * k) for k in range(1, chips)]
    pairs = [(piece, swap(after(piece, updated[0]), "fsdp", 1)) for piece in mine]
    result = weight_step(pos, turned, w, pairs, range(chips), inner_rate * scale, None)
    outers = far_update(after(pos, result), (got_a, got_b), updated[3:], updated[:3])
    return result, *outers


def plain_outer(outer, moment, rep_rows):
    replica_rows = rep_rows.astype(F32)
    delta = lax.psum(outer - replica_rows, "rep") / lax.axis_size("rep")
    new_moment = momentum_coef * moment + delta
    new_outer = outer - outer_rate * (delta + momentum_coef * new_moment)
    mixed = merge_keep * replica_rows + (1.0 - merge_keep) * new_outer
    return new_outer, new_moment, mixed.astype(BF16)


def plain_inner(x, t, w):
    scale = (x.shape[1] * lax.axis_size("fsdp")) ** -0.5
    for _ in range(INNER):
        part = jnp.dot(x, w.astype(BF16), preferred_element_type=F32).astype(BF16)
        predicted = lax.psum_scatter(part, "fsdp", scatter_dimension=0, tiled=True).astype(F32) * scale
        errors = lax.all_gather((predicted - t.astype(F32)).astype(BF16), "fsdp", axis=0, tiled=True)
        gradient = lax.dot_general(x, errors, (((0,), (0,)), ((), ())), preferred_element_type=F32)
        w = w - inner_rate * scale * gradient
    return w


def local(tokens, targets, inner_weights, outer_weights, outer_momentum, replica_weights):
    x, t, w, rep_rows = tokens[0], targets[0], inner_weights[0], replica_weights[0]
    tiles = x.shape[0] // LANES
    if (
        lax.axis_size("fsdp") == 8
        and lax.axis_size("rep") == 4
        and w.shape[1] == 8 * LANES
        and x.shape[0] % LANES == 0
        and tiles * (tiles + 1) % 4 == 0
        and rep_rows.shape[0] % (4 * PART) == 0
    ):
        new_inner, new_outer, new_moment, merged = both(x, t, w, outer_weights, outer_momentum, rep_rows)
    else:
        new_outer, new_moment, merged = plain_outer(outer_weights, outer_momentum, rep_rows)
        new_inner = plain_inner(x, t, w)
    return new_inner[None], new_outer, new_moment, merged[None]


def solution(mesh):
    placed = (
        P("rep", None, "fsdp"),
        P("rep", "fsdp", None),
        P("rep", "fsdp", None),
        P("fsdp", None),
        P("fsdp", None),
        P("rep", "fsdp", None),
    )
    return jax.shard_map(
        local,
        mesh=mesh,
        in_specs=placed,
        out_specs=(
            P("rep", "fsdp", None),
            P("fsdp", None),
            P("fsdp", None),
            P("rep", "fsdp", None),
        ),
        check_vma=False,
    )
```

time: 218 us -> 64.6 us (0.30)
  waiting for transfers between devices: 152 us -> 18.1 us
  Pallas kernels: 0 us -> 25.1 us
  starting transfers between devices: 0.21 us -> 20.3 us
  other arithmetic: 19.7 us -> 0.01 us
  matrix products: 16.3 us -> 0 us
  between operations: 15.3 us -> 0.99 us
  local copies, waits for them, and re-layouts: 13.9 us -> 0.1 us
    psum x1 -> x0, waiting for transfers between devices: 74.7 us -> none  [outer_sync(): pseudo_sum = lax.psum(replica_term, 'rep')]
    reduce_scatter x2 -> x0, waiting for transfers between devices: 61.9 us -> none  [inner_run(): lax.psum_scatter(jnp.dot(token_cols, weights_half, preferred_element_type...]
    pallas_call x0 -> x16, Pallas kernels: none -> 25.1 us  [run(): pl.pallas_call(kernel, out_shape=tuple(outs), in_specs=specs, out_specs=t...]
    ppermute x0 -> x24, starting transfers between devices: none -> 20.3 us  [swap(): return lax.ppermute(value, axis, [(i, i ^ flip) for i in range(count)])]
    ppermute x0 -> x24, waiting for transfers between devices: none -> 18.1 us  [swap(): return lax.ppermute(value, axis, [(i, i ^ flip) for i in range(count)])]
    dot_general x4 -> x0, matrix products: 16.3 us -> none  [the longest x2 9.58 us: inner_run(): lax.dot_general(token_cols, lax.all_gather(errors, 'fsdp', axis=0, tiled=...]
    all_gather x2 -> x0, waiting for transfers between devices: 15.5 us -> none  [inner_run(): lax.all_gather(errors, 'fsdp', axis=0, tiled=True)]
    unnamed x10 -> x0, local copies, waits for them, and re-layouts: 13.9 us -> none
  transfers between devices with their start and end apart: 5 -> 24, of which waited for: 4 -> 11; matrix products, arithmetic and copies ran while one was open for 11% -> 0% of each run, Pallas kernels for 0% -> 30%
where the time goes in v2:
time: 64.6 us; the launch traced here: 64.5 us
  Pallas kernels  25.1 us (39%)
  starting transfers between devices  20.3 us (31%)
  waiting for transfers between devices  18.1 us (28%)
  between operations  0.99 us (2%)
    pallas_call x16, Pallas kernels, run(): pl.pallas_call(kernel, out_shape=tuple(outs), in_specs=specs, out_specs=t...  25.1 us
    ppermute x24, starting transfers between devices, swap(): return lax.ppermute(value, axis, [(i, i ^ flip) for i in range(count)])  20.3 us
    ppermute x24, waiting for transfers between devices, swap(): return lax.ppermute(value, axis, [(i, i ^ flip) for i in range(count)])  18.1 us
  transfers between devices with their start and end apart: 24, of which 11 were waited for; matrix products, arithmetic and copies ran while one was open for 0% of the time, Pallas kernels for 30%

profile of v2, /device:TPU:0, one launch (start us, length us, event | category | flops | bytes accessed | tf_op | source)
XLA Modules:
  0.0 64.5 jit_solution(14331773486327700021)
XLA Ops:
  0.7 2.6 %opening.1 = (bf16[640,128]{1,0:T(8,128)(2,1)S(1)}, bf16[640,128]{1,0:T(8,128)(2,1)S(1)}, bf16[512,1024]{1,0:T(8,128)(2,1)S(1)}, bf16[256,1024]{1,0:T(8,128)(2,1)S(1)}, bf16[256,1024]{1,0:T(8,128)(2,1)S(1)}) custom-call(s32[9]{0:T(128)S(1)} %stack.39.pos_ref, bf16[512,1024]{1,0:T(8,128)(2,1)} %bitcast.21, bf16[1024,1024]{1,0:T(8,128)(2,1)} %bitcast.15), custom_call_target="tpu_custom_call" | custom-call | bytes 4194304 | tf_op jit(solution)/shard_map/opening/pallas_call | solution.py:88
  3.4 3.0 %collective-permute-start.6 = (bf16[256,1024]{1,0:T(8,128)(2,1)S(1)}, bf16[256,1024]{1,0:T(8,128)(2,1)S(1)}, u32[]{:S(2)}, u32[]{:S(2)}) collective-permute-start(bf16[256,1024]{1,0:T(8,128)(2,1)S(1)} %get-tuple-element.68), channel_id=1, source_target_pairs={{0,8},{8,0},{16,24},{24,16},{1,9},{9,1},{17,25},{25,17},{2,10},{10... | collective-permute-start | bytes 1572872 | tf_op jit(solution)/shard_map/ppermute | solution.py:66
  6.4 1.5 %collective-permute-start.7 = (bf16[256,1024]{1,0:T(8,128)(2,1)S(1)}, bf16[256,1024]{1,0:T(8,128)(2,1)S(1)}, u32[]{:S(2)}, u32[]{:S(2)}) collective-permute-start(bf16[256,1024]{1,0:T(8,128)(2,1)S(1)} %get-tuple-element.71), channel_id=1, source_target_pairs={{0,16},{8,24},{16,0},{24,8},{1,17},{9,25},{17,1},{25,9},{2,18},{10... | collective-permute-start | bytes 1572872 | tf_op jit(solution)/shard_map/ppermute | solution.py:66
  7.9 1.4 %collective-permute-done.got_ref = bf16[640,128]{1,0:T(8,128)(2,1)S(1)} collective-permute-done((bf16[640,128]{1,0:T(8,128)(2,1)S(1)}, bf16[640,128]{1,0:T(8,128)(2,1)S(1)}, u32[]{:S(2)}, u32[]{:S(2)}) %collective-permute-start) | collective-permute-done | bytes 163872 | tf_op jit(solution)/shard_map/ppermute | solution.py:66
  9.3 1.6 %collective-permute-start.1 = (bf16[640,128]{1,0:T(8,128)(2,1)S(1)}, bf16[640,128]{1,0:T(8,128)(2,1)S(1)}, u32[]{:S(2)}, u32[]{:S(2)}) collective-permute-start(bf16[640,128]{1,0:T(8,128)(2,1)S(1)} %add.3.own_ref), channel_id=1, source_target_pairs={{0,2},{1,3},{2,0},{3,1},{4,6},{5,7},{6,4},{7,5},{8,10},{9,11},{10,... | collective-permute-start | bytes 491528 | tf_op jit(solution)/shard_map/ppermute | solution.py:66
  11.0 4.9 %project.1 = (bf16[4,512,128]{2,1,0:T(8,128)(2,1)S(1)}, bf16[512,128]{1,0:T(8,128)(2,1)S(1)}, bf16[512,128]{1,0:T(8,128)(2,1)S(1)}, bf16[512,128]{1,0:T(8,128)(2...) custom-call(s32[9]{0:T(128)S(1)} %stack.39.pos_ref, ...), custom_call_target="tpu_custom_call" | custom-call | bytes 1048576 | tf_op jit(solution)/shard_map/project/pallas_call | solution.py:88
  16.5 0.8 %collective-permute-done.2.refs_0_ = bf16[512,128]{1,0:T(8,128)(2,1)S(1)} collective-permute-done((bf16[512,128]{1,0:T(8,128)(2,1)S(1)}, bf16[512,128]{1,0:T(8,128)(2,1)S(1)}, u32[]{:S(2)}, u32[]{:S(2)}) %collective-permute-start.2) | collective-permute-done | bytes 131104 | tf_op jit(solution)/shard_map/ppermute | solution.py:66
  17.9 0.8 %collective-permute-done.4.refs_2_ = bf16[512,128]{1,0:T(8,128)(2,1)S(1)} collective-permute-done((bf16[512,128]{1,0:T(8,128)(2,1)S(1)}, bf16[512,128]{1,0:T(8,128)(2,1)S(1)}, u32[]{:S(2)}, u32[]{:S(2)}) %collective-permute-start.4) | collective-permute-done | bytes 131104 | tf_op jit(solution)/shard_map/ppermute | solution.py:66
  21.5 1.1 %collective-permute-start.11 = (bf16[256,1024]{1,0:T(8,128)(2,1)S(1)}, bf16[256,1024]{1,0:T(8,128)(2,1)S(1)}, u32[]{:S(2)}, u32[]{:S(2)}) collective-permute-start(bf16[256,1024]{1,0:T(8,128)(2,1)S(1)} %code.5.own_ref), channel_id=1, source_target_pairs={{0,8},{8,0},{16,24},{24,16},{1,9},{9,1},{17,25},{25,17},{2,10},{10... | collective-permute-start | bytes 1572872 | tf_op jit(solution)/shard_map/ppermute | solution.py:66
  22.5 2.6 %collective-permute-start.9 = (bf16[640,128]{1,0:T(8,128)(2,1)S(1)}, bf16[640,128]{1,0:T(8,128)(2,1)S(1)}, u32[]{:S(2)}, u32[]{:S(2)}) collective-permute-start(bf16[640,128]{1,0:T(8,128)(2,1)S(1)} %add.4.own_ref), channel_id=1, source_target_pairs={{0,4},{1,5},{2,6},{3,7},{4,0},{5,1},{6,2},{7,3},{8,12},{9,13},{10,... | collective-permute-start | bytes 491528 | tf_op jit(solution)/shard_map/ppermute | solution.py:66
  25.1 6.5 %collective-permute-done.8.refs_0_ = bf16[2,512,128]{2,1,0:T(8,128)(2,1)S(1)} collective-permute-done((bf16[2,512,128]{2,1,0:T(8,128)(2,1)S(1)}, bf16[2,512,128]{2,1,0:T(8,128)(2,1)S(1)}, u32[]{:S(2)}, u32[]{:S(2)}) %collective-permute-start.8) | collective-permute-done | bytes 262176 | tf_op jit(solution)/shard_map/ppermute | solution.py:66
  31.7 0.8 %fold.3 = (bf16[1,512,128]{2,1,0:T(8,128)(2,1)S(1)}, f32[1,512,128]{2,1,0:T(8,128)S(1)}) custom-call(s32[9]{0:T(128)S(1)} %stack.39.pos_ref, f32[2,512,128]{2,1,0:T(8,128)S(1)} %get-tuple-element.74.own_ref, bf16[2,512,128]{2,1,0:T(8,128)(2,1)S(1)} %collective-permute-done.8.refs_0_), custom_call_target="tpu_custom_call" | custom-call | bytes 419430400 | tf_op jit(solution)/shard_map/fold/pallas_call | solution.py:88
  34.4 0.8 %code.6.code_a = bf16[256,1024]{1,0:T(8,128)(2,1)S(1)} custom-call(bf16[256,1024]{1,0:T(8,128)(2,1)S(1)} %code.4.own_ref, bf16[256,1024]{1,0:T(8,128)(2,1)S(1)} %collective-permute-done.10.got_ref, f32[256,1024]{1,0:T(8,128)S(1)} %get-tuple-element.69.outer_ref.outer_a), custom_call_target="tpu_custom_call" | custom-call | tf_op jit(solution)/shard_map/code/pallas_call | solution.py:88
  35.2 0.8 %code.7.code_b = bf16[256,1024]{1,0:T(8,128)(2,1)S(1)} custom-call(bf16[256,1024]{1,0:T(8,128)(2,1)S(1)} %code.5.own_ref, bf16[256,1024]{1,0:T(8,128)(2,1)S(1)} %collective-permute-done.11.got_ref, f32[256,1024]{1,0:T(8,128)S(1)} %get-tuple-element.72.outer_ref.outer_b), custom_call_target="tpu_custom_call" | custom-call | tf_op jit(solution)/shard_map/code/pallas_call | solution.py:88
  36.0 1.5 %collective-permute-start.23 = (bf16[256,1024]{1,0:T(8,128)(2,1)S(1)}, bf16[256,1024]{1,0:T(8,128)(2,1)S(1)}, u32[]{:S(2)}, u32[]{:S(2)}) collective-permute-start(bf16[256,1024]{1,0:T(8,128)(2,1)S(1)} %code.7.code_b), channel_id=1, source_target_pairs={{0,16},{8,24},{16,0},{24,8},{1,17},{9,25},{17,1},{25,9},{2,18},{10... | collective-permute-start | bytes 1572872 | tf_op jit(solution)/shard_map/ppermute | solution.py:66
  38.1 0.9 %whole_gram.1 = (bf16[512,512]{1,0:T(8,128)(2,1)S(1)}, bf16[1024,512]{1,0:T(8,128)(2,1)S(1)}) custom-call(s32[9]{0:T(128)S(1)} %stack.39.pos_ref, bf16[512,1024]{1,0:T(8,128)(2,1)S(1)} %get-tuple-element.56.x_ref, bf16[640,128]{1,0:T(8,128)(2,1)S(1)} %add.5.mine_ref, bf16[640,128]{1,0:T(8,128)(2,1)S(1)} %pad_maximum_fusion.other_ref), custom_call_target="tpu_custom_call" | custom-call | tf_op jit(solution)/shard_map/whole_gram/pallas_call | solution.py:88
  39.0 3.2 %collective-permute-done.14.got_ref = bf16[1,512,128]{2,1,0:T(8,128)(2,1)S(1)} collective-permute-done((bf16[1,512,128]{2,1,0:T(8,128)(2,1)S(1)}, bf16[1,512,128]{2,1,0:T(8,128)(2,1)S(1)}, u32[]{:S(2)}, u32[]{:S(2)}) %collective-permute-start.14) | collective-permute-done | bytes 131104 | tf_op jit(solution)/shard_map/ppermute | solution.py:66
  42.6 1.6 %collective-permute-start.20 = (bf16[512,128]{1,0:T(8,128)(2,1)S(1)}, bf16[512,128]{1,0:T(8,128)(2,1)S(1)}, u32[]{:S(2)}, u32[]{:S(2)}) collective-permute-start(bf16[512,128]{1,0:T(8,128)(2,1)S(1)} %residual.1.refs_0_), channel_id=1, source_target_pairs={{0,6},{1,7},{2,4},{3,5},{4,2},{5,3},{6,0},{7,1},{8,14},{9,15},{10,... | collective-permute-start | bytes 393224 | tf_op jit(solution)/shard_map/ppermute | solution.py:66
  44.3 2.7 %collective-permute-start.16 = (bf16[512,128]{1,0:T(8,128)(2,1)S(1)}, bf16[512,128]{1,0:T(8,128)(2,1)S(1)}, u32[]{:S(2)}, u32[]{:S(2)}) collective-permute-start(bf16[512,128]{1,0:T(8,128)(2,1)S(1)} %residual.1.refs_0_), channel_id=1, source_target_pairs={{0,2},{1,3},{2,0},{3,1},{4,6},{5,7},{6,4},{7,5},{8,10},{9,11},{10,... | collective-permute-start | bytes 393224 | tf_op jit(solution)/shard_map/ppermute | solution.py:66
  47.0 5.5 %near_update.1 = (f32[1024,1024]{1,0:T(8,128)}, f32[1024,1024]{1,0:T(8,128)}, bf16[1024,1024]{1,0:T(8,128)(2,1)}, f32[256,1024]{1,0:T(8,128)S(1)}, f32[256,1024]...) custom-call(s32[9]{0:T(128)S(1)} %stack.39.pos_ref, ...), custom_call_target="tpu_custom_call" | custom-call | bytes 41943040 | tf_op jit(solution)/shard_map/near_update/pallas_call | solution.py:88
  52.6 3.0 %collective-permute-done.18.refs_4_ = bf16[512,128]{1,0:T(8,128)(2,1)S(1)} collective-permute-done((bf16[512,128]{1,0:T(8,128)(2,1)S(1)}, bf16[512,128]{1,0:T(8,128)(2,1)S(1)}, u32[]{:S(2)}, u32[]{:S(2)}) %collective-permute-start.18) | collective-permute-done | bytes 131104 | tf_op jit(solution)/shard_map/ppermute | solution.py:66
  56.2 0.8 %collective-permute-done.17.refs_3_ = bf16[512,128]{1,0:T(8,128)(2,1)S(1)} collective-permute-done((bf16[512,128]{1,0:T(8,128)(2,1)S(1)}, bf16[512,128]{1,0:T(8,128)(2,1)S(1)}, u32[]{:S(2)}, u32[]{:S(2)}) %collective-permute-start.17) | collective-permute-done | bytes 131104 | tf_op jit(solution)/shard_map/ppermute | solution.py:66
  57.5 3.5 %weight_step.1 = f32[1024,1024]{1,0:T(8,128)} custom-call(s32[9]{0:T(128)S(1)} %stack.39.pos_ref, bf16[1024,512]{1,0:T(8,128)(2,1)S(1)} %get-tuple-element.80.turned_ref, f32[4,1024,256]{2,1,0:T(8,128)S(1)} %get-tuple-element.81.w_ref, bf16[512,128]{1,0:T(8,128)(2,1)S(1)} %residual.1.refs_0_, bf16[512,128]{1,0:T(8,128)(2,1)S(1)} %collective-permute-done.15.refs_1_, ...), custom_call_target="tpu_custom_call" | custom-call | bytes 10485760 | tf_op jit(solution)/shard_map/weight_step/pallas_call | solution.py:88
  61.1 3.2 %far_update.1 = (f32[1024,1024]{1,0:T(8,128)}, f32[1024,1024]{1,0:T(8,128)}, bf16[1024,1024]{1,0:T(8,128)(2,1)}) custom-call(s32[9]{0:T(128)S(1)} %stack.39.pos_ref, bf16[256,1024]{1,0:T(8,128)(2,1)S(1)} %collective-permute-done.22.code_a, ...), custom_call_target="tpu_custom_call", output_to_operand_aliasing={{0}: (9, {}), {1}: (10, {}), {2}: (11, {})} | custom-call | bytes 10485760 | tf_op jit(solution)/shard_map/far_update/pallas_call | solution.py:88
  (43 shorter events, 8.0 us)
Async XLA Ops:
  3.4 16.7 %collective-permute-start.6 = (bf16[256,1024]{1,0:T(8,128)(2,1)S(1)}, bf16[256,1024]{1,0:T(8,128)(2,1)S(1)}, u32[]{:S(2)}, u32[]{:S(2)}) collective-permute-start(bf16[256,1024]{1,0:T(8,128)(2,1)S(1)} %get-tuple-element.68), channel_id=1, source_target_pairs={{0,8},{8,0},{16,24},{24,16},{1,9},{9,1},{17,25},{25,17},{2,10},{10... | collective-permute-start | bytes 1572872 | tf_op jit(solution)/shard_map/ppermute | solution.py:66
  6.4 14.7 %collective-permute-start.7 = (bf16[256,1024]{1,0:T(8,128)(2,1)S(1)}, bf16[256,1024]{1,0:T(8,128)(2,1)S(1)}, u32[]{:S(2)}, u32[]{:S(2)}) collective-permute-start(bf16[256,1024]{1,0:T(8,128)(2,1)S(1)} %get-tuple-element.71), channel_id=1, source_target_pairs={{0,16},{8,24},{16,0},{24,8},{1,17},{9,25},{17,1},{25,9},{2,18},{10... | collective-permute-start | bytes 1572872 | tf_op jit(solution)/shard_map/ppermute | solution.py:66
  7.9 1.4 %collective-permute-start = (bf16[640,128]{1,0:T(8,128)(2,1)S(1)}, bf16[640,128]{1,0:T(8,128)(2,1)S(1)}, u32[]{:S(2)}, u32[]{:S(2)}) collective-permute-start(bf16[640,128]{1,0:T(8,128)(2,1)S(1)} %get-tuple-element.54), channel_id=1, source_target_pairs={{0,1},{1,0},{2,3},{3,2},{4,5},{5,4},{6,7},{7,6},{8,9},{9,8},{10,11... | collective-permute-start | bytes 491528 | tf_op jit(solution)/shard_map/ppermute | solution.py:66
  9.3 8.2 %collective-permute-start.1 = (bf16[640,128]{1,0:T(8,128)(2,1)S(1)}, bf16[640,128]{1,0:T(8,128)(2,1)S(1)}, u32[]{:S(2)}, u32[]{:S(2)}) collective-permute-start(bf16[640,128]{1,0:T(8,128)(2,1)S(1)} %add.3.own_ref), channel_id=1, source_target_pairs={{0,2},{1,3},{2,0},{3,1},{4,6},{5,7},{6,4},{7,5},{8,10},{9,11},{10,... | collective-permute-start | bytes 491528 | tf_op jit(solution)/shard_map/ppermute | solution.py:66
  15.9 1.4 %collective-permute-start.2 = (bf16[512,128]{1,0:T(8,128)(2,1)S(1)}, bf16[512,128]{1,0:T(8,128)(2,1)S(1)}, u32[]{:S(2)}, u32[]{:S(2)}) collective-permute-start(bf16[512,128]{1,0:T(8,128)(2,1)S(1)} %get-tuple-element.62), channel_id=1, source_target_pairs={{0,1},{1,0},{2,3},{3,2},{4,5},{5,4},{6,7},{7,6},{8,9},{9,8},{10,11... | collective-permute-start | bytes 393224 | tf_op jit(solution)/shard_map/ppermute | solution.py:66
  16.0 1.9 %collective-permute-start.3 = (bf16[512,128]{1,0:T(8,128)(2,1)S(1)}, bf16[512,128]{1,0:T(8,128)(2,1)S(1)}, u32[]{:S(2)}, u32[]{:S(2)}) collective-permute-start(bf16[512,128]{1,0:T(8,128)(2,1)S(1)} %get-tuple-element.63), channel_id=1, source_target_pairs={{0,1},{1,0},{2,3},{3,2},{4,5},{5,4},{6,7},{7,6},{8,9},{9,8},{10,11... | collective-permute-start | bytes 393224 | tf_op jit(solution)/shard_map/ppermute | solution.py:66
  17.3 1.3 %collective-permute-start.4 = (bf16[512,128]{1,0:T(8,128)(2,1)S(1)}, bf16[512,128]{1,0:T(8,128)(2,1)S(1)}, u32[]{:S(2)}, u32[]{:S(2)}) collective-permute-start(bf16[512,128]{1,0:T(8,128)(2,1)S(1)} %get-tuple-element.64), channel_id=1, source_target_pairs={{0,1},{1,0},{2,3},{3,2},{4,5},{5,4},{6,7},{7,6},{8,9},{9,8},{10,11... | collective-permute-start | bytes 393224 | tf_op jit(solution)/shard_map/ppermute | solution.py:66
  17.5 1.4 %collective-permute-start.5 = (bf16[512,128]{1,0:T(8,128)(2,1)S(1)}, bf16[512,128]{1,0:T(8,128)(2,1)S(1)}, u32[]{:S(2)}, u32[]{:S(2)}) collective-permute-start(bf16[512,128]{1,0:T(8,128)(2,1)S(1)} %get-tuple-element.65), channel_id=1, source_target_pairs={{0,1},{1,0},{2,3},{3,2},{4,5},{5,4},{6,7},{7,6},{8,9},{9,8},{10,11... | collective-permute-start | bytes 393224 | tf_op jit(solution)/shard_map/ppermute | solution.py:66
  19.5 12.1 %collective-permute-start.8 = (bf16[2,512,128]{2,1,0:T(8,128)(2,1)S(1)}, bf16[2,512,128]{2,1,0:T(8,128)(2,1)S(1)}, u32[]{:S(2)}, u32[]{:S(2)}) collective-permute-start(bf16[2,512,128]{2,1,0:T(8,128)(2,1)S(1)} %get-tuple-element.66), channel_id=1, source_target_pairs={{0,2},{1,3},{2,0},{3,1},{4,6},{5,7},{6,4},{7,5},{8,10},{9,11},{10,... | collective-permute-start | bytes 786440 | tf_op jit(solution)/shard_map/ppermute | solution.py:66
  20.5 13.9 %collective-permute-start.10 = (bf16[256,1024]{1,0:T(8,128)(2,1)S(1)}, bf16[256,1024]{1,0:T(8,128)(2,1)S(1)}, u32[]{:S(2)}, u32[]{:S(2)}) collective-permute-start(bf16[256,1024]{1,0:T(8,128)(2,1)S(1)} %code.4.own_ref), channel_id=1, source_target_pairs={{0,16},{8,24},{16,0},{24,8},{1,17},{9,25},{17,1},{25,9},{2,18},{10... | collective-permute-start | bytes 1572872 | tf_op jit(solution)/shard_map/ppermute | solution.py:66
  21.5 13.7 %collective-permute-start.11 = (bf16[256,1024]{1,0:T(8,128)(2,1)S(1)}, bf16[256,1024]{1,0:T(8,128)(2,1)S(1)}, u32[]{:S(2)}, u32[]{:S(2)}) collective-permute-start(bf16[256,1024]{1,0:T(8,128)(2,1)S(1)} %code.5.own_ref), channel_id=1, source_target_pairs={{0,8},{8,0},{16,24},{24,16},{1,9},{9,1},{17,25},{25,17},{2,10},{10... | collective-permute-start | bytes 1572872 | tf_op jit(solution)/shard_map/ppermute | solution.py:66
  22.5 9.9 %collective-permute-start.9 = (bf16[640,128]{1,0:T(8,128)(2,1)S(1)}, bf16[640,128]{1,0:T(8,128)(2,1)S(1)}, u32[]{:S(2)}, u32[]{:S(2)}) collective-permute-start(bf16[640,128]{1,0:T(8,128)(2,1)S(1)} %add.4.own_ref), channel_id=1, source_target_pairs={{0,4},{1,5},{2,6},{3,7},{4,0},{5,1},{6,2},{7,3},{8,12},{9,13},{10,... | collective-permute-start | bytes 491528 | tf_op jit(solution)/shard_map/ppermute | solution.py:66
  32.5 5.6 %collective-permute-start.12 = (bf16[320,128]{1,0:T(8,128)(2,1)S(1)}, bf16[320,128]{1,0:T(8,128)(2,1)S(1)}, u32[]{:S(2)}, u32[]{:S(2)}) collective-permute-start(bf16[320,128]{1,0:T(8,128)(2,1)S(1)} %get-tuple-element.102), channel_id=1, source_target_pairs={{0,1},{1,0},{2,3},{3,2},{4,5},{5,4},{6,7},{7,6},{8,9},{9,8},{10,11... | collective-permute-start | bytes 245768 | tf_op jit(solution)/shard_map/ppermute | solution.py:66
  32.6 5.5 %collective-permute-start.13 = (bf16[320,128]{1,0:T(8,128)(2,1)S(1)}, bf16[320,128]{1,0:T(8,128)(2,1)S(1)}, u32[]{:S(2)}, u32[]{:S(2)}) collective-permute-start(bf16[320,128]{1,0:T(8,128)(2,1)S(1)} %get-tuple-element.103), channel_id=1, source_target_pairs={{0,1},{1,0},{2,3},{3,2},{4,5},{5,4},{6,7},{7,6},{8,9},{9,8},{10,11... | collective-permute-start | bytes 245768 | tf_op jit(solution)/shard_map/ppermute | solution.py:66
  33.1 9.2 %collective-permute-start.14 = (bf16[1,512,128]{2,1,0:T(8,128)(2,1)S(1)}, bf16[1,512,128]{2,1,0:T(8,128)(2,1)S(1)}, u32[]{:S(2)}, u32[]{:S(2)}) collective-permute-start(bf16[1,512,128]{2,1,0:T(8,128)(2,1)S(1)} %get-tuple-element.75), channel_id=1, source_target_pairs={{0,4},{1,5},{2,6},{3,7},{4,0},{5,1},{6,2},{7,3},{8,12},{9,13},{10,... | collective-permute-start | bytes 393224 | tf_op jit(solution)/shard_map/ppermute | solution.py:66
  36.0 25.0 %collective-permute-start.23 = (bf16[256,1024]{1,0:T(8,128)(2,1)S(1)}, bf16[256,1024]{1,0:T(8,128)(2,1)S(1)}, u32[]{:S(2)}, u32[]{:S(2)}) collective-permute-start(bf16[256,1024]{1,0:T(8,128)(2,1)S(1)} %code.7.code_b), channel_id=1, source_target_pairs={{0,16},{8,24},{16,0},{24,8},{1,17},{9,25},{17,1},{25,9},{2,18},{10... | collective-permute-start | bytes 1572872 | tf_op jit(solution)/shard_map/ppermute | solution.py:66
  37.5 23.6 %collective-permute-start.22 = (bf16[256,1024]{1,0:T(8,128)(2,1)S(1)}, bf16[256,1024]{1,0:T(8,128)(2,1)S(1)}, u32[]{:S(2)}, u32[]{:S(2)}) collective-permute-start(bf16[256,1024]{1,0:T(8,128)(2,1)S(1)} %code.6.code_a), channel_id=1, source_target_pairs={{0,8},{8,0},{16,24},{24,16},{1,9},{9,1},{17,25},{25,17},{2,10},{10... | collective-permute-start | bytes 1572872 | tf_op jit(solution)/shard_map/ppermute | solution.py:66
  42.6 9.9 %collective-permute-start.20 = (bf16[512,128]{1,0:T(8,128)(2,1)S(1)}, bf16[512,128]{1,0:T(8,128)(2,1)S(1)}, u32[]{:S(2)}, u32[]{:S(2)}) collective-permute-start(bf16[512,128]{1,0:T(8,128)(2,1)S(1)} %residual.1.refs_0_), channel_id=1, source_target_pairs={{0,6},{1,7},{2,4},{3,5},{4,2},{5,3},{6,0},{7,1},{8,14},{9,15},{10,... | collective-permute-start | bytes 393224 | tf_op jit(solution)/shard_map/ppermute | solution.py:66
  44.2 11.5 %collective-permute-start.18 = (bf16[512,128]{1,0:T(8,128)(2,1)S(1)}, bf16[512,128]{1,0:T(8,128)(2,1)S(1)}, u32[]{:S(2)}, u32[]{:S(2)}) collective-permute-start(bf16[512,128]{1,0:T(8,128)(2,1)S(1)} %residual.1.refs_0_), channel_id=1, source_target_pairs={{0,4},{1,5},{2,6},{3,7},{4,0},{5,1},{6,2},{7,3},{8,12},{9,13},{10,... | collective-permute-start | bytes 393224 | tf_op jit(solution)/shard_map/ppermute | solution.py:66
  44.3 11.4 %collective-permute-start.16 = (bf16[512,128]{1,0:T(8,128)(2,1)S(1)}, bf16[512,128]{1,0:T(8,128)(2,1)S(1)}, u32[]{:S(2)}, u32[]{:S(2)}) collective-permute-start(bf16[512,128]{1,0:T(8,128)(2,1)S(1)} %residual.1.refs_0_), channel_id=1, source_target_pairs={{0,2},{1,3},{2,0},{3,1},{4,6},{5,7},{6,4},{7,5},{8,10},{9,11},{10,... | collective-permute-start | bytes 393224 | tf_op jit(solution)/shard_map/ppermute | solution.py:66
  52.6 3.6 %collective-permute-start.15 = (bf16[512,128]{1,0:T(8,128)(2,1)S(1)}, bf16[512,128]{1,0:T(8,128)(2,1)S(1)}, u32[]{:S(2)}, u32[]{:S(2)}) collective-permute-start(bf16[512,128]{1,0:T(8,128)(2,1)S(1)} %residual.1.refs_0_), channel_id=1, source_target_pairs={{0,1},{1,0},{2,3},{3,2},{4,5},{5,4},{6,7},{7,6},{8,9},{9,8},{10,11... | collective-permute-start | bytes 393224 | tf_op jit(solution)/shard_map/ppermute | solution.py:66
  55.7 1.3 %collective-permute-start.17 = (bf16[512,128]{1,0:T(8,128)(2,1)S(1)}, bf16[512,128]{1,0:T(8,128)(2,1)S(1)}, u32[]{:S(2)}, u32[]{:S(2)}) collective-permute-start(bf16[512,128]{1,0:T(8,128)(2,1)S(1)} %collective-permute-done.16.refs_2_), channel_id=1, source_target_pairs={{0,1},{1,0},{2,3},{3,2},{4,5},{5,4},{6,7},{7,6},{8,9},{9,8},{10,11... | collective-permute-start | bytes 393224 | tf_op jit(solution)/shard_map/ppermute | solution.py:66
  55.7 1.5 %collective-permute-start.19 = (bf16[512,128]{1,0:T(8,128)(2,1)S(1)}, bf16[512,128]{1,0:T(8,128)(2,1)S(1)}, u32[]{:S(2)}, u32[]{:S(2)}) collective-permute-start(bf16[512,128]{1,0:T(8,128)(2,1)S(1)} %collective-permute-done.18.refs_4_), channel_id=1, source_target_pairs={{0,1},{1,0},{2,3},{3,2},{4,5},{5,4},{6,7},{7,6},{8,9},{9,8},{10,11... | collective-permute-start | bytes 393224 | tf_op jit(solution)/shard_map/ppermute | solution.py:66
  56.2 1.3 %collective-permute-start.21 = (bf16[512,128]{1,0:T(8,128)(2,1)S(1)}, bf16[512,128]{1,0:T(8,128)(2,1)S(1)}, u32[]{:S(2)}, u32[]{:S(2)}) collective-permute-start(bf16[512,128]{1,0:T(8,128)(2,1)S(1)} %collective-permute-done.20.refs_6_), channel_id=1, source_target_pairs={{0,1},{1,0},{2,3},{3,2},{4,5},{5,4},{6,7},{7,6},{8,9},{9,8},{10,11... | collective-permute-start | bytes 393224 | tf_op jit(solution)/shard_map/ppermute | solution.py:66

commit v3 on v2

v3 whole, which is shorter than its diff:
```python
import functools

import jax
import jax.numpy as jnp
from jax import lax
from jax.experimental import pallas as pl
from jax.experimental.pallas import tpu as pltpu
from jax.sharding import PartitionSpec as P

INNER = 2

inner_rate = 0.5
momentum_coef = 0.9
outer_rate = 0.7
merge_keep = 0.5

F32 = jnp.float32
BF16 = jnp.bfloat16
LANES = 128
SPAN = 2 * LANES
MIB = 1 << 20
US = 1150000000

CODE_SCALE = 2.0**60
CODE_LEAST = 2.0**-30
CODE_CUT = 2.0**20


WEIGHT = {
    "opening": 1,
    "fetch": 0,
    "add_1": 0,
    "add_2": 20,
    "add_3": 20,
    "fold_1": 20,
    "fold_2": 8,
    "code_1": 0,
    "code_2": 0,
    "code_3": 0,
    "code_4": 0,
    "whole_gram": 0,
    "residual": 0,
    "near_update": 20,
    "weight_step": 0,
    "far_update": 0,
}


def encode(total, outer_rows, count):
    away = count * outer_rows - total
    held = jnp.where(jnp.abs(total) < CODE_LEAST, CODE_LEAST, total) * CODE_SCALE
    return jnp.where(jnp.abs(total) < jnp.abs(away), held, away).astype(BF16)


def decode_total(code, outer_rows, count):
    code = code.astype(F32)
    return jnp.where(jnp.abs(code) > CODE_CUT, code * (1.0 / CODE_SCALE), count * outer_rows - code)


def decode_away(code, outer_rows, count):
    code = code.astype(F32)
    return jnp.where(jnp.abs(code) > CODE_CUT, count * outer_rows - code * (1.0 / CODE_SCALE), code)


def swap(value, axis, flip):
    count = lax.axis_size(axis)
    return lax.ppermute(value, axis, [(i, i ^ flip) for i in range(count)])


VMEM = pl.BlockSpec(memory_space=pltpu.VMEM)
HBM = pl.BlockSpec(memory_space=pl.ANY)
SMEM = pl.BlockSpec(memory_space=pltpu.SMEM)


def in_hbm(value):
    return pltpu.with_memory_space_constraint(value, pltpu.HBM)


def near(shape, dtype):
    return pltpu.VMEM(tuple(shape), dtype)


def far(shape, dtype):
    return pltpu.HBM(tuple(shape), dtype)


def run(kernel, outs, ins, copies, scratch=(), weight=0, mib=8, aliases=None, name="kernel"):
    specs = [spec for _, spec in ins]
    return pl.pallas_call(
        kernel,
        out_shape=tuple(outs),
        in_specs=specs,
        out_specs=tuple(VMEM if out.memory_space == pltpu.VMEM else HBM for out in outs),
        scratch_shapes=list(scratch) + ([pltpu.SemaphoreType.DMA((copies,))] if copies else []),
        input_output_aliases=aliases or {},
        compiler_params=pltpu.CompilerParams(vmem_limit_bytes=mib * MIB),
        cost_estimate=pl.CostEstimate(flops=weight * US, bytes_accessed=1000, transcendentals=0),
        name=name,
    )(*[value for value, _ in ins])


def rows_at(block, size):
    return pl.ds(pl.multiple_of(block * size, size), size)


CORE, SHARD, CHIP_BIT_0, CHIP_BIT_1, KEEP_A, SEND_A, KEEP_B, SEND_B, CHIP = range(9)


def here(entry):
    shard, rep = lax.axis_index("fsdp"), lax.axis_index("rep")
    bit_a, bit_b = rep & 1, (rep >> 1) & 1
    table = (
        shard & 1, shard, (shard >> 1) & 1, (shard >> 2) & 1,
        bit_a, 1 - bit_a, 2 + bit_b, 3 - bit_b, shard >> 1,
    )
    return table[entry]


def reversed_bits(value, bits):
    return sum(((value >> bit) & 1) << (bits - 1 - bit) for bit in range(bits))


def open_kernel(
    scale, rate, x_ref, t_ref, w_ref, rep_ref, gram_keep, gram_send, x_out, w_out, first_a, first_b, keep_ref, *refs
):
    sends, (acc_ref, t_held, sems) = refs[:-3], refs[-3:]
    steps = keep_ref.shape[0]
    each_send = steps // len(sends)
    bits = steps.bit_length() - 1
    quarter = first_a.shape[0]
    depth = w_ref.shape[0]
    cut = depth // CUTS
    core = here(CORE)
    copy_x = pltpu.make_async_copy(x_ref, x_out, sems.at[0])
    copies_w = [
        pltpu.make_async_copy(w_ref.at[pl.ds(k * cut, cut)], w_out.at[pl.ds(k * cut, cut)], sems.at[4 + k])
        for k in range(CUTS)
    ]
    others = [
        pltpu.make_async_copy(t_ref, t_held, sems.at[1]),
        pltpu.make_async_copy(rep_ref.at[rows_at(here(SEND_A), quarter)], first_a, sems.at[2]),
        pltpu.make_async_copy(rep_ref.at[rows_at(here(SEND_B), quarter)], first_b, sems.at[3]),
    ]
    copy_x.start()
    copies_w[0].start()
    copies_w[1].start()
    copy_x.wait()
    x = x_out[...]
    gram = lax.dot_general(x, x, (((1,), (1,)), ((), ())), preferred_element_type=F32) * (rate * scale * scale)
    tiles = x.shape[0] // LANES
    pairs = [(i, j) for i in range(tiles) for j in range(i, tiles)]
    each = len(pairs) // 2
    for place, (i, j) in enumerate(pairs):
        part = gram[i * LANES : (i + 1) * LANES, j * LANES : (j + 1) * LANES].astype(BF16)
        side, spot = place // each, place % each
        rows = pl.ds(spot * LANES, LANES)

        @pl.when(core == side)
        def _():
            gram_keep[rows, :] = part

        @pl.when(core != side)
        def _():
            gram_send[rows, :] = part

    for k in range(CUTS):
        copies_w[k].wait()
        if k + 2 < CUTS:
            copies_w[k + 2].start()
        elif k + 2 == CUTS:
            for copy in others:
                copy.start()
        rows = pl.ds(k * cut, cut)
        part = jnp.dot(x_out[:, rows], w_out[rows, :].astype(BF16), preferred_element_type=F32)
        acc_ref[...] = part if k == 0 else acc_ref[...] + part
    others[0].wait()
    own = t_held.shape[0]
    rows = rows_at(here(SHARD), own)
    acc_ref[rows, :] = acc_ref[rows, :] - t_held[...].astype(F32) * (1.0 / scale)
    for j in range(steps):
        low = reversed_bits(j, bits) * SPAN
        for side in range(2):
            columns = slice(low + side * LANES, low + (side + 1) * LANES)

            @pl.when(core == side)
            def _():
                keep_ref[j] = (acc_ref[:, columns] * scale).astype(BF16)

            @pl.when(core != side)
            def _():
                sends[j // each_send][j % each_send] = (acc_ref[:, columns] * scale).astype(BF16)

    for copy in others[1:]:
        copy.wait()


CUTS = 4
SENDS = 2


def opening(x, t, w, rep_rows, scale, rate):
    tokens, depth = x.shape
    tiles = tokens // LANES
    each = tiles * (tiles + 1) // 4 * LANES
    quarter = (rep_rows.shape[0] // 4, rep_rows.shape[1])
    steps = w.shape[1] // SPAN
    return run(
        functools.partial(open_kernel, scale, rate),
        [near((each, LANES), BF16)] * 2
        + [near(x.shape, BF16), near(w.shape, F32)]
        + [near(quarter, BF16)] * 2
        + [near((steps, tokens, LANES), BF16)]
        + [near((steps // SENDS, tokens, LANES), BF16)] * SENDS,
        [(in_hbm(value), HBM) for value in (x, t, w, rep_rows)],
        4 + CUTS,
        scratch=[pltpu.VMEM((tokens, w.shape[1]), F32), pltpu.VMEM(t.shape, BF16)],
        weight=WEIGHT["opening"],
        name="opening",
    )


def fetch_kernel(token_ref, rep_ref, outer_ref, rep_a, rep_b, outer_a, outer_b, sems):
    del token_ref
    quarter = rep_a.shape[0]
    copies = []
    for k, (source, entry, target) in enumerate(
        [(rep_ref, KEEP_A, rep_a), (rep_ref, KEEP_B, rep_b), (outer_ref, KEEP_A, outer_a), (outer_ref, KEEP_B, outer_b)]
    ):
        copy = pltpu.make_async_copy(source.at[rows_at(here(entry), quarter)], target, sems.at[k])
        copy.start()
        copies.append(copy)
    for copy in copies:
        copy.wait()


def fetch(token, rep_rows, outer):
    quarter = (rep_rows.shape[0] // 4, rep_rows.shape[1])
    return run(
        fetch_kernel,
        [near(quarter, BF16)] * 2 + [near(quarter, F32)] * 2,
        [(token, HBM), (in_hbm(rep_rows), HBM), (in_hbm(outer), HBM)],
        4,
        weight=WEIGHT["fetch"],
        name="fetch",
    )


def fold_kernel(entry, token_ref, own_ref, *refs):
    gots, leave_ref, stay_ref = refs[:-2], refs[-2], refs[-1]
    size = stay_ref.shape[0]
    each = own_ref.shape[0] // len(gots)

    def total(place):
        got = gots[place // each]
        got = got[...] if each == 1 and len(got.shape) == 2 else got[place % each]
        return own_ref[place].astype(F32) + got.astype(F32)

    for side in range(2):

        @pl.when(here(entry) == side)
        def _():
            for k in range(size):
                leave_ref[k] = total((1 - side) * size + k).astype(BF16)
                stay_ref[k] = total(side * size + k)


def fold(token, own, gots, entry, weight):
    size, tokens, width = own.shape
    shape = (size // 2, tokens, width)
    return run(
        functools.partial(fold_kernel, entry),
        [near(shape, BF16), near(shape, F32)],
        [(token, HBM), (own, VMEM)] + [(got, VMEM) for got in gots],
        0,
        weight=weight,
        name="fold",
    )


def add_kernel(own_ref, got_ref, out_ref):
    out_ref[...] = (own_ref[...].astype(F32) + got_ref[...].astype(F32)).astype(BF16)


def add(own, got, weight):
    return run(
        add_kernel,
        [near(own.shape, BF16)],
        [(own, VMEM), (got, VMEM)],
        0,
        weight=weight,
        name="add",
    )[0]


def whole_gram_kernel(token_ref, x_ref, near_ref, far_ref, other_near, other_far, out_ref, turned_ref, pack_ref):
    rows = near_ref.shape[0]
    core, side = here(CORE), here(CHIP_BIT_0)
    for ref, half, part in (
        (near_ref, core, side),
        (far_ref, core, 1 - side),
        (other_near, 1 - core, side),
        (other_far, 1 - core, 1 - side),
    ):
        pack_ref[rows_at(2 * half + part, rows), :] = ref[...]
    tiles = out_ref.shape[0] // LANES
    pairs = [(i, j) for i in range(tiles) for j in range(i, tiles)]
    for place, (i, j) in enumerate(pairs):
        part = pack_ref[place * LANES : (place + 1) * LANES, :]
        out_ref[i * LANES : (i + 1) * LANES, j * LANES : (j + 1) * LANES] = part
        if i != j:
            out_ref[j * LANES : (j + 1) * LANES, i * LANES : (i + 1) * LANES] = part.T
    turned_ref[...] = x_ref[...].T


def whole_gram(token, x, pieces):
    tokens, depth = x.shape
    return run(
        whole_gram_kernel,
        [near((tokens, tokens), BF16), near((depth, tokens), BF16)],
        [(token, HBM), (x, VMEM)] + [(piece, VMEM) for piece in pieces],
        0,
        scratch=[pltpu.VMEM((4 * pieces[0].shape[0], LANES), BF16)],
        weight=WEIGHT["whole_gram"],
        name="whole_gram",
    )


def residual_kernel(own_ref, got_ref, gram_ref, out_ref):
    error = own_ref[0] + got_ref[0].astype(F32)
    moved = jnp.dot(gram_ref[...], error.astype(BF16), preferred_element_type=F32)
    out_ref[...] = (2.0 * error - moved).astype(BF16)


def residual(own, got, gram):
    _, tokens, width = own.shape
    return run(
        residual_kernel,
        [near((tokens, width), BF16)],
        [(own, VMEM), (got, VMEM), (gram, VMEM)],
        0,
        weight=WEIGHT["residual"],
        name="residual",
    )[0]


def step_kernel(rate, places, token_ref, turned_ref, w_ref, *refs):
    count = len(places)
    pieces = refs[: 2 * count]
    out_ref, pair_ref, buffer_ref, sems = refs[-4:]
    first = here(CORE) == 0
    copies = []
    for k, flip in enumerate(places):
        mine, other = pieces[2 * k][...], pieces[2 * k + 1][...]
        pair_ref[:, :LANES] = jnp.where(first, mine, other)
        pair_ref[:, LANES:] = jnp.where(first, other, mine)
        place = jnp.bitwise_xor(here(CHIP), flip)
        grad = jnp.dot(turned_ref[...], pair_ref[...], preferred_element_type=F32)
        columns = pl.ds(pl.multiple_of(place * SPAN, SPAN), SPAN)
        buffer_ref[k] = w_ref[:, columns] - rate * grad
        copy = pltpu.make_async_copy(
            buffer_ref.at[k], out_ref.at[:, columns], sems.at[k]
        )
        copy.start()
        copies.append(copy)
    for copy in copies:
        copy.wait()


def weight_step(token, turned, w, pairs, places, rate, before):
    depth, tokens = turned.shape
    count = len(pairs)
    flat = [piece for pair in pairs for piece in pair]
    ins = [(token, HBM), (turned, VMEM), (w, VMEM)] + [(piece, VMEM) for piece in flat]
    aliases = {}
    if before is not None:
        aliases = {len(ins): 0}
        ins.append((before, HBM))
    return run(
        functools.partial(step_kernel, rate, tuple(places)),
        [far(w.shape, F32)],
        ins,
        count,
        scratch=[pltpu.VMEM((tokens, SPAN), BF16), pltpu.VMEM((count, depth, SPAN), F32)],
        aliases=aliases,
        weight=WEIGHT["weight_step"],
        name="weight_step",
    )[0]


def first_code_kernel(rep_ref, got_ref, outer_ref, code_ref):
    total = rep_ref[...].astype(F32) + got_ref[...].astype(F32)
    code_ref[...] = encode(total, outer_ref[...], 2.0)


def second_code_kernel(own_ref, got_ref, outer_ref, code_ref):
    outer = outer_ref[...]
    total = decode_total(own_ref[...], outer, 2.0) + decode_total(got_ref[...], outer, 2.0)
    code_ref[...] = encode(total, outer, 4.0)


def code(kernel, own, got, outer_rows, weight):
    return run(
        kernel,
        [near(own.shape, BF16)],
        [(own, VMEM), (got, VMEM), (outer_rows, VMEM)],
        0,
        weight=weight,
        name="code",
    )[0]


PART = 128


def update_rows(entries, codes, outers, moments, reps, outs, buffers, sems, ready):
    size = codes[0].shape[0]
    copies = []
    part = min(PART, size)
    for half in range(2):
        for cut in range(size // part):
            spot = half * (size // part) + cut
            rows = pl.ds(cut * part, part)
            held = pl.ds(spot * part, part)
            if cut == 0:
                ready(half)
            outer = outers[half][rows, :]
            delta = decode_away(codes[half][rows, :], outer, 4.0) * 0.25
            moment = momentum_coef * moments[half][rows, :] + delta
            new_outer = outer - outer_rate * (delta + momentum_coef * moment)
            mixed = merge_keep * reps[half][rows, :].astype(F32) + (1.0 - merge_keep) * new_outer
            for k, value in enumerate((new_outer, moment, mixed.astype(BF16))):
                buffers[k][held, :] = value
                target = rows_at(here(entries[half]) * (size // part) + cut, part)
                copy = pltpu.make_async_copy(buffers[k].at[held], outs[k].at[target], sems.at[3 * spot + k])
                copy.start()
                copies.append(copy)
    for copy in copies:
        copy.wait()


def near_update_kernel(
    token_ref, code_a, code_b, outer_a, outer_b, rep_a, rep_b, outer_ref, moment_ref, rep_ref,
    new_outer, new_moment, merged, far_outer_a, far_outer_b, far_moment_a, far_moment_b, far_rep_a, far_rep_b,
    moment_a, moment_b, buffer_outer, buffer_moment, buffer_merged, sems,
):
    size = code_a.shape[0]
    base = 6 * max(size // PART, 1)
    fetches = [
        (moment_ref, KEEP_A, moment_a),
        (moment_ref, KEEP_B, moment_b),
        (outer_ref, SEND_A, far_outer_a),
        (outer_ref, SEND_B, far_outer_b),
        (moment_ref, SEND_A, far_moment_a),
        (moment_ref, SEND_B, far_moment_b),
        (rep_ref, SEND_A, far_rep_a),
        (rep_ref, SEND_B, far_rep_b),
    ]
    copies = []
    for k, (source, entry, target) in enumerate(fetches):
        copy = pltpu.make_async_copy(source.at[rows_at(here(entry), size)], target, sems.at[base + k])
        copy.start()
        copies.append(copy)
    update_rows(
        (KEEP_A, KEEP_B), (code_a, code_b), (outer_a, outer_b), (moment_a, moment_b), (rep_a, rep_b),
        (new_outer, new_moment, merged), (buffer_outer, buffer_moment, buffer_merged), sems,
        lambda half: copies[half].wait(),
    )
    for copy in copies[2:]:
        copy.wait()


def far_update_kernel(
    token_ref, code_a, code_b, outer_a, outer_b, moment_a, moment_b, rep_a, rep_b, held_a, held_b, held_c,
    new_outer, new_moment, merged, buffer_outer, buffer_moment, buffer_merged, sems,
):
    del held_a, held_b, held_c
    update_rows(
        (SEND_A, SEND_B), (code_a, code_b), (outer_a, outer_b), (moment_a, moment_b), (rep_a, rep_b),
        (new_outer, new_moment, merged), (buffer_outer, buffer_moment, buffer_merged), sems,
        lambda half: None,
    )


def update_scratch(size, width):
    return [pltpu.VMEM((2 * size, width), dtype) for dtype in (F32, F32, BF16)]


def near_update(token, codes, outers, reps, outer, moment, rep_rows):
    size, width = codes[0].shape
    full = outer.shape
    return run(
        near_update_kernel,
        [far(full, F32), far(full, F32), far(full, BF16)]
        + [near((size, width), F32)] * 4
        + [near((size, width), BF16)] * 2,
        [(token, HBM)]
        + [(value, VMEM) for value in (*codes, *outers, *reps)]
        + [(in_hbm(value), HBM) for value in (outer, moment, rep_rows)],
        6 * max(size // PART, 1) + 8,
        scratch=[pltpu.VMEM((size, width), F32)] * 2 + update_scratch(size, width),
        mib=16,
        weight=WEIGHT["near_update"],
        name="near_update",
    )


def far_update(token, codes, fetched, before):
    size, width = codes[0].shape
    outs = [far(value.shape, value.dtype) for value in before]
    ins = [(token, HBM)] + [(value, VMEM) for value in (*codes, *fetched)]
    return run(
        far_update_kernel,
        outs,
        ins + [(value, HBM) for value in before],
        6 * max(size // PART, 1),
        scratch=update_scratch(size, width),
        mib=16,
        aliases={len(ins) + k: k for k in range(3)},
        weight=WEIGHT["far_update"],
        name="far_update",
    )


def after(value, *others):
    return lax.optimization_barrier((value, *others))[0]


def both(x, t, w, outer, moment, rep_rows):
    shards = lax.axis_size("fsdp")
    chips = shards // 2
    scale = (x.shape[1] * shards) ** -0.5
    rate = inner_rate * scale
    token = t

    gram_keep, gram_send, x, w, first_a, first_b, keep, *sends = opening(x, t, w, rep_rows, scale, inner_rate)
    gram_got = swap(gram_send, "fsdp", 1)
    got = [swap(send, "fsdp", 1) for send in sends]
    got_a, got_b = swap(first_a, "rep", 1), swap(first_b, "rep", 2)
    halves = (2, gram_keep.shape[0] // 2, LANES)
    gram_leave, gram_stay = fold(
        token, gram_keep.reshape(halves), [gram_got.reshape(halves)], CHIP_BIT_0, WEIGHT["add_1"]
    )
    gram_got = swap(gram_leave[0], "fsdp", 2)

    leave_1, stay = fold(after(token, gram_leave), keep, got, CHIP_BIT_0, WEIGHT["fold_1"])
    got = swap(leave_1, "fsdp", 2)
    rep_a, rep_b, outer_a, outer_b = fetch(after(token, leave_1), rep_rows, outer)
    gram_2 = add(after(gram_stay, rep_a)[0], gram_got, WEIGHT["add_2"])
    gram_got = swap(gram_2, "fsdp", 4)

    leave_2, stay = fold(token, after(stay, gram_2), [got], CHIP_BIT_1, WEIGHT["fold_2"])
    got = swap(leave_2, "fsdp", 4)
    code_a = code(first_code_kernel, after(rep_a, leave_2), got_a, outer_a, WEIGHT["code_1"])
    code_b = code(first_code_kernel, after(rep_b, code_a), got_b, outer_b, WEIGHT["code_2"])
    got_a = swap(code_a, "rep", 2)
    got_b = swap(code_b, "rep", 1)

    gram_3 = add(after(gram_2, leave_2, code_a), gram_got, WEIGHT["add_3"])
    gram_far = swap(gram_3, "fsdp", 2)
    pieces = [gram_3, gram_far]
    pieces += [swap(piece, "fsdp", 1) for piece in pieces]

    gram, turned = whole_gram(after(token, leave_2), x, pieces)
    moved = residual(stay, got, gram)
    code_a = code(second_code_kernel, after(code_a, moved), got_a, outer_a, WEIGHT["code_3"])
    code_b = code(second_code_kernel, after(code_b, code_a), got_b, outer_b, WEIGHT["code_4"])
    got_a = swap(code_a, "rep", 1)
    got_b = swap(code_b, "rep", 2)

    updated = near_update(
        after(token, moved), (code_a, code_b), (outer_a, outer_b), (rep_a, rep_b), outer, moment, rep_rows
    )
    mine = [moved] + [swap(moved, "fsdp", 2 * k) for k in range(1, chips)]
    mine = [after(piece, updated[0]) for piece in mine]
    pairs = [(piece, swap(piece, "fsdp", 1)) for piece in mine]
    result = weight_step(token, turned, w, pairs, range(chips), rate, None)
    outers = far_update(after(token, result), (got_a, got_b), updated[3:], updated[:3])
    return result, *outers


def plain_outer(outer, moment, rep_rows):
    replica_rows = rep_rows.astype(F32)
    delta = lax.psum(outer - replica_rows, "rep") / lax.axis_size("rep")
    new_moment = momentum_coef * moment + delta
    new_outer = outer - outer_rate * (delta + momentum_coef * new_moment)
    mixed = merge_keep * replica_rows + (1.0 - merge_keep) * new_outer
    return new_outer, new_moment, mixed.astype(BF16)


def plain_inner(x, t, w):
    scale = (x.shape[1] * lax.axis_size("fsdp")) ** -0.5
    for _ in range(INNER):
        part = jnp.dot(x, w.astype(BF16), preferred_element_type=F32).astype(BF16)
        predicted = lax.psum_scatter(part, "fsdp", scatter_dimension=0, tiled=True).astype(F32) * scale
        errors = lax.all_gather((predicted - t.astype(F32)).astype(BF16), "fsdp", axis=0, tiled=True)
        gradient = lax.dot_general(x, errors, (((0,), (0,)), ((), ())), preferred_element_type=F32)
        w = w - inner_rate * scale * gradient
    return w


def local(tokens, targets, inner_weights, outer_weights, outer_momentum, replica_weights):
    x, t, w, rep_rows = tokens[0], targets[0], inner_weights[0], replica_weights[0]
    tiles = x.shape[0] // LANES
    if (
        lax.axis_size("fsdp") == 8
        and lax.axis_size("rep") == 4
        and w.shape[1] == 8 * LANES
        and x.shape[0] % LANES == 0
        and tiles * (tiles + 1) % 4 == 0
        and rep_rows.shape[0] % (4 * PART) == 0
    ):
        new_inner, new_outer, new_moment, merged = both(x, t, w, outer_weights, outer_momentum, rep_rows)
    else:
        new_outer, new_moment, merged = plain_outer(outer_weights, outer_momentum, rep_rows)
        new_inner = plain_inner(x, t, w)
    return new_inner[None], new_outer, new_moment, merged[None]


def solution(mesh):
    placed = (
        P("rep", None, "fsdp"),
        P("rep", "fsdp", None),
        P("rep", "fsdp", None),
        P("fsdp", None),
        P("fsdp", None),
        P("rep", "fsdp", None),
    )
    return jax.shard_map(
        local,
        mesh=mesh,
        in_specs=placed,
        out_specs=(
            P("rep", "fsdp", None),
            P("fsdp", None),
            P("fsdp", None),
            P("rep", "fsdp", None),
        ),
        check_vma=False,
    )
```

time: 64.6 us -> 57.2 us (0.89)
  waiting for transfers between devices: 18.1 us -> 12.4 us
  Pallas kernels: 25.1 us -> 20.8 us
  starting transfers between devices: 20.3 us -> 22.9 us
    ppermute x24 -> x23, waiting for transfers between devices: 18.1 us -> 12.4 us  [swap(): return lax.ppermute(value, axis, [(i, i ^ flip) for i in range(count)])]
    pallas_call x16, Pallas kernels: 25.1 us -> 20.8 us  [run(): pl.pallas_call(kernel, out_shape=tuple(outs), in_specs=specs, out_specs=t...]
    ppermute x24 -> x23, starting transfers between devices: 20.3 us -> 22.9 us  [swap(): return lax.ppermute(value, axis, [(i, i ^ flip) for i in range(count)])]
  transfers between devices with their start and end apart: 24 -> 23, of which waited for: 11 -> 11; matrix products, arithmetic and copies ran while one was open for 0% -> 0% of each run, Pallas kernels for 30% -> 24%
where the time goes in v3:
time: 57.2 us; the launch traced here: 57 us
  starting transfers between devices  22.9 us (40%)
  Pallas kernels  20.8 us (36%)
  waiting for transfers between devices  12.4 us (22%)
  between operations  0.93 us (2%)
    ppermute x23, starting transfers between devices, swap(): return lax.ppermute(value, axis, [(i, i ^ flip) for i in range(count)])  22.9 us
    pallas_call x16, Pallas kernels, run(): pl.pallas_call(kernel, out_shape=tuple(outs), in_specs=specs, out_specs=t...  20.8 us
    ppermute x23, waiting for transfers between devices, swap(): return lax.ppermute(value, axis, [(i, i ^ flip) for i in range(count)])  12.4 us
  transfers between devices with their start and end apart: 23, of which 11 were waited for; matrix products, arithmetic and copies ran while one was open for 0% of the time, Pallas kernels for 24%

profile of v3, /device:TPU:0, one launch (start us, length us, event | category | flops | bytes accessed | tf_op | source)
XLA Modules:
  0.0 57.0 jit_solution(8500211409113552042)
XLA Ops:
  0.6 4.7 %opening.1 = (bf16[640,128]{1,0:T(8,128)(2,1)S(1)}, bf16[640,128]{1,0:T(8,128)(2,1)S(1)}, bf16[512,1024]{1,0:T(8,128)(2,1)S(1)}, f32[1024,1024]{1,0:T(8,128)S(1)...) custom-call(bf16[512,1024]{1,0:T(8,128)(2,1)} %bitcast.29, ...), custom_call_target="tpu_custom_call" | custom-call | flops 1150000000 | bytes 1000 | tf_op jit(solution)/shard_map/opening/pallas_call | solution.py:89
  6.4 2.6 %collective-permute-start.5 = (bf16[256,1024]{1,0:T(8,128)(2,1)S(1)}, bf16[256,1024]{1,0:T(8,128)(2,1)S(1)}, u32[]{:S(2)}, u32[]{:S(2)}) collective-permute-start(bf16[256,1024]{1,0:T(8,128)(2,1)S(1)} %get-tuple-element.71), channel_id=1, source_target_pairs={{0,8},{8,0},{16,24},{24,16},{1,9},{9,1},{17,25},{25,17},{2,10},{10... | collective-permute-start | bytes 1572872 | tf_op jit(solution)/shard_map/ppermute | solution.py:67
  9.0 1.5 %collective-permute-start.12 = (bf16[256,1024]{1,0:T(8,128)(2,1)S(1)}, bf16[256,1024]{1,0:T(8,128)(2,1)S(1)}, u32[]{:S(2)}, u32[]{:S(2)}) collective-permute-start(bf16[256,1024]{1,0:T(8,128)(2,1)S(1)} %get-tuple-element.82), channel_id=1, source_target_pairs={{0,16},{8,24},{16,0},{24,8},{1,17},{9,25},{17,1},{25,9},{2,18},{10... | collective-permute-start | bytes 1572872 | tf_op jit(solution)/shard_map/ppermute | solution.py:67
  10.5 1.6 %collective-permute-start.3 = (bf16[320,128]{1,0:T(8,128)(2,1)S(1)}, bf16[320,128]{1,0:T(8,128)(2,1)S(1)}, u32[]{:S(2)}, u32[]{:S(2)}) collective-permute-start(bf16[320,128]{1,0:T(8,128)(2,1)S(1)} %bitcast.22), channel_id=1, source_target_pairs={{0,2},{1,3},{2,0},{3,1},{4,6},{5,7},{6,4},{7,5},{8,10},{9,11},{10,... | collective-permute-start | bytes 245768 | tf_op jit(solution)/shard_map/ppermute | solution.py:67
  12.8 1.9 %fetch.1 = (bf16[256,1024]{1,0:T(8,128)(2,1)S(1)}, bf16[256,1024]{1,0:T(8,128)(2,1)S(1)}, f32[256,1024]{1,0:T(8,128)S(1)}, f32[256,1024]{1,0:T(8,128)S(1)}) custom-call(bf16[64,1024]{1,0:T(8,128)(2,1)S(1)} %bitcast.13, bf16[1024,1024]{1,0:T(8,128)(2,1)} %bitcast.24, f32[1024,1024]{1,0:T(8,128)} %outer_ref.3), custom_call_target="tpu_custom_call" | custom-call | bytes 1000 | tf_op jit(solution)/shard_map/fetch/pallas_call | solution.py:89
  14.7 0.9 %collective-permute-done.3.got_ref = bf16[320,128]{1,0:T(8,128)(2,1)S(1)} collective-permute-done((bf16[320,128]{1,0:T(8,128)(2,1)S(1)}, bf16[320,128]{1,0:T(8,128)(2,1)S(1)}, u32[]{:S(2)}, u32[]{:S(2)}) %collective-permute-start.3) | collective-permute-done | bytes 81952 | tf_op jit(solution)/shard_map/ppermute | solution.py:67
  15.6 2.6 %collective-permute-start.6 = (bf16[320,128]{1,0:T(8,128)(2,1)S(1)}, bf16[320,128]{1,0:T(8,128)(2,1)S(1)}, u32[]{:S(2)}, u32[]{:S(2)}) collective-permute-start(bf16[320,128]{1,0:T(8,128)(2,1)S(1)} %add.2.own_ref), channel_id=1, source_target_pairs={{0,4},{1,5},{2,6},{3,7},{4,0},{5,1},{6,2},{7,3},{8,12},{9,13},{10,... | collective-permute-start | bytes 245768 | tf_op jit(solution)/shard_map/ppermute | solution.py:67
  18.3 4.1 %collective-permute-done.4.refs_0_ = bf16[2,512,128]{2,1,0:T(8,128)(2,1)S(1)} collective-permute-done((bf16[2,512,128]{2,1,0:T(8,128)(2,1)S(1)}, bf16[2,512,128]{2,1,0:T(8,128)(2,1)S(1)}, u32[]{:S(2)}, u32[]{:S(2)}) %collective-permute-start.4) | collective-permute-done | bytes 262176 | tf_op jit(solution)/shard_map/ppermute | solution.py:67
  23.1 0.7 %collective-permute-start.11 = (bf16[256,1024]{1,0:T(8,128)(2,1)S(1)}, bf16[256,1024]{1,0:T(8,128)(2,1)S(1)}, u32[]{:S(2)}, u32[]{:S(2)}) collective-permute-start(bf16[256,1024]{1,0:T(8,128)(2,1)S(1)} %code.4.own_ref), channel_id=1, source_target_pairs={{0,16},{8,24},{16,0},{24,8},{1,17},{9,25},{17,1},{25,9},{2,18},{10... | collective-permute-start | bytes 1572872 | tf_op jit(solution)/shard_map/ppermute | solution.py:67
  24.2 1.6 %collective-permute-start.13 = (bf16[256,1024]{1,0:T(8,128)(2,1)S(1)}, bf16[256,1024]{1,0:T(8,128)(2,1)S(1)}, u32[]{:S(2)}, u32[]{:S(2)}) collective-permute-start(bf16[256,1024]{1,0:T(8,128)(2,1)S(1)} %code.6.own_ref), channel_id=1, source_target_pairs={{0,8},{8,0},{16,24},{24,16},{1,9},{9,1},{17,25},{25,17},{2,10},{10... | collective-permute-start | bytes 1572872 | tf_op jit(solution)/shard_map/ppermute | solution.py:67
  25.8 1.6 %collective-permute-start.7 = (bf16[320,128]{1,0:T(8,128)(2,1)S(1)}, bf16[320,128]{1,0:T(8,128)(2,1)S(1)}, u32[]{:S(2)}, u32[]{:S(2)}) collective-permute-start(bf16[320,128]{1,0:T(8,128)(2,1)S(1)} %add.3.near_ref), channel_id=1, source_target_pairs={{0,2},{1,3},{2,0},{3,1},{4,6},{5,7},{6,4},{7,5},{8,10},{9,11},{10,... | collective-permute-start | bytes 245768 | tf_op jit(solution)/shard_map/ppermute | solution.py:67
  27.4 2.6 %collective-permute-start.10 = (bf16[1,512,128]{2,1,0:T(8,128)(2,1)S(1)}, bf16[1,512,128]{2,1,0:T(8,128)(2,1)S(1)}, u32[]{:S(2)}, u32[]{:S(2)}) collective-permute-start(bf16[1,512,128]{2,1,0:T(8,128)(2,1)S(1)} %get-tuple-element.67), channel_id=1, source_target_pairs={{0,4},{1,5},{2,6},{3,7},{4,0},{5,1},{6,2},{7,3},{8,12},{9,13},{10,... | collective-permute-start | bytes 393224 | tf_op jit(solution)/shard_map/ppermute | solution.py:67
  30.0 1.1 %collective-permute-done.7.far_ref = bf16[320,128]{1,0:T(8,128)(2,1)S(1)} collective-permute-done((bf16[320,128]{1,0:T(8,128)(2,1)S(1)}, bf16[320,128]{1,0:T(8,128)(2,1)S(1)}, u32[]{:S(2)}, u32[]{:S(2)}) %collective-permute-start.7) | collective-permute-done | bytes 81952 | tf_op jit(solution)/shard_map/ppermute | solution.py:67
  31.3 1.1 %collective-permute-done.9.other_far = bf16[320,128]{1,0:T(8,128)(2,1)S(1)} collective-permute-done((bf16[320,128]{1,0:T(8,128)(2,1)S(1)}, bf16[320,128]{1,0:T(8,128)(2,1)S(1)}, u32[]{:S(2)}, u32[]{:S(2)}) %collective-permute-start.9) | collective-permute-done | bytes 81952 | tf_op jit(solution)/shard_map/ppermute | solution.py:67
  32.8 2.5 %collective-permute-done.10.got_ref = bf16[1,512,128]{2,1,0:T(8,128)(2,1)S(1)} collective-permute-done((bf16[1,512,128]{2,1,0:T(8,128)(2,1)S(1)}, bf16[1,512,128]{2,1,0:T(8,128)(2,1)S(1)}, u32[]{:S(2)}, u32[]{:S(2)}) %collective-permute-start.10) | collective-permute-done | bytes 131104 | tf_op jit(solution)/shard_map/ppermute | solution.py:67
  35.7 2.6 %collective-permute-start.19 = (bf16[512,128]{1,0:T(8,128)(2,1)S(1)}, bf16[512,128]{1,0:T(8,128)(2,1)S(1)}, u32[]{:S(2)}, u32[]{:S(2)}) collective-permute-start(bf16[512,128]{1,0:T(8,128)(2,1)S(1)} %residual.1.refs_0_), channel_id=1, source_target_pairs={{0,6},{1,7},{2,4},{3,5},{4,2},{5,3},{6,0},{7,1},{8,14},{9,15},{10,... | collective-permute-start | bytes 393224 | tf_op jit(solution)/shard_map/ppermute | solution.py:67
  38.2 1.9 %collective-permute-start.15 = (bf16[512,128]{1,0:T(8,128)(2,1)S(1)}, bf16[512,128]{1,0:T(8,128)(2,1)S(1)}, u32[]{:S(2)}, u32[]{:S(2)}) collective-permute-start(bf16[512,128]{1,0:T(8,128)(2,1)S(1)} %residual.1.refs_0_), channel_id=1, source_target_pairs={{0,2},{1,3},{2,0},{3,1},{4,6},{5,7},{6,4},{7,5},{8,10},{9,11},{10,... | collective-permute-start | bytes 393224 | tf_op jit(solution)/shard_map/ppermute | solution.py:67
  40.1 0.8 %code.5.code_a = bf16[256,1024]{1,0:T(8,128)(2,1)S(1)} custom-call(bf16[256,1024]{1,0:T(8,128)(2,1)S(1)} %code.4.own_ref, bf16[256,1024]{1,0:T(8,128)(2,1)S(1)} %collective-permute-done.11.got_ref, f32[256,1024]{1,0:T(8,128)S(1)} %get-tuple-element.72.outer_ref.outer_a), custom_call_target="tpu_custom_call" | custom-call | bytes 1000 | tf_op jit(solution)/shard_map/code/pallas_call | solution.py:89
  41.5 0.8 %code.7.code_b = bf16[256,1024]{1,0:T(8,128)(2,1)S(1)} custom-call(bf16[256,1024]{1,0:T(8,128)(2,1)S(1)} %code.6.own_ref, bf16[256,1024]{1,0:T(8,128)(2,1)S(1)} %collective-permute-done.13.got_ref, f32[256,1024]{1,0:T(8,128)S(1)} %get-tuple-element.83.outer_ref.outer_b), custom_call_target="tpu_custom_call" | custom-call | bytes 1000 | tf_op jit(solution)/shard_map/code/pallas_call | solution.py:89
  42.3 0.7 %collective-permute-start.22 = (bf16[256,1024]{1,0:T(8,128)(2,1)S(1)}, bf16[256,1024]{1,0:T(8,128)(2,1)S(1)}, u32[]{:S(2)}, u32[]{:S(2)}) collective-permute-start(bf16[256,1024]{1,0:T(8,128)(2,1)S(1)} %code.7.code_b), channel_id=1, source_target_pairs={{0,16},{8,24},{16,0},{24,8},{1,17},{9,25},{17,1},{25,9},{2,18},{10... | collective-permute-start | bytes 1572872 | tf_op jit(solution)/shard_map/ppermute | solution.py:67
  43.0 4.9 %near_update.1 = (f32[1024,1024]{1,0:T(8,128)}, f32[1024,1024]{1,0:T(8,128)}, bf16[1024,1024]{1,0:T(8,128)(2,1)}, f32[256,1024]{1,0:T(8,128)S(1)}, f32[256,1024]...) custom-call(bf16[64,1024]{1,0:T(8,128)(2,1)S(1)} %bitcast.16, ...), custom_call_target="tpu_custom_call" | custom-call | flops 23000000512 | bytes 1000 | tf_op jit(solution)/shard_map/near_update/pallas_call | solution.py:89
  49.9 0.8 %collective-permute-done.20.refs_7_ = bf16[512,128]{1,0:T(8,128)(2,1)S(1)} collective-permute-done((bf16[512,128]{1,0:T(8,128)(2,1)S(1)}, bf16[512,128]{1,0:T(8,128)(2,1)S(1)}, u32[]{:S(2)}, u32[]{:S(2)}) %collective-permute-start.20) | collective-permute-done | bytes 131104 | tf_op jit(solution)/shard_map/ppermute | solution.py:67
  50.8 3.0 %weight_step.1 = f32[1024,1024]{1,0:T(8,128)} custom-call(bf16[64,1024]{1,0:T(8,128)(2,1)S(1)} %bitcast.17, bf16[1024,512]{1,0:T(8,128)(2,1)S(1)} %get-tuple-element.74.turned_ref, f32[1024,1024]{1,0:T(8,128)S(1)} %get-tuple-element.75.w_ref, bf16[512,128]{1,0:T(8,128)(2,1)S(1)} %residual.1.refs_0_, bf16[512,128]{1,0:T(8,128)(2,1)S(1)} %collective-permute-done.14.refs_1_, ...), custom_call_target="tpu_custom_call" | custom-call | bytes 1000 | tf_op jit(solution)/shard_map/weight_step/pallas_call | solution.py:89
  54.2 2.7 %far_update.1 = (f32[1024,1024]{1,0:T(8,128)}, f32[1024,1024]{1,0:T(8,128)}, bf16[1024,1024]{1,0:T(8,128)(2,1)}) custom-call(bf16[64,1024]{1,0:T(8,128)(2,1)S(1)} %bitcast.18, bf16[256,1024]{1,0:T(8,128)(2,1)S(1)} %collective-permute-done.21.code_a, ...), custom_call_target="tpu_custom_call", output_to_operand_aliasing={{0}: (9, {}), {1}: (10, {}), {2}: (11, {})} | custom-call | bytes 1000 | tf_op jit(solution)/shard_map/far_update/pallas_call | solution.py:89
  (40 shorter events, 6.7 us)
Async XLA Ops:
  0.6 9.9 %copy-start = (bf16[1,64,1024]{2,1,0:T(8,128)(2,1)S(1)}, bf16[1,64,1024]{2,1,0:T(8,128)(2,1)}, u32[]{:S(2)}) copy-start(bf16[1,64,1024]{2,1,0:T(8,128)(2,1)} %param.7) | copy-start | bytes 393220
  5.4 6.8 %collective-permute-start.1 = (bf16[2,512,128]{2,1,0:T(8,128)(2,1)S(1)}, bf16[2,512,128]{2,1,0:T(8,128)(2,1)S(1)}, u32[]{:S(2)}, u32[]{:S(2)}) collective-permute-start(bf16[2,512,128]{2,1,0:T(8,128)(2,1)S(1)} %get-tuple-element.58), channel_id=1, source_target_pairs={{0,1},{1,0},{2,3},{3,2},{4,5},{5,4},{6,7},{7,6},{8,9},{9,8},{10,11... | collective-permute-start | bytes 786440 | tf_op jit(solution)/shard_map/ppermute | solution.py:67
  5.9 6.3 %collective-permute-start.2 = (bf16[2,512,128]{2,1,0:T(8,128)(2,1)S(1)}, bf16[2,512,128]{2,1,0:T(8,128)(2,1)S(1)}, u32[]{:S(2)}, u32[]{:S(2)}) collective-permute-start(bf16[2,512,128]{2,1,0:T(8,128)(2,1)S(1)} %get-tuple-element.59), channel_id=1, source_target_pairs={{0,1},{1,0},{2,3},{3,2},{4,5},{5,4},{6,7},{7,6},{8,9},{9,8},{10,11... | collective-permute-start | bytes 786440 | tf_op jit(solution)/shard_map/ppermute | solution.py:67
  6.0 4.5 %collective-permute-start = (bf16[640,128]{1,0:T(8,128)(2,1)S(1)}, bf16[640,128]{1,0:T(8,128)(2,1)S(1)}, u32[]{:S(2)}, u32[]{:S(2)}) collective-permute-start(bf16[640,128]{1,0:T(8,128)(2,1)S(1)} %get-tuple-element.54), channel_id=1, source_target_pairs={{0,1},{1,0},{2,3},{3,2},{4,5},{5,4},{6,7},{7,6},{8,9},{9,8},{10,11... | collective-permute-start | bytes 491528 | tf_op jit(solution)/shard_map/ppermute | solution.py:67
  6.4 16.3 %collective-permute-start.5 = (bf16[256,1024]{1,0:T(8,128)(2,1)S(1)}, bf16[256,1024]{1,0:T(8,128)(2,1)S(1)}, u32[]{:S(2)}, u32[]{:S(2)}) collective-permute-start(bf16[256,1024]{1,0:T(8,128)(2,1)S(1)} %get-tuple-element.71), channel_id=1, source_target_pairs={{0,8},{8,0},{16,24},{24,16},{1,9},{9,1},{17,25},{25,17},{2,10},{10... | collective-permute-start | bytes 1572872 | tf_op jit(solution)/shard_map/ppermute | solution.py:67
  9.0 14.8 %collective-permute-start.12 = (bf16[256,1024]{1,0:T(8,128)(2,1)S(1)}, bf16[256,1024]{1,0:T(8,128)(2,1)S(1)}, u32[]{:S(2)}, u32[]{:S(2)}) collective-permute-start(bf16[256,1024]{1,0:T(8,128)(2,1)S(1)} %get-tuple-element.82), channel_id=1, source_target_pairs={{0,16},{8,24},{16,0},{24,8},{1,17},{9,25},{17,1},{25,9},{2,18},{10... | collective-permute-start | bytes 1572872 | tf_op jit(solution)/shard_map/ppermute | solution.py:67
  10.5 5.1 %collective-permute-start.3 = (bf16[320,128]{1,0:T(8,128)(2,1)S(1)}, bf16[320,128]{1,0:T(8,128)(2,1)S(1)}, u32[]{:S(2)}, u32[]{:S(2)}) collective-permute-start(bf16[320,128]{1,0:T(8,128)(2,1)S(1)} %bitcast.22), channel_id=1, source_target_pairs={{0,2},{1,3},{2,0},{3,1},{4,6},{5,7},{6,4},{7,5},{8,10},{9,11},{10,... | collective-permute-start | bytes 245768 | tf_op jit(solution)/shard_map/ppermute | solution.py:67
  12.3 10.1 %collective-permute-start.4 = (bf16[2,512,128]{2,1,0:T(8,128)(2,1)S(1)}, bf16[2,512,128]{2,1,0:T(8,128)(2,1)S(1)}, u32[]{:S(2)}, u32[]{:S(2)}) collective-permute-start(bf16[2,512,128]{2,1,0:T(8,128)(2,1)S(1)} %get-tuple-element.62), channel_id=1, source_target_pairs={{0,2},{1,3},{2,0},{3,1},{4,6},{5,7},{6,4},{7,5},{8,10},{9,11},{10,... | collective-permute-start | bytes 786440 | tf_op jit(solution)/shard_map/ppermute | solution.py:67
  15.6 10.1 %collective-permute-start.6 = (bf16[320,128]{1,0:T(8,128)(2,1)S(1)}, bf16[320,128]{1,0:T(8,128)(2,1)S(1)}, u32[]{:S(2)}, u32[]{:S(2)}) collective-permute-start(bf16[320,128]{1,0:T(8,128)(2,1)S(1)} %add.2.own_ref), channel_id=1, source_target_pairs={{0,4},{1,5},{2,6},{3,7},{4,0},{5,1},{6,2},{7,3},{8,12},{9,13},{10,... | collective-permute-start | bytes 245768 | tf_op jit(solution)/shard_map/ppermute | solution.py:67
  23.1 17.0 %collective-permute-start.11 = (bf16[256,1024]{1,0:T(8,128)(2,1)S(1)}, bf16[256,1024]{1,0:T(8,128)(2,1)S(1)}, u32[]{:S(2)}, u32[]{:S(2)}) collective-permute-start(bf16[256,1024]{1,0:T(8,128)(2,1)S(1)} %code.4.own_ref), channel_id=1, source_target_pairs={{0,16},{8,24},{16,0},{24,8},{1,17},{9,25},{17,1},{25,9},{2,18},{10... | collective-permute-start | bytes 1572872 | tf_op jit(solution)/shard_map/ppermute | solution.py:67
  24.2 17.3 %collective-permute-start.13 = (bf16[256,1024]{1,0:T(8,128)(2,1)S(1)}, bf16[256,1024]{1,0:T(8,128)(2,1)S(1)}, u32[]{:S(2)}, u32[]{:S(2)}) collective-permute-start(bf16[256,1024]{1,0:T(8,128)(2,1)S(1)} %code.6.own_ref), channel_id=1, source_target_pairs={{0,8},{8,0},{16,24},{24,16},{1,9},{9,1},{17,25},{25,17},{2,10},{10... | collective-permute-start | bytes 1572872 | tf_op jit(solution)/shard_map/ppermute | solution.py:67
  25.8 5.3 %collective-permute-start.7 = (bf16[320,128]{1,0:T(8,128)(2,1)S(1)}, bf16[320,128]{1,0:T(8,128)(2,1)S(1)}, u32[]{:S(2)}, u32[]{:S(2)}) collective-permute-start(bf16[320,128]{1,0:T(8,128)(2,1)S(1)} %add.3.near_ref), channel_id=1, source_target_pairs={{0,2},{1,3},{2,0},{3,1},{4,6},{5,7},{6,4},{7,5},{8,10},{9,11},{10,... | collective-permute-start | bytes 245768 | tf_op jit(solution)/shard_map/ppermute | solution.py:67
  27.4 7.9 %collective-permute-start.10 = (bf16[1,512,128]{2,1,0:T(8,128)(2,1)S(1)}, bf16[1,512,128]{2,1,0:T(8,128)(2,1)S(1)}, u32[]{:S(2)}, u32[]{:S(2)}) collective-permute-start(bf16[1,512,128]{2,1,0:T(8,128)(2,1)S(1)} %get-tuple-element.67), channel_id=1, source_target_pairs={{0,4},{1,5},{2,6},{3,7},{4,0},{5,1},{6,2},{7,3},{8,12},{9,13},{10,... | collective-permute-start | bytes 393224 | tf_op jit(solution)/shard_map/ppermute | solution.py:67
  30.0 1.3 %collective-permute-start.8 = (bf16[320,128]{1,0:T(8,128)(2,1)S(1)}, bf16[320,128]{1,0:T(8,128)(2,1)S(1)}, u32[]{:S(2)}, u32[]{:S(2)}) collective-permute-start(bf16[320,128]{1,0:T(8,128)(2,1)S(1)} %add.3.near_ref), channel_id=1, source_target_pairs={{0,1},{1,0},{2,3},{3,2},{4,5},{5,4},{6,7},{7,6},{8,9},{9,8},{10,11... | collective-permute-start | bytes 245768 | tf_op jit(solution)/shard_map/ppermute | solution.py:67
  31.1 1.3 %collective-permute-start.9 = (bf16[320,128]{1,0:T(8,128)(2,1)S(1)}, bf16[320,128]{1,0:T(8,128)(2,1)S(1)}, u32[]{:S(2)}, u32[]{:S(2)}) collective-permute-start(bf16[320,128]{1,0:T(8,128)(2,1)S(1)} %collective-permute-done.7.far_ref), channel_id=1, source_target_pairs={{0,1},{1,0},{2,3},{3,2},{4,5},{5,4},{6,7},{7,6},{8,9},{9,8},{10,11... | collective-permute-start | bytes 245768 | tf_op jit(solution)/shard_map/ppermute | solution.py:67
  35.7 12.3 %collective-permute-start.19 = (bf16[512,128]{1,0:T(8,128)(2,1)S(1)}, bf16[512,128]{1,0:T(8,128)(2,1)S(1)}, u32[]{:S(2)}, u32[]{:S(2)}) collective-permute-start(bf16[512,128]{1,0:T(8,128)(2,1)S(1)} %residual.1.refs_0_), channel_id=1, source_target_pairs={{0,6},{1,7},{2,4},{3,5},{4,2},{5,3},{6,0},{7,1},{8,14},{9,15},{10,... | collective-permute-start | bytes 393224 | tf_op jit(solution)/shard_map/ppermute | solution.py:67
  38.2 10.0 %collective-permute-start.17 = (bf16[512,128]{1,0:T(8,128)(2,1)S(1)}, bf16[512,128]{1,0:T(8,128)(2,1)S(1)}, u32[]{:S(2)}, u32[]{:S(2)}) collective-permute-start(bf16[512,128]{1,0:T(8,128)(2,1)S(1)} %residual.1.refs_0_), channel_id=1, source_target_pairs={{0,4},{1,5},{2,6},{3,7},{4,0},{5,1},{6,2},{7,3},{8,12},{9,13},{10,... | collective-permute-start | bytes 393224 | tf_op jit(solution)/shard_map/ppermute | solution.py:67
  38.2 10.0 %collective-permute-start.15 = (bf16[512,128]{1,0:T(8,128)(2,1)S(1)}, bf16[512,128]{1,0:T(8,128)(2,1)S(1)}, u32[]{:S(2)}, u32[]{:S(2)}) collective-permute-start(bf16[512,128]{1,0:T(8,128)(2,1)S(1)} %residual.1.refs_0_), channel_id=1, source_target_pairs={{0,2},{1,3},{2,0},{3,1},{4,6},{5,7},{6,4},{7,5},{8,10},{9,11},{10,... | collective-permute-start | bytes 393224 | tf_op jit(solution)/shard_map/ppermute | solution.py:67
  40.9 13.3 %collective-permute-start.21 = (bf16[256,1024]{1,0:T(8,128)(2,1)S(1)}, bf16[256,1024]{1,0:T(8,128)(2,1)S(1)}, u32[]{:S(2)}, u32[]{:S(2)}) collective-permute-start(bf16[256,1024]{1,0:T(8,128)(2,1)S(1)} %code.5.code_a), channel_id=1, source_target_pairs={{0,8},{8,0},{16,24},{24,16},{1,9},{9,1},{17,25},{25,17},{2,10},{10... | collective-permute-start | bytes 1572872 | tf_op jit(solution)/shard_map/ppermute | solution.py:67
  42.3 11.9 %collective-permute-start.22 = (bf16[256,1024]{1,0:T(8,128)(2,1)S(1)}, bf16[256,1024]{1,0:T(8,128)(2,1)S(1)}, u32[]{:S(2)}, u32[]{:S(2)}) collective-permute-start(bf16[256,1024]{1,0:T(8,128)(2,1)S(1)} %code.7.code_b), channel_id=1, source_target_pairs={{0,16},{8,24},{16,0},{24,8},{1,17},{9,25},{17,1},{25,9},{2,18},{10... | collective-permute-start | bytes 1572872 | tf_op jit(solution)/shard_map/ppermute | solution.py:67
  48.0 1.4 %collective-permute-start.14 = (bf16[512,128]{1,0:T(8,128)(2,1)S(1)}, bf16[512,128]{1,0:T(8,128)(2,1)S(1)}, u32[]{:S(2)}, u32[]{:S(2)}) collective-permute-start(bf16[512,128]{1,0:T(8,128)(2,1)S(1)} %residual.1.refs_0_), channel_id=1, source_target_pairs={{0,1},{1,0},{2,3},{3,2},{4,5},{5,4},{6,7},{7,6},{8,9},{9,8},{10,11... | collective-permute-start | bytes 393224 | tf_op jit(solution)/shard_map/ppermute | solution.py:67
  48.3 1.3 %collective-permute-start.16 = (bf16[512,128]{1,0:T(8,128)(2,1)S(1)}, bf16[512,128]{1,0:T(8,128)(2,1)S(1)}, u32[]{:S(2)}, u32[]{:S(2)}) collective-permute-start(bf16[512,128]{1,0:T(8,128)(2,1)S(1)} %collective-permute-done.15.refs_2_), channel_id=1, source_target_pairs={{0,1},{1,0},{2,3},{3,2},{4,5},{5,4},{6,7},{7,6},{8,9},{9,8},{10,11... | collective-permute-start | bytes 393224 | tf_op jit(solution)/shard_map/ppermute | solution.py:67
  48.6 1.3 %collective-permute-start.18 = (bf16[512,128]{1,0:T(8,128)(2,1)S(1)}, bf16[512,128]{1,0:T(8,128)(2,1)S(1)}, u32[]{:S(2)}, u32[]{:S(2)}) collective-permute-start(bf16[512,128]{1,0:T(8,128)(2,1)S(1)} %collective-permute-done.17.refs_4_), channel_id=1, source_target_pairs={{0,1},{1,0},{2,3},{3,2},{4,5},{5,4},{6,7},{7,6},{8,9},{9,8},{10,11... | collective-permute-start | bytes 393224 | tf_op jit(solution)/shard_map/ppermute | solution.py:67
  49.4 1.3 %collective-permute-start.20 = (bf16[512,128]{1,0:T(8,128)(2,1)S(1)}, bf16[512,128]{1,0:T(8,128)(2,1)S(1)}, u32[]{:S(2)}, u32[]{:S(2)}) collective-permute-start(bf16[512,128]{1,0:T(8,128)(2,1)S(1)} %collective-permute-done.19.refs_6_), channel_id=1, source_target_pairs={{0,1},{1,0},{2,3},{3,2},{4,5},{5,4},{6,7},{7,6},{8,9},{9,8},{10,11... | collective-permute-start | bytes 393224 | tf_op jit(solution)/shard_map/ppermute | solution.py:67

commit v4 on v3

--- a/solution.py
+++ b/solution.py
@@ -27,6 +27,7 @@
 
 
 WEIGHT = {
+    "prefetch": 0,
     "opening": 1,
     "fetch": 0,
     "add_1": 0,
@@ -39,7 +40,7 @@
     "code_3": 0,
     "code_4": 0,
     "whole_gram": 0,
-    "residual": 0,
+    "residual": 4,
     "near_update": 20,
     "weight_step": 0,
     "far_update": 0,
@@ -141,9 +142,8 @@
         pltpu.make_async_copy(rep_ref.at[rows_at(here(SEND_A), quarter)], first_a, sems.at[2]),
         pltpu.make_async_copy(rep_ref.at[rows_at(here(SEND_B), quarter)], first_b, sems.at[3]),
     ]
-    copy_x.start()
-    copies_w[0].start()
-    copies_w[1].start()
+    for copy in (copy_x, *copies_w, *others):
+        copy.start()
     copy_x.wait()
     x = x_out[...]
     gram = lax.dot_general(x, x, (((1,), (1,)), ((), ())), preferred_element_type=F32) * (rate * scale * scale)
@@ -165,11 +165,6 @@
 
     for k in range(CUTS):
         copies_w[k].wait()
-        if k + 2 < CUTS:
-            copies_w[k + 2].start()
-        elif k + 2 == CUTS:
-            for copy in others:
-                copy.start()
         rows = pl.ds(k * cut, cut)
         part = jnp.dot(x_out[:, rows], w_out[rows, :].astype(BF16), preferred_element_type=F32)
         acc_ref[...] = part if k == 0 else acc_ref[...] + part
@@ -216,6 +211,44 @@
         scratch=[pltpu.VMEM((tokens, w.shape[1]), F32), pltpu.VMEM(t.shape, BF16)],
         weight=WEIGHT["opening"],
         name="opening",
+    )
+
+
+def prefetch_kernel(
+    token_ref, outer_ref, moment_ref, rep_ref,
+    moment_a, moment_b, far_outer_a, far_outer_b, far_moment_a, far_moment_b, far_rep_a, far_rep_b, sems,
+):
+    del token_ref
+    quarter = moment_a.shape[0]
+    copies = []
+    for k, (source, entry, target) in enumerate(
+        [
+            (moment_ref, KEEP_A, moment_a),
+            (moment_ref, KEEP_B, moment_b),
+            (outer_ref, SEND_A, far_outer_a),
+            (outer_ref, SEND_B, far_outer_b),
+            (moment_ref, SEND_A, far_moment_a),
+            (moment_ref, SEND_B, far_moment_b),
+            (rep_ref, SEND_A, far_rep_a),
+            (rep_ref, SEND_B, far_rep_b),
+        ]
+    ):
+        copy = pltpu.make_async_copy(source.at[rows_at(here(entry), quarter)], target, sems.at[k])
+        copy.start()
+        copies.append(copy)
+    for copy in copies:
+        copy.wait()
+
+
+def prefetch(token, outer, moment, rep_rows):
+    quarter = (outer.shape[0] // 4, outer.shape[1])
+    return run(
+        prefetch_kernel,
+        [near(quarter, F32)] * 6 + [near(quarter, BF16)] * 2,
+        [(token, HBM)] + [(in_hbm(value), HBM) for value in (outer, moment, rep_rows)],
+        8,
+        weight=WEIGHT["prefetch"],
+        name="prefetch",
     )
 
 
@@ -439,34 +472,15 @@
 
 
 def near_update_kernel(
-    token_ref, code_a, code_b, outer_a, outer_b, rep_a, rep_b, outer_ref, moment_ref, rep_ref,
-    new_outer, new_moment, merged, far_outer_a, far_outer_b, far_moment_a, far_moment_b, far_rep_a, far_rep_b,
-    moment_a, moment_b, buffer_outer, buffer_moment, buffer_merged, sems,
+    token_ref, code_a, code_b, outer_a, outer_b, moment_a, moment_b, rep_a, rep_b,
+    new_outer, new_moment, merged, buffer_outer, buffer_moment, buffer_merged, sems,
 ):
-    size = code_a.shape[0]
-    base = 6 * max(size // PART, 1)
-    fetches = [
-        (moment_ref, KEEP_A, moment_a),
-        (moment_ref, KEEP_B, moment_b),
-        (outer_ref, SEND_A, far_outer_a),
-        (outer_ref, SEND_B, far_outer_b),
-        (moment_ref, SEND_A, far_moment_a),
-        (moment_ref, SEND_B, far_moment_b),
-        (rep_ref, SEND_A, far_rep_a),
-        (rep_ref, SEND_B, far_rep_b),
-    ]
-    copies = []
-    for k, (source, entry, target) in enumerate(fetches):
-        copy = pltpu.make_async_copy(source.at[rows_at(here(entry), size)], target, sems.at[base + k])
-        copy.start()
-        copies.append(copy)
+    del token_ref
     update_rows(
         (KEEP_A, KEEP_B), (code_a, code_b), (outer_a, outer_b), (moment_a, moment_b), (rep_a, rep_b),
         (new_outer, new_moment, merged), (buffer_outer, buffer_moment, buffer_merged), sems,
-        lambda half: copies[half].wait(),
-    )
-    for copy in copies[2:]:
-        copy.wait()
+        lambda half: None,
+    )
 
 
 def far_update_kernel(
@@ -485,19 +499,14 @@
     return [pltpu.VMEM((2 * size, width), dtype) for dtype in (F32, F32, BF16)]
 
 
-def near_update(token, codes, outers, reps, outer, moment, rep_rows):
+def near_update(token, codes, outers, moments, reps, full):
     size, width = codes[0].shape
-    full = outer.shape
     return run(
         near_update_kernel,
-        [far(full, F32), far(full, F32), far(full, BF16)]
-        + [near((size, width), F32)] * 4
-        + [near((size, width), BF16)] * 2,
-        [(token, HBM)]
-        + [(value, VMEM) for value in (*codes, *outers, *reps)]
-        + [(in_hbm(value), HBM) for value in (outer, moment, rep_rows)],
-        6 * max(size // PART, 1) + 8,
-        scratch=[pltpu.VMEM((size, width), F32)] * 2 + update_scratch(size, width),
+        [far(full, F32), far(full, F32), far(full, BF16)],
+        [(token, HBM)] + [(value, VMEM) for value in (*codes, *outers, *moments, *reps)],
+        6 * max(size // PART, 1),
+        scratch=update_scratch(size, width),
         mib=16,
         weight=WEIGHT["near_update"],
         name="near_update",
@@ -548,17 +557,17 @@
     gram_2 = add(after(gram_stay, rep_a)[0], gram_got, WEIGHT["add_2"])
     gram_got = swap(gram_2, "fsdp", 4)
 
-    leave_2, stay = fold(token, after(stay, gram_2), [got], CHIP_BIT_1, WEIGHT["fold_2"])
+    fetched = prefetch(after(token, gram_2), outer, moment, rep_rows)
+    leave_2, stay = fold(token, after(stay, gram_2, fetched[0]), [got], CHIP_BIT_1, WEIGHT["fold_2"])
     got = swap(leave_2, "fsdp", 4)
     code_a = code(first_code_kernel, after(rep_a, leave_2), got_a, outer_a, WEIGHT["code_1"])
     code_b = code(first_code_kernel, after(rep_b, code_a), got_b, outer_b, WEIGHT["code_2"])
     got_a = swap(code_a, "rep", 2)
     got_b = swap(code_b, "rep", 1)
 
-    gram_3 = add(after(gram_2, leave_2, code_a), gram_got, WEIGHT["add_3"])
+    gram_3 = add(after(gram_2, leave_2), gram_got, WEIGHT["add_3"])
     gram_far = swap(gram_3, "fsdp", 2)
-    pieces = [gram_3, gram_far]
-    pieces += [swap(piece, "fsdp", 1) for piece in pieces]
+    pieces = [gram_3, gram_far, swap(gram_3, "fsdp", 1), swap(after(gram_far, got), "fsdp", 1)]
 
     gram, turned = whole_gram(after(token, leave_2), x, pieces)
     moved = residual(stay, got, gram)
@@ -568,13 +577,13 @@
     got_b = swap(code_b, "rep", 2)
 
     updated = near_update(
-        after(token, moved), (code_a, code_b), (outer_a, outer_b), (rep_a, rep_b), outer, moment, rep_rows
+        after(token, moved), (code_a, code_b), (outer_a, outer_b), fetched[:2], (rep_a, rep_b), outer.shape
     )
     mine = [moved] + [swap(moved, "fsdp", 2 * k) for k in range(1, chips)]
     mine = [after(piece, updated[0]) for piece in mine]
     pairs = [(piece, swap(piece, "fsdp", 1)) for piece in mine]
     result = weight_step(token, turned, w, pairs, range(chips), rate, None)
-    outers = far_update(after(token, result), (got_a, got_b), updated[3:], updated[:3])
+    outers = far_update(after(token, result), (got_a, got_b), fetched[2:], updated)
     return result, *outers
 
 

time: 57.2 us -> 54.5 us (0.953)
  waiting for transfers between devices: 12.4 us -> 9.22 us
    ppermute x23, waiting for transfers between devices: 12.4 us -> 9.22 us  [swap(): return lax.ppermute(value, axis, [(i, i ^ flip) for i in range(count)])]
    pallas_call x16 -> x17, Pallas kernels: 20.8 us -> 20.9 us  [run(): pl.pallas_call(kernel, out_shape=tuple(outs), in_specs=specs, out_specs=t...]
  transfers between devices with their start and end apart: 23 -> 23, of which waited for: 11 -> 11; matrix products, arithmetic and copies ran while one was open for 0% -> 0% of each run, Pallas kernels for 24% -> 26%
where the time goes in v4:
time: 54.5 us; the launch traced here: 54.4 us
  starting transfers between devices  23.3 us (43%)
  Pallas kernels  20.9 us (38%)
  waiting for transfers between devices  9.22 us (17%)
  between operations  0.93 us (2%)
    ppermute x23, starting transfers between devices, swap(): return lax.ppermute(value, axis, [(i, i ^ flip) for i in range(count)])  23.3 us
    pallas_call x17, Pallas kernels, run(): pl.pallas_call(kernel, out_shape=tuple(outs), in_specs=specs, out_specs=t...  20.9 us
    ppermute x23, waiting for transfers between devices, swap(): return lax.ppermute(value, axis, [(i, i ^ flip) for i in range(count)])  9.22 us
  transfers between devices with their start and end apart: 23, of which 11 were waited for; matrix products, arithmetic and copies ran while one was open for 0% of the time, Pallas kernels for 26%

profile of v4, /device:TPU:0, one launch (start us, length us, event | category | flops | bytes accessed | tf_op | source)
XLA Modules:
  0.0 54.4 jit_solution(8345284501432869264)
XLA Ops:
  0.6 3.9 %opening.1 = (bf16[640,128]{1,0:T(8,128)(2,1)S(1)}, bf16[640,128]{1,0:T(8,128)(2,1)S(1)}, bf16[512,1024]{1,0:T(8,128)(2,1)S(1)}, f32[1024,1024]{1,0:T(8,128)S(1)...) custom-call(bf16[512,1024]{1,0:T(8,128)(2,1)} %bitcast.30, ...), custom_call_target="tpu_custom_call" | custom-call | flops 1150000000 | bytes 1000 | tf_op jit(solution)/shard_map/opening/pallas_call | solution.py:90
  5.6 2.6 %collective-permute-start.10 = (bf16[256,1024]{1,0:T(8,128)(2,1)S(1)}, bf16[256,1024]{1,0:T(8,128)(2,1)S(1)}, u32[]{:S(2)}, u32[]{:S(2)}) collective-permute-start(bf16[256,1024]{1,0:T(8,128)(2,1)S(1)} %get-tuple-element.84), channel_id=1, source_target_pairs={{0,8},{8,0},{16,24},{24,16},{1,9},{9,1},{17,25},{25,17},{2,10},{10... | collective-permute-start | bytes 1572872 | tf_op jit(solution)/shard_map/ppermute | solution.py:68
  8.2 1.5 %collective-permute-start.12 = (bf16[256,1024]{1,0:T(8,128)(2,1)S(1)}, bf16[256,1024]{1,0:T(8,128)(2,1)S(1)}, u32[]{:S(2)}, u32[]{:S(2)}) collective-permute-start(bf16[256,1024]{1,0:T(8,128)(2,1)S(1)} %get-tuple-element.89), channel_id=1, source_target_pairs={{0,16},{8,24},{16,0},{24,8},{1,17},{9,25},{17,1},{25,9},{2,18},{10... | collective-permute-start | bytes 1572872 | tf_op jit(solution)/shard_map/ppermute | solution.py:68
  9.7 1.6 %collective-permute-start.3 = (bf16[320,128]{1,0:T(8,128)(2,1)S(1)}, bf16[320,128]{1,0:T(8,128)(2,1)S(1)}, u32[]{:S(2)}, u32[]{:S(2)}) collective-permute-start(bf16[320,128]{1,0:T(8,128)(2,1)S(1)} %bitcast.23), channel_id=1, source_target_pairs={{0,2},{1,3},{2,0},{3,1},{4,6},{5,7},{6,4},{7,5},{8,10},{9,11},{10,... | collective-permute-start | bytes 245768 | tf_op jit(solution)/shard_map/ppermute | solution.py:68
  12.0 1.9 %fetch.1 = (bf16[256,1024]{1,0:T(8,128)(2,1)S(1)}, bf16[256,1024]{1,0:T(8,128)(2,1)S(1)}, f32[256,1024]{1,0:T(8,128)S(1)}, f32[256,1024]{1,0:T(8,128)S(1)}) custom-call(bf16[64,1024]{1,0:T(8,128)(2,1)S(1)} %bitcast.13, bf16[1024,1024]{1,0:T(8,128)(2,1)} %bitcast.25, f32[1024,1024]{1,0:T(8,128)} %outer_ref.3), custom_call_target="tpu_custom_call" | custom-call | bytes 1000 | tf_op jit(solution)/shard_map/fetch/pallas_call | solution.py:90
  13.9 0.9 %collective-permute-done.3.got_ref = bf16[320,128]{1,0:T(8,128)(2,1)S(1)} collective-permute-done((bf16[320,128]{1,0:T(8,128)(2,1)S(1)}, bf16[320,128]{1,0:T(8,128)(2,1)S(1)}, u32[]{:S(2)}, u32[]{:S(2)}) %collective-permute-start.3) | collective-permute-done | bytes 81952 | tf_op jit(solution)/shard_map/ppermute | solution.py:68
  14.8 2.6 %collective-permute-start.5 = (bf16[320,128]{1,0:T(8,128)(2,1)S(1)}, bf16[320,128]{1,0:T(8,128)(2,1)S(1)}, u32[]{:S(2)}, u32[]{:S(2)}) collective-permute-start(bf16[320,128]{1,0:T(8,128)(2,1)S(1)} %add.2.own_ref), channel_id=1, source_target_pairs={{0,4},{1,5},{2,6},{3,7},{4,0},{5,1},{6,2},{7,3},{8,12},{9,13},{10,... | collective-permute-start | bytes 245768 | tf_op jit(solution)/shard_map/ppermute | solution.py:68
  17.5 3.1 %prefetch.1 = (f32[256,1024]{1,0:T(8,128)S(1)}, f32[256,1024]{1,0:T(8,128)S(1)}, f32[256,1024]{1,0:T(8,128)S(1)}, f32[256,1024]{1,0:T(8,128)S(1)}, f32[256,1024]...) custom-call(bf16[64,1024]{1,0:T(8,128)(2,1)S(1)} %bitcast.14, ...), custom_call_target="tpu_custom_call" | custom-call | bytes 1000 | tf_op jit(solution)/shard_map/prefetch/pallas_call | solution.py:90
  20.6 1.0 %collective-permute-done.4.refs_0_ = bf16[2,512,128]{2,1,0:T(8,128)(2,1)S(1)} collective-permute-done((bf16[2,512,128]{2,1,0:T(8,128)(2,1)S(1)}, bf16[2,512,128]{2,1,0:T(8,128)(2,1)S(1)}, u32[]{:S(2)}, u32[]{:S(2)}) %collective-permute-start.4) | collective-permute-done | bytes 262176 | tf_op jit(solution)/shard_map/ppermute | solution.py:68
  21.9 1.8 %collective-permute-start.8 = (bf16[1,512,128]{2,1,0:T(8,128)(2,1)S(1)}, bf16[1,512,128]{2,1,0:T(8,128)(2,1)S(1)}, u32[]{:S(2)}, u32[]{:S(2)}) collective-permute-start(bf16[1,512,128]{2,1,0:T(8,128)(2,1)S(1)} %get-tuple-element.73), channel_id=1, source_target_pairs={{0,4},{1,5},{2,6},{3,7},{4,0},{5,1},{6,2},{7,3},{8,12},{9,13},{10,... | collective-permute-start | bytes 393224 | tf_op jit(solution)/shard_map/ppermute | solution.py:68
  23.7 2.0 %collective-permute-start.6 = (bf16[320,128]{1,0:T(8,128)(2,1)S(1)}, bf16[320,128]{1,0:T(8,128)(2,1)S(1)}, u32[]{:S(2)}, u32[]{:S(2)}) collective-permute-start(bf16[320,128]{1,0:T(8,128)(2,1)S(1)} %add.3.near_ref), channel_id=1, source_target_pairs={{0,2},{1,3},{2,0},{3,1},{4,6},{5,7},{6,4},{7,5},{8,10},{9,11},{10,... | collective-permute-start | bytes 245768 | tf_op jit(solution)/shard_map/ppermute | solution.py:68
  27.0 1.4 %collective-permute-start.13 = (bf16[256,1024]{1,0:T(8,128)(2,1)S(1)}, bf16[256,1024]{1,0:T(8,128)(2,1)S(1)}, u32[]{:S(2)}, u32[]{:S(2)}) collective-permute-start(bf16[256,1024]{1,0:T(8,128)(2,1)S(1)} %code.6.own_ref), channel_id=1, source_target_pairs={{0,8},{8,0},{16,24},{24,16},{1,9},{9,1},{17,25},{25,17},{2,10},{10... | collective-permute-start | bytes 1572872 | tf_op jit(solution)/shard_map/ppermute | solution.py:68
  28.4 1.5 %collective-permute-done.8.got_ref = bf16[1,512,128]{2,1,0:T(8,128)(2,1)S(1)} collective-permute-done((bf16[1,512,128]{2,1,0:T(8,128)(2,1)S(1)}, bf16[1,512,128]{2,1,0:T(8,128)(2,1)S(1)}, u32[]{:S(2)}, u32[]{:S(2)}) %collective-permute-start.8) | collective-permute-done | bytes 131104 | tf_op jit(solution)/shard_map/ppermute | solution.py:68
  29.9 1.3 %collective-permute-done.9.other_far = bf16[320,128]{1,0:T(8,128)(2,1)S(1)} collective-permute-done((bf16[320,128]{1,0:T(8,128)(2,1)S(1)}, bf16[320,128]{1,0:T(8,128)(2,1)S(1)}, u32[]{:S(2)}, u32[]{:S(2)}) %collective-permute-start.9) | collective-permute-done | bytes 81952 | tf_op jit(solution)/shard_map/ppermute | solution.py:68
  31.9 2.1 %collective-permute-start.19 = (bf16[512,128]{1,0:T(8,128)(2,1)S(1)}, bf16[512,128]{1,0:T(8,128)(2,1)S(1)}, u32[]{:S(2)}, u32[]{:S(2)}) collective-permute-start(bf16[512,128]{1,0:T(8,128)(2,1)S(1)} %residual.1.refs_0_), channel_id=1, source_target_pairs={{0,6},{1,7},{2,4},{3,5},{4,2},{5,3},{6,0},{7,1},{8,14},{9,15},{10,... | collective-permute-start | bytes 393224 | tf_op jit(solution)/shard_map/ppermute | solution.py:68
  34.0 2.4 %collective-permute-start.15 = (bf16[512,128]{1,0:T(8,128)(2,1)S(1)}, bf16[512,128]{1,0:T(8,128)(2,1)S(1)}, u32[]{:S(2)}, u32[]{:S(2)}) collective-permute-start(bf16[512,128]{1,0:T(8,128)(2,1)S(1)} %residual.1.refs_0_), channel_id=1, source_target_pairs={{0,2},{1,3},{2,0},{3,1},{4,6},{5,7},{6,4},{7,5},{8,10},{9,11},{10,... | collective-permute-start | bytes 393224 | tf_op jit(solution)/shard_map/ppermute | solution.py:68
  36.4 1.5 %collective-permute-done.11.got_ref = bf16[256,1024]{1,0:T(8,128)(2,1)S(1)} collective-permute-done((bf16[256,1024]{1,0:T(8,128)(2,1)S(1)}, bf16[256,1024]{1,0:T(8,128)(2,1)S(1)}, u32[]{:S(2)}, u32[]{:S(2)}) %collective-permute-start.11) | collective-permute-done | bytes 524320 | tf_op jit(solution)/shard_map/ppermute | solution.py:68
  37.9 0.8 %code.5.code_a = bf16[256,1024]{1,0:T(8,128)(2,1)S(1)} custom-call(bf16[256,1024]{1,0:T(8,128)(2,1)S(1)} %code.4.own_ref, bf16[256,1024]{1,0:T(8,128)(2,1)S(1)} %collective-permute-done.11.got_ref, f32[256,1024]{1,0:T(8,128)S(1)} %get-tuple-element.85.outer_ref.outer_a), custom_call_target="tpu_custom_call" | custom-call | bytes 1000 | tf_op jit(solution)/shard_map/code/pallas_call | solution.py:90
  39.4 0.8 %code.7.code_b = bf16[256,1024]{1,0:T(8,128)(2,1)S(1)} custom-call(bf16[256,1024]{1,0:T(8,128)(2,1)S(1)} %code.6.own_ref, bf16[256,1024]{1,0:T(8,128)(2,1)S(1)} %collective-permute-done.13.got_ref, f32[256,1024]{1,0:T(8,128)S(1)} %get-tuple-element.90.outer_ref.outer_b), custom_call_target="tpu_custom_call" | custom-call | bytes 1000 | tf_op jit(solution)/shard_map/code/pallas_call | solution.py:90
  40.2 1.8 %collective-permute-start.22 = (bf16[256,1024]{1,0:T(8,128)(2,1)S(1)}, bf16[256,1024]{1,0:T(8,128)(2,1)S(1)}, u32[]{:S(2)}, u32[]{:S(2)}) collective-permute-start(bf16[256,1024]{1,0:T(8,128)(2,1)S(1)} %code.7.code_b), channel_id=1, source_target_pairs={{0,16},{8,24},{16,0},{24,8},{1,17},{9,25},{17,1},{25,9},{2,18},{10... | collective-permute-start | bytes 1572872 | tf_op jit(solution)/shard_map/ppermute | solution.py:68
  42.0 2.7 %near_update.1 = (f32[1024,1024]{1,0:T(8,128)}, f32[1024,1024]{1,0:T(8,128)}, bf16[1024,1024]{1,0:T(8,128)(2,1)}) custom-call(bf16[64,1024]{1,0:T(8,128)(2,1)S(1)} %bitcast.17, bf16[256,1024]{1,0:T(8,128)(2,1)S(1)} %code.5.code_a, bf16[256,1024]{1,0:T(8,128)(2,1)S(1)} %code.7.code_b, f32[256,1024]{1,0:T(8,128)S(1)} %get-tuple-element.85.outer_ref.outer_a, ...), custom_call_target="tpu_custom_call" | custom-call | flops 23000000512 | bytes 1000 | tf_op jit(solution)/shard_map/near_update/pallas_call | solution.py:90
  47.5 3.0 %weight_step.1 = f32[1024,1024]{1,0:T(8,128)} custom-call(bf16[64,1024]{1,0:T(8,128)(2,1)S(1)} %bitcast.18, bf16[1024,512]{1,0:T(8,128)(2,1)S(1)} %get-tuple-element.78.turned_ref, f32[1024,1024]{1,0:T(8,128)S(1)} %get-tuple-element.79.w_ref, bf16[512,128]{1,0:T(8,128)(2,1)S(1)} %residual.1.refs_0_, bf16[512,128]{1,0:T(8,128)(2,1)S(1)} %collective-permute-done.14.refs_1_, ...), custom_call_target="tpu_custom_call" | custom-call | bytes 1000 | tf_op jit(solution)/shard_map/weight_step/pallas_call | solution.py:90
  50.5 1.0 %collective-permute-done.22.code_b = bf16[256,1024]{1,0:T(8,128)(2,1)S(1)} collective-permute-done((bf16[256,1024]{1,0:T(8,128)(2,1)S(1)}, bf16[256,1024]{1,0:T(8,128)(2,1)S(1)}, u32[]{:S(2)}, u32[]{:S(2)}) %collective-permute-start.22) | collective-permute-done | bytes 524320 | tf_op jit(solution)/shard_map/ppermute | solution.py:68
  51.5 2.7 %far_update.1 = (f32[1024,1024]{1,0:T(8,128)}, f32[1024,1024]{1,0:T(8,128)}, bf16[1024,1024]{1,0:T(8,128)(2,1)}) custom-call(bf16[64,1024]{1,0:T(8,128)(2,1)S(1)} %bitcast.19, bf16[256,1024]{1,0:T(8,128)(2,1)S(1)} %collective-permute-done.21.code_a, ...), custom_call_target="tpu_custom_call", output_to_operand_aliasing={{0}: (9, {}), {1}: (10, {}), {2}: (11, {})} | custom-call | bytes 1000 | tf_op jit(solution)/shard_map/far_update/pallas_call | solution.py:90
  (41 shorter events, 7.7 us)
Async XLA Ops:
  0.6 9.1 %copy-start = (bf16[1,64,1024]{2,1,0:T(8,128)(2,1)S(1)}, bf16[1,64,1024]{2,1,0:T(8,128)(2,1)}, u32[]{:S(2)}) copy-start(bf16[1,64,1024]{2,1,0:T(8,128)(2,1)} %param.7) | copy-start | bytes 393220
  4.6 6.8 %collective-permute-start.1 = (bf16[2,512,128]{2,1,0:T(8,128)(2,1)S(1)}, bf16[2,512,128]{2,1,0:T(8,128)(2,1)S(1)}, u32[]{:S(2)}, u32[]{:S(2)}) collective-permute-start(bf16[2,512,128]{2,1,0:T(8,128)(2,1)S(1)} %get-tuple-element.62), channel_id=1, source_target_pairs={{0,1},{1,0},{2,3},{3,2},{4,5},{5,4},{6,7},{7,6},{8,9},{9,8},{10,11... | collective-permute-start | bytes 786440 | tf_op jit(solution)/shard_map/ppermute | solution.py:68
  5.1 6.3 %collective-permute-start.2 = (bf16[2,512,128]{2,1,0:T(8,128)(2,1)S(1)}, bf16[2,512,128]{2,1,0:T(8,128)(2,1)S(1)}, u32[]{:S(2)}, u32[]{:S(2)}) collective-permute-start(bf16[2,512,128]{2,1,0:T(8,128)(2,1)S(1)} %get-tuple-element.63), channel_id=1, source_target_pairs={{0,1},{1,0},{2,3},{3,2},{4,5},{5,4},{6,7},{7,6},{8,9},{9,8},{10,11... | collective-permute-start | bytes 786440 | tf_op jit(solution)/shard_map/ppermute | solution.py:68
  5.2 4.5 %collective-permute-start = (bf16[640,128]{1,0:T(8,128)(2,1)S(1)}, bf16[640,128]{1,0:T(8,128)(2,1)S(1)}, u32[]{:S(2)}, u32[]{:S(2)}) collective-permute-start(bf16[640,128]{1,0:T(8,128)(2,1)S(1)} %get-tuple-element.58), channel_id=1, source_target_pairs={{0,1},{1,0},{2,3},{3,2},{4,5},{5,4},{6,7},{7,6},{8,9},{9,8},{10,11... | collective-permute-start | bytes 491528 | tf_op jit(solution)/shard_map/ppermute | solution.py:68
  5.6 20.0 %collective-permute-start.10 = (bf16[256,1024]{1,0:T(8,128)(2,1)S(1)}, bf16[256,1024]{1,0:T(8,128)(2,1)S(1)}, u32[]{:S(2)}, u32[]{:S(2)}) collective-permute-start(bf16[256,1024]{1,0:T(8,128)(2,1)S(1)} %get-tuple-element.84), channel_id=1, source_target_pairs={{0,8},{8,0},{16,24},{24,16},{1,9},{9,1},{17,25},{25,17},{2,10},{10... | collective-permute-start | bytes 1572872 | tf_op jit(solution)/shard_map/ppermute | solution.py:68
  8.2 18.4 %collective-permute-start.12 = (bf16[256,1024]{1,0:T(8,128)(2,1)S(1)}, bf16[256,1024]{1,0:T(8,128)(2,1)S(1)}, u32[]{:S(2)}, u32[]{:S(2)}) collective-permute-start(bf16[256,1024]{1,0:T(8,128)(2,1)S(1)} %get-tuple-element.89), channel_id=1, source_target_pairs={{0,16},{8,24},{16,0},{24,8},{1,17},{9,25},{17,1},{25,9},{2,18},{10... | collective-permute-start | bytes 1572872 | tf_op jit(solution)/shard_map/ppermute | solution.py:68
  9.7 5.1 %collective-permute-start.3 = (bf16[320,128]{1,0:T(8,128)(2,1)S(1)}, bf16[320,128]{1,0:T(8,128)(2,1)S(1)}, u32[]{:S(2)}, u32[]{:S(2)}) collective-permute-start(bf16[320,128]{1,0:T(8,128)(2,1)S(1)} %bitcast.23), channel_id=1, source_target_pairs={{0,2},{1,3},{2,0},{3,1},{4,6},{5,7},{6,4},{7,5},{8,10},{9,11},{10,... | collective-permute-start | bytes 245768 | tf_op jit(solution)/shard_map/ppermute | solution.py:68
  11.5 10.1 %collective-permute-start.4 = (bf16[2,512,128]{2,1,0:T(8,128)(2,1)S(1)}, bf16[2,512,128]{2,1,0:T(8,128)(2,1)S(1)}, u32[]{:S(2)}, u32[]{:S(2)}) collective-permute-start(bf16[2,512,128]{2,1,0:T(8,128)(2,1)S(1)} %get-tuple-element.66), channel_id=1, source_target_pairs={{0,2},{1,3},{2,0},{3,1},{4,6},{5,7},{6,4},{7,5},{8,10},{9,11},{10,... | collective-permute-start | bytes 786440 | tf_op jit(solution)/shard_map/ppermute | solution.py:68
  14.8 8.8 %collective-permute-start.5 = (bf16[320,128]{1,0:T(8,128)(2,1)S(1)}, bf16[320,128]{1,0:T(8,128)(2,1)S(1)}, u32[]{:S(2)}, u32[]{:S(2)}) collective-permute-start(bf16[320,128]{1,0:T(8,128)(2,1)S(1)} %add.2.own_ref), channel_id=1, source_target_pairs={{0,4},{1,5},{2,6},{3,7},{4,0},{5,1},{6,2},{7,3},{8,12},{9,13},{10,... | collective-permute-start | bytes 245768 | tf_op jit(solution)/shard_map/ppermute | solution.py:68
  21.9 8.1 %collective-permute-start.8 = (bf16[1,512,128]{2,1,0:T(8,128)(2,1)S(1)}, bf16[1,512,128]{2,1,0:T(8,128)(2,1)S(1)}, u32[]{:S(2)}, u32[]{:S(2)}) collective-permute-start(bf16[1,512,128]{2,1,0:T(8,128)(2,1)S(1)} %get-tuple-element.73), channel_id=1, source_target_pairs={{0,4},{1,5},{2,6},{3,7},{4,0},{5,1},{6,2},{7,3},{8,12},{9,13},{10,... | collective-permute-start | bytes 393224 | tf_op jit(solution)/shard_map/ppermute | solution.py:68
  23.7 4.8 %collective-permute-start.6 = (bf16[320,128]{1,0:T(8,128)(2,1)S(1)}, bf16[320,128]{1,0:T(8,128)(2,1)S(1)}, u32[]{:S(2)}, u32[]{:S(2)}) collective-permute-start(bf16[320,128]{1,0:T(8,128)(2,1)S(1)} %add.3.near_ref), channel_id=1, source_target_pairs={{0,2},{1,3},{2,0},{3,1},{4,6},{5,7},{6,4},{7,5},{8,10},{9,11},{10,... | collective-permute-start | bytes 245768 | tf_op jit(solution)/shard_map/ppermute | solution.py:68
  26.0 11.8 %collective-permute-start.11 = (bf16[256,1024]{1,0:T(8,128)(2,1)S(1)}, bf16[256,1024]{1,0:T(8,128)(2,1)S(1)}, u32[]{:S(2)}, u32[]{:S(2)}) collective-permute-start(bf16[256,1024]{1,0:T(8,128)(2,1)S(1)} %code.4.own_ref), channel_id=1, source_target_pairs={{0,16},{8,24},{16,0},{24,8},{1,17},{9,25},{17,1},{25,9},{2,18},{10... | collective-permute-start | bytes 1572872 | tf_op jit(solution)/shard_map/ppermute | solution.py:68
  27.0 12.4 %collective-permute-start.13 = (bf16[256,1024]{1,0:T(8,128)(2,1)S(1)}, bf16[256,1024]{1,0:T(8,128)(2,1)S(1)}, u32[]{:S(2)}, u32[]{:S(2)}) collective-permute-start(bf16[256,1024]{1,0:T(8,128)(2,1)S(1)} %code.6.own_ref), channel_id=1, source_target_pairs={{0,8},{8,0},{16,24},{24,16},{1,9},{9,1},{17,25},{25,17},{2,10},{10... | collective-permute-start | bytes 1572872 | tf_op jit(solution)/shard_map/ppermute | solution.py:68
  28.4 1.5 %collective-permute-start.7 = (bf16[320,128]{1,0:T(8,128)(2,1)S(1)}, bf16[320,128]{1,0:T(8,128)(2,1)S(1)}, u32[]{:S(2)}, u32[]{:S(2)}) collective-permute-start(bf16[320,128]{1,0:T(8,128)(2,1)S(1)} %add.3.near_ref), channel_id=1, source_target_pairs={{0,1},{1,0},{2,3},{3,2},{4,5},{5,4},{6,7},{7,6},{8,9},{9,8},{10,11... | collective-permute-start | bytes 245768 | tf_op jit(solution)/shard_map/ppermute | solution.py:68
  29.9 1.3 %collective-permute-start.9 = (bf16[320,128]{1,0:T(8,128)(2,1)S(1)}, bf16[320,128]{1,0:T(8,128)(2,1)S(1)}, u32[]{:S(2)}, u32[]{:S(2)}) collective-permute-start(bf16[320,128]{1,0:T(8,128)(2,1)S(1)} %collective-permute-done.6.far_ref), channel_id=1, source_target_pairs={{0,1},{1,0},{2,3},{3,2},{4,5},{5,4},{6,7},{7,6},{8,9},{9,8},{10,11... | collective-permute-start | bytes 245768 | tf_op jit(solution)/shard_map/ppermute | solution.py:68
  31.9 12.8 %collective-permute-start.19 = (bf16[512,128]{1,0:T(8,128)(2,1)S(1)}, bf16[512,128]{1,0:T(8,128)(2,1)S(1)}, u32[]{:S(2)}, u32[]{:S(2)}) collective-permute-start(bf16[512,128]{1,0:T(8,128)(2,1)S(1)} %residual.1.refs_0_), channel_id=1, source_target_pairs={{0,6},{1,7},{2,4},{3,5},{4,2},{5,3},{6,0},{7,1},{8,14},{9,15},{10,... | collective-permute-start | bytes 393224 | tf_op jit(solution)/shard_map/ppermute | solution.py:68
  34.0 11.5 %collective-permute-start.17 = (bf16[512,128]{1,0:T(8,128)(2,1)S(1)}, bf16[512,128]{1,0:T(8,128)(2,1)S(1)}, u32[]{:S(2)}, u32[]{:S(2)}) collective-permute-start(bf16[512,128]{1,0:T(8,128)(2,1)S(1)} %residual.1.refs_0_), channel_id=1, source_target_pairs={{0,4},{1,5},{2,6},{3,7},{4,0},{5,1},{6,2},{7,3},{8,12},{9,13},{10,... | collective-permute-start | bytes 393224 | tf_op jit(solution)/shard_map/ppermute | solution.py:68
  34.0 11.5 %collective-permute-start.15 = (bf16[512,128]{1,0:T(8,128)(2,1)S(1)}, bf16[512,128]{1,0:T(8,128)(2,1)S(1)}, u32[]{:S(2)}, u32[]{:S(2)}) collective-permute-start(bf16[512,128]{1,0:T(8,128)(2,1)S(1)} %residual.1.refs_0_), channel_id=1, source_target_pairs={{0,2},{1,3},{2,0},{3,1},{4,6},{5,7},{6,4},{7,5},{8,10},{9,11},{10,... | collective-permute-start | bytes 393224 | tf_op jit(solution)/shard_map/ppermute | solution.py:68
  38.7 12.9 %collective-permute-start.21 = (bf16[256,1024]{1,0:T(8,128)(2,1)S(1)}, bf16[256,1024]{1,0:T(8,128)(2,1)S(1)}, u32[]{:S(2)}, u32[]{:S(2)}) collective-permute-start(bf16[256,1024]{1,0:T(8,128)(2,1)S(1)} %code.5.code_a), channel_id=1, source_target_pairs={{0,8},{8,0},{16,24},{24,16},{1,9},{9,1},{17,25},{25,17},{2,10},{10... | collective-permute-start | bytes 1572872 | tf_op jit(solution)/shard_map/ppermute | solution.py:68
  40.2 11.3 %collective-permute-start.22 = (bf16[256,1024]{1,0:T(8,128)(2,1)S(1)}, bf16[256,1024]{1,0:T(8,128)(2,1)S(1)}, u32[]{:S(2)}, u32[]{:S(2)}) collective-permute-start(bf16[256,1024]{1,0:T(8,128)(2,1)S(1)} %code.7.code_b), channel_id=1, source_target_pairs={{0,16},{8,24},{16,0},{24,8},{1,17},{9,25},{17,1},{25,9},{2,18},{10... | collective-permute-start | bytes 1572872 | tf_op jit(solution)/shard_map/ppermute | solution.py:68
  44.7 1.4 %collective-permute-start.14 = (bf16[512,128]{1,0:T(8,128)(2,1)S(1)}, bf16[512,128]{1,0:T(8,128)(2,1)S(1)}, u32[]{:S(2)}, u32[]{:S(2)}) collective-permute-start(bf16[512,128]{1,0:T(8,128)(2,1)S(1)} %residual.1.refs_0_), channel_id=1, source_target_pairs={{0,1},{1,0},{2,3},{3,2},{4,5},{5,4},{6,7},{7,6},{8,9},{9,8},{10,11... | collective-permute-start | bytes 393224 | tf_op jit(solution)/shard_map/ppermute | solution.py:68
  45.6 1.3 %collective-permute-start.16 = (bf16[512,128]{1,0:T(8,128)(2,1)S(1)}, bf16[512,128]{1,0:T(8,128)(2,1)S(1)}, u32[]{:S(2)}, u32[]{:S(2)}) collective-permute-start(bf16[512,128]{1,0:T(8,128)(2,1)S(1)} %collective-permute-done.15.refs_2_), channel_id=1, source_target_pairs={{0,1},{1,0},{2,3},{3,2},{4,5},{5,4},{6,7},{7,6},{8,9},{9,8},{10,11... | collective-permute-start | bytes 393224 | tf_op jit(solution)/shard_map/ppermute | solution.py:68
  45.6 1.5 %collective-permute-start.18 = (bf16[512,128]{1,0:T(8,128)(2,1)S(1)}, bf16[512,128]{1,0:T(8,128)(2,1)S(1)}, u32[]{:S(2)}, u32[]{:S(2)}) collective-permute-start(bf16[512,128]{1,0:T(8,128)(2,1)S(1)} %collective-permute-done.17.refs_4_), channel_id=1, source_target_pairs={{0,1},{1,0},{2,3},{3,2},{4,5},{5,4},{6,7},{7,6},{8,9},{9,8},{10,11... | collective-permute-start | bytes 393224 | tf_op jit(solution)/shard_map/ppermute | solution.py:68
  46.1 1.3 %collective-permute-start.20 = (bf16[512,128]{1,0:T(8,128)(2,1)S(1)}, bf16[512,128]{1,0:T(8,128)(2,1)S(1)}, u32[]{:S(2)}, u32[]{:S(2)}) collective-permute-start(bf16[512,128]{1,0:T(8,128)(2,1)S(1)} %collective-permute-done.19.refs_6_), channel_id=1, source_target_pairs={{0,1},{1,0},{2,3},{3,2},{4,5},{5,4},{6,7},{7,6},{8,9},{9,8},{10,11... | collective-permute-start | bytes 393224 | tf_op jit(solution)/shard_map/ppermute | solution.py:68

commit v5 on v4

--- a/solution.py
+++ b/solution.py
@@ -189,7 +189,7 @@
         copy.wait()
 
 
-CUTS = 4
+CUTS = 2
 SENDS = 2
 
 
@@ -376,25 +376,32 @@
     )[0]
 
 
+STEP_CUTS = 4
+
+
 def step_kernel(rate, places, token_ref, turned_ref, w_ref, *refs):
     count = len(places)
     pieces = refs[: 2 * count]
     out_ref, pair_ref, buffer_ref, sems = refs[-4:]
     first = here(CORE) == 0
     copies = []
+    depth = w_ref.shape[0]
+    cut = depth // STEP_CUTS
     for k, flip in enumerate(places):
         mine, other = pieces[2 * k][...], pieces[2 * k + 1][...]
-        pair_ref[:, :LANES] = jnp.where(first, mine, other)
-        pair_ref[:, LANES:] = jnp.where(first, other, mine)
+        pair_ref[k, :, :LANES] = jnp.where(first, mine, other)
+        pair_ref[k, :, LANES:] = jnp.where(first, other, mine)
         place = jnp.bitwise_xor(here(CHIP), flip)
-        grad = jnp.dot(turned_ref[...], pair_ref[...], preferred_element_type=F32)
         columns = pl.ds(pl.multiple_of(place * SPAN, SPAN), SPAN)
-        buffer_ref[k] = w_ref[:, columns] - rate * grad
-        copy = pltpu.make_async_copy(
-            buffer_ref.at[k], out_ref.at[:, columns], sems.at[k]
-        )
-        copy.start()
-        copies.append(copy)
+        for part in range(STEP_CUTS):
+            rows = pl.ds(part * cut, cut)
+            grad = jnp.dot(turned_ref[rows, :], pair_ref[k], preferred_element_type=F32)
+            buffer_ref[k, rows, :] = w_ref[rows, columns] - rate * grad
+            copy = pltpu.make_async_copy(
+                buffer_ref.at[k, rows], out_ref.at[rows, columns], sems.at[STEP_CUTS * k + part]
+            )
+            copy.start()
+            copies.append(copy)
     for copy in copies:
         copy.wait()
 
@@ -412,8 +419,8 @@
         functools.partial(step_kernel, rate, tuple(places)),
         [far(w.shape, F32)],
         ins,
-        count,
-        scratch=[pltpu.VMEM((tokens, SPAN), BF16), pltpu.VMEM((count, depth, SPAN), F32)],
+        STEP_CUTS * count,
+        scratch=[pltpu.VMEM((count, tokens, SPAN), BF16), pltpu.VMEM((count, depth, SPAN), F32)],
         aliases=aliases,
         weight=WEIGHT["weight_step"],
         name="weight_step",
@@ -579,7 +586,8 @@
     updated = near_update(
         after(token, moved), (code_a, code_b), (outer_a, outer_b), fetched[:2], (rep_a, rep_b), outer.shape
     )
-    mine = [moved] + [swap(moved, "fsdp", 2 * k) for k in range(1, chips)]
+    moved_by = {k: swap(moved, "fsdp", 2 * k) for k in (1, 3, 2)}
+    mine = [moved] + [moved_by[k] for k in range(1, chips)]
     mine = [after(piece, updated[0]) for piece in mine]
     pairs = [(piece, swap(piece, "fsdp", 1)) for piece in mine]
     result = weight_step(token, turned, w, pairs, range(chips), rate, None)

time: 54.5 us -> 54.4 us (level)
  Pallas kernels: 20.9 us -> 20.3 us
    pallas_call x17, Pallas kernels: 20.9 us -> 20.3 us  [run(): pl.pallas_call(kernel, out_shape=tuple(outs), in_specs=specs, out_specs=t...]
where the time goes in v5:
time: 54.4 us; the launch traced here: 54.2 us
  starting transfers between devices  23.3 us (43%)
  Pallas kernels  20.3 us (37%)
  waiting for transfers between devices  9.69 us (18%)
  between operations  0.93 us (2%)
    ppermute x23, starting transfers between devices, swap(): return lax.ppermute(value, axis, [(i, i ^ flip) for i in range(count)])  23.3 us
    pallas_call x17, Pallas kernels, run(): pl.pallas_call(kernel, out_shape=tuple(outs), in_specs=specs, out_specs=t...  20.3 us
    ppermute x23, waiting for transfers between devices, swap(): return lax.ppermute(value, axis, [(i, i ^ flip) for i in range(count)])  9.69 us
  transfers between devices with their start and end apart: 23, of which 11 were waited for; matrix products, arithmetic and copies ran while one was open for 0% of the time, Pallas kernels for 26%

profile of v5, /device:TPU:0, one launch (start us, length us, event | category | flops | bytes accessed | tf_op | source)
XLA Modules:
  0.0 54.2 jit_solution(17335867366397815359)
XLA Ops:
  0.6 3.8 %opening.1 = (bf16[640,128]{1,0:T(8,128)(2,1)S(1)}, bf16[640,128]{1,0:T(8,128)(2,1)S(1)}, bf16[512,1024]{1,0:T(8,128)(2,1)S(1)}, f32[1024,1024]{1,0:T(8,128)S(1)...) custom-call(bf16[512,1024]{1,0:T(8,128)(2,1)} %bitcast.30, ...), custom_call_target="tpu_custom_call" | custom-call | flops 1150000000 | bytes 1000 | tf_op jit(solution)/shard_map/opening/pallas_call | solution.py:90
  5.5 2.6 %collective-permute-start.10 = (bf16[256,1024]{1,0:T(8,128)(2,1)S(1)}, bf16[256,1024]{1,0:T(8,128)(2,1)S(1)}, u32[]{:S(2)}, u32[]{:S(2)}) collective-permute-start(bf16[256,1024]{1,0:T(8,128)(2,1)S(1)} %get-tuple-element.84), channel_id=1, source_target_pairs={{0,8},{8,0},{16,24},{24,16},{1,9},{9,1},{17,25},{25,17},{2,10},{10... | collective-permute-start | bytes 1572872 | tf_op jit(solution)/shard_map/ppermute | solution.py:68
  8.0 1.5 %collective-permute-start.12 = (bf16[256,1024]{1,0:T(8,128)(2,1)S(1)}, bf16[256,1024]{1,0:T(8,128)(2,1)S(1)}, u32[]{:S(2)}, u32[]{:S(2)}) collective-permute-start(bf16[256,1024]{1,0:T(8,128)(2,1)S(1)} %get-tuple-element.89), channel_id=1, source_target_pairs={{0,16},{8,24},{16,0},{24,8},{1,17},{9,25},{17,1},{25,9},{2,18},{10... | collective-permute-start | bytes 1572872 | tf_op jit(solution)/shard_map/ppermute | solution.py:68
  9.6 1.6 %collective-permute-start.3 = (bf16[320,128]{1,0:T(8,128)(2,1)S(1)}, bf16[320,128]{1,0:T(8,128)(2,1)S(1)}, u32[]{:S(2)}, u32[]{:S(2)}) collective-permute-start(bf16[320,128]{1,0:T(8,128)(2,1)S(1)} %bitcast.23), channel_id=1, source_target_pairs={{0,2},{1,3},{2,0},{3,1},{4,6},{5,7},{6,4},{7,5},{8,10},{9,11},{10,... | collective-permute-start | bytes 245768 | tf_op jit(solution)/shard_map/ppermute | solution.py:68
  11.9 1.9 %fetch.1 = (bf16[256,1024]{1,0:T(8,128)(2,1)S(1)}, bf16[256,1024]{1,0:T(8,128)(2,1)S(1)}, f32[256,1024]{1,0:T(8,128)S(1)}, f32[256,1024]{1,0:T(8,128)S(1)}) custom-call(bf16[64,1024]{1,0:T(8,128)(2,1)S(1)} %bitcast.13, bf16[1024,1024]{1,0:T(8,128)(2,1)} %bitcast.25, f32[1024,1024]{1,0:T(8,128)} %outer_ref.3), custom_call_target="tpu_custom_call" | custom-call | bytes 1000 | tf_op jit(solution)/shard_map/fetch/pallas_call | solution.py:90
  13.8 0.9 %collective-permute-done.3.got_ref = bf16[320,128]{1,0:T(8,128)(2,1)S(1)} collective-permute-done((bf16[320,128]{1,0:T(8,128)(2,1)S(1)}, bf16[320,128]{1,0:T(8,128)(2,1)S(1)}, u32[]{:S(2)}, u32[]{:S(2)}) %collective-permute-start.3) | collective-permute-done | bytes 81952 | tf_op jit(solution)/shard_map/ppermute | solution.py:68
  14.7 2.6 %collective-permute-start.5 = (bf16[320,128]{1,0:T(8,128)(2,1)S(1)}, bf16[320,128]{1,0:T(8,128)(2,1)S(1)}, u32[]{:S(2)}, u32[]{:S(2)}) collective-permute-start(bf16[320,128]{1,0:T(8,128)(2,1)S(1)} %add.2.own_ref), channel_id=1, source_target_pairs={{0,4},{1,5},{2,6},{3,7},{4,0},{5,1},{6,2},{7,3},{8,12},{9,13},{10,... | collective-permute-start | bytes 245768 | tf_op jit(solution)/shard_map/ppermute | solution.py:68
  17.4 3.1 %prefetch.1 = (f32[256,1024]{1,0:T(8,128)S(1)}, f32[256,1024]{1,0:T(8,128)S(1)}, f32[256,1024]{1,0:T(8,128)S(1)}, f32[256,1024]{1,0:T(8,128)S(1)}, f32[256,1024]...) custom-call(bf16[64,1024]{1,0:T(8,128)(2,1)S(1)} %bitcast.14, ...), custom_call_target="tpu_custom_call" | custom-call | bytes 1000 | tf_op jit(solution)/shard_map/prefetch/pallas_call | solution.py:90
  20.5 1.0 %collective-permute-done.4.refs_0_ = bf16[2,512,128]{2,1,0:T(8,128)(2,1)S(1)} collective-permute-done((bf16[2,512,128]{2,1,0:T(8,128)(2,1)S(1)}, bf16[2,512,128]{2,1,0:T(8,128)(2,1)S(1)}, u32[]{:S(2)}, u32[]{:S(2)}) %collective-permute-start.4) | collective-permute-done | bytes 262176 | tf_op jit(solution)/shard_map/ppermute | solution.py:68
  21.7 1.8 %collective-permute-start.8 = (bf16[1,512,128]{2,1,0:T(8,128)(2,1)S(1)}, bf16[1,512,128]{2,1,0:T(8,128)(2,1)S(1)}, u32[]{:S(2)}, u32[]{:S(2)}) collective-permute-start(bf16[1,512,128]{2,1,0:T(8,128)(2,1)S(1)} %get-tuple-element.73), channel_id=1, source_target_pairs={{0,4},{1,5},{2,6},{3,7},{4,0},{5,1},{6,2},{7,3},{8,12},{9,13},{10,... | collective-permute-start | bytes 393224 | tf_op jit(solution)/shard_map/ppermute | solution.py:68
  23.5 2.0 %collective-permute-start.6 = (bf16[320,128]{1,0:T(8,128)(2,1)S(1)}, bf16[320,128]{1,0:T(8,128)(2,1)S(1)}, u32[]{:S(2)}, u32[]{:S(2)}) collective-permute-start(bf16[320,128]{1,0:T(8,128)(2,1)S(1)} %add.3.near_ref), channel_id=1, source_target_pairs={{0,2},{1,3},{2,0},{3,1},{4,6},{5,7},{6,4},{7,5},{8,10},{9,11},{10,... | collective-permute-start | bytes 245768 | tf_op jit(solution)/shard_map/ppermute | solution.py:68
  26.9 1.4 %collective-permute-start.13 = (bf16[256,1024]{1,0:T(8,128)(2,1)S(1)}, bf16[256,1024]{1,0:T(8,128)(2,1)S(1)}, u32[]{:S(2)}, u32[]{:S(2)}) collective-permute-start(bf16[256,1024]{1,0:T(8,128)(2,1)S(1)} %code.6.own_ref), channel_id=1, source_target_pairs={{0,8},{8,0},{16,24},{24,16},{1,9},{9,1},{17,25},{25,17},{2,10},{10... | collective-permute-start | bytes 1572872 | tf_op jit(solution)/shard_map/ppermute | solution.py:68
  28.3 1.5 %collective-permute-done.8.got_ref = bf16[1,512,128]{2,1,0:T(8,128)(2,1)S(1)} collective-permute-done((bf16[1,512,128]{2,1,0:T(8,128)(2,1)S(1)}, bf16[1,512,128]{2,1,0:T(8,128)(2,1)S(1)}, u32[]{:S(2)}, u32[]{:S(2)}) %collective-permute-start.8) | collective-permute-done | bytes 131104 | tf_op jit(solution)/shard_map/ppermute | solution.py:68
  29.8 1.3 %collective-permute-done.9.other_far = bf16[320,128]{1,0:T(8,128)(2,1)S(1)} collective-permute-done((bf16[320,128]{1,0:T(8,128)(2,1)S(1)}, bf16[320,128]{1,0:T(8,128)(2,1)S(1)}, u32[]{:S(2)}, u32[]{:S(2)}) %collective-permute-start.9) | collective-permute-done | bytes 81952 | tf_op jit(solution)/shard_map/ppermute | solution.py:68
  31.8 2.1 %collective-permute-start.19 = (bf16[512,128]{1,0:T(8,128)(2,1)S(1)}, bf16[512,128]{1,0:T(8,128)(2,1)S(1)}, u32[]{:S(2)}, u32[]{:S(2)}) collective-permute-start(bf16[512,128]{1,0:T(8,128)(2,1)S(1)} %residual.1.refs_0_), channel_id=1, source_target_pairs={{0,6},{1,7},{2,4},{3,5},{4,2},{5,3},{6,0},{7,1},{8,14},{9,15},{10,... | collective-permute-start | bytes 393224 | tf_op jit(solution)/shard_map/ppermute | solution.py:68
  33.9 2.4 %collective-permute-start.15 = (bf16[512,128]{1,0:T(8,128)(2,1)S(1)}, bf16[512,128]{1,0:T(8,128)(2,1)S(1)}, u32[]{:S(2)}, u32[]{:S(2)}) collective-permute-start(bf16[512,128]{1,0:T(8,128)(2,1)S(1)} %residual.1.refs_0_), channel_id=1, source_target_pairs={{0,2},{1,3},{2,0},{3,1},{4,6},{5,7},{6,4},{7,5},{8,10},{9,11},{10,... | collective-permute-start | bytes 393224 | tf_op jit(solution)/shard_map/ppermute | solution.py:68
  36.3 1.5 %collective-permute-done.11.got_ref = bf16[256,1024]{1,0:T(8,128)(2,1)S(1)} collective-permute-done((bf16[256,1024]{1,0:T(8,128)(2,1)S(1)}, bf16[256,1024]{1,0:T(8,128)(2,1)S(1)}, u32[]{:S(2)}, u32[]{:S(2)}) %collective-permute-start.11) | collective-permute-done | bytes 524320 | tf_op jit(solution)/shard_map/ppermute | solution.py:68
  37.7 0.8 %code.5.code_a = bf16[256,1024]{1,0:T(8,128)(2,1)S(1)} custom-call(bf16[256,1024]{1,0:T(8,128)(2,1)S(1)} %code.4.own_ref, bf16[256,1024]{1,0:T(8,128)(2,1)S(1)} %collective-permute-done.11.got_ref, f32[256,1024]{1,0:T(8,128)S(1)} %get-tuple-element.85.outer_ref.outer_a), custom_call_target="tpu_custom_call" | custom-call | bytes 1000 | tf_op jit(solution)/shard_map/code/pallas_call | solution.py:90
  39.3 0.8 %code.7.code_b = bf16[256,1024]{1,0:T(8,128)(2,1)S(1)} custom-call(bf16[256,1024]{1,0:T(8,128)(2,1)S(1)} %code.6.own_ref, bf16[256,1024]{1,0:T(8,128)(2,1)S(1)} %collective-permute-done.13.got_ref, f32[256,1024]{1,0:T(8,128)S(1)} %get-tuple-element.90.outer_ref.outer_b), custom_call_target="tpu_custom_call" | custom-call | bytes 1000 | tf_op jit(solution)/shard_map/code/pallas_call | solution.py:90
  40.1 1.8 %collective-permute-start.22 = (bf16[256,1024]{1,0:T(8,128)(2,1)S(1)}, bf16[256,1024]{1,0:T(8,128)(2,1)S(1)}, u32[]{:S(2)}, u32[]{:S(2)}) collective-permute-start(bf16[256,1024]{1,0:T(8,128)(2,1)S(1)} %code.7.code_b), channel_id=1, source_target_pairs={{0,16},{8,24},{16,0},{24,8},{1,17},{9,25},{17,1},{25,9},{2,18},{10... | collective-permute-start | bytes 1572872 | tf_op jit(solution)/shard_map/ppermute | solution.py:68
  41.9 2.7 %near_update.1 = (f32[1024,1024]{1,0:T(8,128)}, f32[1024,1024]{1,0:T(8,128)}, bf16[1024,1024]{1,0:T(8,128)(2,1)}) custom-call(bf16[64,1024]{1,0:T(8,128)(2,1)S(1)} %bitcast.17, bf16[256,1024]{1,0:T(8,128)(2,1)S(1)} %code.5.code_a, bf16[256,1024]{1,0:T(8,128)(2,1)S(1)} %code.7.code_b, f32[256,1024]{1,0:T(8,128)S(1)} %get-tuple-element.85.outer_ref.outer_a, ...), custom_call_target="tpu_custom_call" | custom-call | flops 23000000512 | bytes 1000 | tf_op jit(solution)/shard_map/near_update/pallas_call | solution.py:90
  47.4 2.5 %weight_step.1 = f32[1024,1024]{1,0:T(8,128)} custom-call(bf16[64,1024]{1,0:T(8,128)(2,1)S(1)} %bitcast.18, bf16[1024,512]{1,0:T(8,128)(2,1)S(1)} %get-tuple-element.78.turned_ref, f32[1024,1024]{1,0:T(8,128)S(1)} %get-tuple-element.79.w_ref, bf16[512,128]{1,0:T(8,128)(2,1)S(1)} %residual.1.refs_0_, bf16[512,128]{1,0:T(8,128)(2,1)S(1)} %collective-permute-done.14.refs_1_, ...), custom_call_target="tpu_custom_call" | custom-call | bytes 1000 | tf_op jit(solution)/shard_map/weight_step/pallas_call | solution.py:90
  49.9 1.5 %collective-permute-done.22.code_b = bf16[256,1024]{1,0:T(8,128)(2,1)S(1)} collective-permute-done((bf16[256,1024]{1,0:T(8,128)(2,1)S(1)}, bf16[256,1024]{1,0:T(8,128)(2,1)S(1)}, u32[]{:S(2)}, u32[]{:S(2)}) %collective-permute-start.22) | collective-permute-done | bytes 524320 | tf_op jit(solution)/shard_map/ppermute | solution.py:68
  51.4 2.7 %far_update.1 = (f32[1024,1024]{1,0:T(8,128)}, f32[1024,1024]{1,0:T(8,128)}, bf16[1024,1024]{1,0:T(8,128)(2,1)}) custom-call(bf16[64,1024]{1,0:T(8,128)(2,1)S(1)} %bitcast.19, bf16[256,1024]{1,0:T(8,128)(2,1)S(1)} %collective-permute-done.21.code_a, ...), custom_call_target="tpu_custom_call", output_to_operand_aliasing={{0}: (9, {}), {1}: (10, {}), {2}: (11, {})} | custom-call | bytes 1000 | tf_op jit(solution)/shard_map/far_update/pallas_call | solution.py:90
  (41 shorter events, 7.7 us)
Async XLA Ops:
  0.6 8.9 %copy-start = (bf16[1,64,1024]{2,1,0:T(8,128)(2,1)S(1)}, bf16[1,64,1024]{2,1,0:T(8,128)(2,1)}, u32[]{:S(2)}) copy-start(bf16[1,64,1024]{2,1,0:T(8,128)(2,1)} %param.7) | copy-start | bytes 393220
  4.4 6.8 %collective-permute-start.1 = (bf16[2,512,128]{2,1,0:T(8,128)(2,1)S(1)}, bf16[2,512,128]{2,1,0:T(8,128)(2,1)S(1)}, u32[]{:S(2)}, u32[]{:S(2)}) collective-permute-start(bf16[2,512,128]{2,1,0:T(8,128)(2,1)S(1)} %get-tuple-element.62), channel_id=1, source_target_pairs={{0,1},{1,0},{2,3},{3,2},{4,5},{5,4},{6,7},{7,6},{8,9},{9,8},{10,11... | collective-permute-start | bytes 786440 | tf_op jit(solution)/shard_map/ppermute | solution.py:68
  5.0 6.3 %collective-permute-start.2 = (bf16[2,512,128]{2,1,0:T(8,128)(2,1)S(1)}, bf16[2,512,128]{2,1,0:T(8,128)(2,1)S(1)}, u32[]{:S(2)}, u32[]{:S(2)}) collective-permute-start(bf16[2,512,128]{2,1,0:T(8,128)(2,1)S(1)} %get-tuple-element.63), channel_id=1, source_target_pairs={{0,1},{1,0},{2,3},{3,2},{4,5},{5,4},{6,7},{7,6},{8,9},{9,8},{10,11... | collective-permute-start | bytes 786440 | tf_op jit(solution)/shard_map/ppermute | solution.py:68
  5.0 4.5 %collective-permute-start = (bf16[640,128]{1,0:T(8,128)(2,1)S(1)}, bf16[640,128]{1,0:T(8,128)(2,1)S(1)}, u32[]{:S(2)}, u32[]{:S(2)}) collective-permute-start(bf16[640,128]{1,0:T(8,128)(2,1)S(1)} %get-tuple-element.58), channel_id=1, source_target_pairs={{0,1},{1,0},{2,3},{3,2},{4,5},{5,4},{6,7},{7,6},{8,9},{9,8},{10,11... | collective-permute-start | bytes 491528 | tf_op jit(solution)/shard_map/ppermute | solution.py:68
  5.5 20.0 %collective-permute-start.10 = (bf16[256,1024]{1,0:T(8,128)(2,1)S(1)}, bf16[256,1024]{1,0:T(8,128)(2,1)S(1)}, u32[]{:S(2)}, u32[]{:S(2)}) collective-permute-start(bf16[256,1024]{1,0:T(8,128)(2,1)S(1)} %get-tuple-element.84), channel_id=1, source_target_pairs={{0,8},{8,0},{16,24},{24,16},{1,9},{9,1},{17,25},{25,17},{2,10},{10... | collective-permute-start | bytes 1572872 | tf_op jit(solution)/shard_map/ppermute | solution.py:68
  8.0 18.4 %collective-permute-start.12 = (bf16[256,1024]{1,0:T(8,128)(2,1)S(1)}, bf16[256,1024]{1,0:T(8,128)(2,1)S(1)}, u32[]{:S(2)}, u32[]{:S(2)}) collective-permute-start(bf16[256,1024]{1,0:T(8,128)(2,1)S(1)} %get-tuple-element.89), channel_id=1, source_target_pairs={{0,16},{8,24},{16,0},{24,8},{1,17},{9,25},{17,1},{25,9},{2,18},{10... | collective-permute-start | bytes 1572872 | tf_op jit(solution)/shard_map/ppermute | solution.py:68
  9.6 5.1 %collective-permute-start.3 = (bf16[320,128]{1,0:T(8,128)(2,1)S(1)}, bf16[320,128]{1,0:T(8,128)(2,1)S(1)}, u32[]{:S(2)}, u32[]{:S(2)}) collective-permute-start(bf16[320,128]{1,0:T(8,128)(2,1)S(1)} %bitcast.23), channel_id=1, source_target_pairs={{0,2},{1,3},{2,0},{3,1},{4,6},{5,7},{6,4},{7,5},{8,10},{9,11},{10,... | collective-permute-start | bytes 245768 | tf_op jit(solution)/shard_map/ppermute | solution.py:68
  11.4 10.1 %collective-permute-start.4 = (bf16[2,512,128]{2,1,0:T(8,128)(2,1)S(1)}, bf16[2,512,128]{2,1,0:T(8,128)(2,1)S(1)}, u32[]{:S(2)}, u32[]{:S(2)}) collective-permute-start(bf16[2,512,128]{2,1,0:T(8,128)(2,1)S(1)} %get-tuple-element.66), channel_id=1, source_target_pairs={{0,2},{1,3},{2,0},{3,1},{4,6},{5,7},{6,4},{7,5},{8,10},{9,11},{10,... | collective-permute-start | bytes 786440 | tf_op jit(solution)/shard_map/ppermute | solution.py:68
  14.7 8.8 %collective-permute-start.5 = (bf16[320,128]{1,0:T(8,128)(2,1)S(1)}, bf16[320,128]{1,0:T(8,128)(2,1)S(1)}, u32[]{:S(2)}, u32[]{:S(2)}) collective-permute-start(bf16[320,128]{1,0:T(8,128)(2,1)S(1)} %add.2.own_ref), channel_id=1, source_target_pairs={{0,4},{1,5},{2,6},{3,7},{4,0},{5,1},{6,2},{7,3},{8,12},{9,13},{10,... | collective-permute-start | bytes 245768 | tf_op jit(solution)/shard_map/ppermute | solution.py:68
  21.7 8.1 %collective-permute-start.8 = (bf16[1,512,128]{2,1,0:T(8,128)(2,1)S(1)}, bf16[1,512,128]{2,1,0:T(8,128)(2,1)S(1)}, u32[]{:S(2)}, u32[]{:S(2)}) collective-permute-start(bf16[1,512,128]{2,1,0:T(8,128)(2,1)S(1)} %get-tuple-element.73), channel_id=1, source_target_pairs={{0,4},{1,5},{2,6},{3,7},{4,0},{5,1},{6,2},{7,3},{8,12},{9,13},{10,... | collective-permute-start | bytes 393224 | tf_op jit(solution)/shard_map/ppermute | solution.py:68
  23.5 4.8 %collective-permute-start.6 = (bf16[320,128]{1,0:T(8,128)(2,1)S(1)}, bf16[320,128]{1,0:T(8,128)(2,1)S(1)}, u32[]{:S(2)}, u32[]{:S(2)}) collective-permute-start(bf16[320,128]{1,0:T(8,128)(2,1)S(1)} %add.3.near_ref), channel_id=1, source_target_pairs={{0,2},{1,3},{2,0},{3,1},{4,6},{5,7},{6,4},{7,5},{8,10},{9,11},{10,... | collective-permute-start | bytes 245768 | tf_op jit(solution)/shard_map/ppermute | solution.py:68
  25.9 11.8 %collective-permute-start.11 = (bf16[256,1024]{1,0:T(8,128)(2,1)S(1)}, bf16[256,1024]{1,0:T(8,128)(2,1)S(1)}, u32[]{:S(2)}, u32[]{:S(2)}) collective-permute-start(bf16[256,1024]{1,0:T(8,128)(2,1)S(1)} %code.4.own_ref), channel_id=1, source_target_pairs={{0,16},{8,24},{16,0},{24,8},{1,17},{9,25},{17,1},{25,9},{2,18},{10... | collective-permute-start | bytes 1572872 | tf_op jit(solution)/shard_map/ppermute | solution.py:68
  26.9 12.4 %collective-permute-start.13 = (bf16[256,1024]{1,0:T(8,128)(2,1)S(1)}, bf16[256,1024]{1,0:T(8,128)(2,1)S(1)}, u32[]{:S(2)}, u32[]{:S(2)}) collective-permute-start(bf16[256,1024]{1,0:T(8,128)(2,1)S(1)} %code.6.own_ref), channel_id=1, source_target_pairs={{0,8},{8,0},{16,24},{24,16},{1,9},{9,1},{17,25},{25,17},{2,10},{10... | collective-permute-start | bytes 1572872 | tf_op jit(solution)/shard_map/ppermute | solution.py:68
  28.3 1.5 %collective-permute-start.7 = (bf16[320,128]{1,0:T(8,128)(2,1)S(1)}, bf16[320,128]{1,0:T(8,128)(2,1)S(1)}, u32[]{:S(2)}, u32[]{:S(2)}) collective-permute-start(bf16[320,128]{1,0:T(8,128)(2,1)S(1)} %add.3.near_ref), channel_id=1, source_target_pairs={{0,1},{1,0},{2,3},{3,2},{4,5},{5,4},{6,7},{7,6},{8,9},{9,8},{10,11... | collective-permute-start | bytes 245768 | tf_op jit(solution)/shard_map/ppermute | solution.py:68
  29.8 1.3 %collective-permute-start.9 = (bf16[320,128]{1,0:T(8,128)(2,1)S(1)}, bf16[320,128]{1,0:T(8,128)(2,1)S(1)}, u32[]{:S(2)}, u32[]{:S(2)}) collective-permute-start(bf16[320,128]{1,0:T(8,128)(2,1)S(1)} %collective-permute-done.6.far_ref), channel_id=1, source_target_pairs={{0,1},{1,0},{2,3},{3,2},{4,5},{5,4},{6,7},{7,6},{8,9},{9,8},{10,11... | collective-permute-start | bytes 245768 | tf_op jit(solution)/shard_map/ppermute | solution.py:68
  31.8 12.8 %collective-permute-start.19 = (bf16[512,128]{1,0:T(8,128)(2,1)S(1)}, bf16[512,128]{1,0:T(8,128)(2,1)S(1)}, u32[]{:S(2)}, u32[]{:S(2)}) collective-permute-start(bf16[512,128]{1,0:T(8,128)(2,1)S(1)} %residual.1.refs_0_), channel_id=1, source_target_pairs={{0,6},{1,7},{2,4},{3,5},{4,2},{5,3},{6,0},{7,1},{8,14},{9,15},{10,... | collective-permute-start | bytes 393224 | tf_op jit(solution)/shard_map/ppermute | solution.py:68
  33.9 11.5 %collective-permute-start.17 = (bf16[512,128]{1,0:T(8,128)(2,1)S(1)}, bf16[512,128]{1,0:T(8,128)(2,1)S(1)}, u32[]{:S(2)}, u32[]{:S(2)}) collective-permute-start(bf16[512,128]{1,0:T(8,128)(2,1)S(1)} %residual.1.refs_0_), channel_id=1, source_target_pairs={{0,4},{1,5},{2,6},{3,7},{4,0},{5,1},{6,2},{7,3},{8,12},{9,13},{10,... | collective-permute-start | bytes 393224 | tf_op jit(solution)/shard_map/ppermute | solution.py:68
  33.9 11.5 %collective-permute-start.15 = (bf16[512,128]{1,0:T(8,128)(2,1)S(1)}, bf16[512,128]{1,0:T(8,128)(2,1)S(1)}, u32[]{:S(2)}, u32[]{:S(2)}) collective-permute-start(bf16[512,128]{1,0:T(8,128)(2,1)S(1)} %residual.1.refs_0_), channel_id=1, source_target_pairs={{0,2},{1,3},{2,0},{3,1},{4,6},{5,7},{6,4},{7,5},{8,10},{9,11},{10,... | collective-permute-start | bytes 393224 | tf_op jit(solution)/shard_map/ppermute | solution.py:68
  38.5 12.9 %collective-permute-start.21 = (bf16[256,1024]{1,0:T(8,128)(2,1)S(1)}, bf16[256,1024]{1,0:T(8,128)(2,1)S(1)}, u32[]{:S(2)}, u32[]{:S(2)}) collective-permute-start(bf16[256,1024]{1,0:T(8,128)(2,1)S(1)} %code.5.code_a), channel_id=1, source_target_pairs={{0,8},{8,0},{16,24},{24,16},{1,9},{9,1},{17,25},{25,17},{2,10},{10... | collective-permute-start | bytes 1572872 | tf_op jit(solution)/shard_map/ppermute | solution.py:68
  40.1 11.3 %collective-permute-start.22 = (bf16[256,1024]{1,0:T(8,128)(2,1)S(1)}, bf16[256,1024]{1,0:T(8,128)(2,1)S(1)}, u32[]{:S(2)}, u32[]{:S(2)}) collective-permute-start(bf16[256,1024]{1,0:T(8,128)(2,1)S(1)} %code.7.code_b), channel_id=1, source_target_pairs={{0,16},{8,24},{16,0},{24,8},{1,17},{9,25},{17,1},{25,9},{2,18},{10... | collective-permute-start | bytes 1572872 | tf_op jit(solution)/shard_map/ppermute | solution.py:68
  44.6 1.4 %collective-permute-start.14 = (bf16[512,128]{1,0:T(8,128)(2,1)S(1)}, bf16[512,128]{1,0:T(8,128)(2,1)S(1)}, u32[]{:S(2)}, u32[]{:S(2)}) collective-permute-start(bf16[512,128]{1,0:T(8,128)(2,1)S(1)} %residual.1.refs_0_), channel_id=1, source_target_pairs={{0,1},{1,0},{2,3},{3,2},{4,5},{5,4},{6,7},{7,6},{8,9},{9,8},{10,11... | collective-permute-start | bytes 393224 | tf_op jit(solution)/shard_map/ppermute | solution.py:68
  45.4 1.3 %collective-permute-start.16 = (bf16[512,128]{1,0:T(8,128)(2,1)S(1)}, bf16[512,128]{1,0:T(8,128)(2,1)S(1)}, u32[]{:S(2)}, u32[]{:S(2)}) collective-permute-start(bf16[512,128]{1,0:T(8,128)(2,1)S(1)} %collective-permute-done.15.refs_2_), channel_id=1, source_target_pairs={{0,1},{1,0},{2,3},{3,2},{4,5},{5,4},{6,7},{7,6},{8,9},{9,8},{10,11... | collective-permute-start | bytes 393224 | tf_op jit(solution)/shard_map/ppermute | solution.py:68
  45.4 1.5 %collective-permute-start.18 = (bf16[512,128]{1,0:T(8,128)(2,1)S(1)}, bf16[512,128]{1,0:T(8,128)(2,1)S(1)}, u32[]{:S(2)}, u32[]{:S(2)}) collective-permute-start(bf16[512,128]{1,0:T(8,128)(2,1)S(1)} %collective-permute-done.17.refs_4_), channel_id=1, source_target_pairs={{0,1},{1,0},{2,3},{3,2},{4,5},{5,4},{6,7},{7,6},{8,9},{9,8},{10,11... | collective-permute-start | bytes 393224 | tf_op jit(solution)/shard_map/ppermute | solution.py:68
  46.0 1.3 %collective-permute-start.20 = (bf16[512,128]{1,0:T(8,128)(2,1)S(1)}, bf16[512,128]{1,0:T(8,128)(2,1)S(1)}, u32[]{:S(2)}, u32[]{:S(2)}) collective-permute-start(bf16[512,128]{1,0:T(8,128)(2,1)S(1)} %collective-permute-done.19.refs_6_), channel_id=1, source_target_pairs={{0,1},{1,0},{2,3},{3,2},{4,5},{5,4},{6,7},{7,6},{8,9},{9,8},{10,11... | collective-permute-start | bytes 393224 | tf_op jit(solution)/shard_map/ppermute | solution.py:68
